TPU v7x, 128 devices: a whole 4x4x4 slice. The times are simulated.
128 devices in a mesh: dp: 4 (over y_lo, core), mp: 32 (over y_hi, z, x).
Axes of the slice: x: 4, y: 4 (y_hi: 2, y_lo: 2; y = y_hi * 2 + y_lo), z: 4, core: 2. Of those that a mesh axis runs over, the one named last changes fastest.
Arguments:
- inputs: bfloat16 [512, 8192], P(None, ('dp', 'mp')), may hold values from -6 to 6
- grad_out: bfloat16 [512, 8192], P(None, ('dp', 'mp')), may hold values from -6 to 6
- gate_weight: bfloat16 [8192, 28672], P('dp', 'mp'), may hold values from -0.125 to 0.125
- up_weight: bfloat16 [8192, 28672], P('dp', 'mp'), may hold values from -0.125 to 0.125
- down_weight: bfloat16 [28672, 8192], P('mp', 'dp'), may hold values from -0.03125 to 0.03125
Outputs:
- grad_inputs: bfloat16 [512, 8192], P(None, ('dp', 'mp'))
- grad_gate: bfloat16 [8192, 28672], P('dp', 'mp')
- grad_up: bfloat16 [8192, 28672], P('dp', 'mp')
- grad_down: bfloat16 [28672, 8192], P('mp', 'dp')
All inputs are finite; a program needn't handle non-finite values.
Results may differ from a plain program's by a relative error of at most 0.0014.
Values may be sent and summed in bfloat16 or wider, within the bound.
No kernel may reach another device: no remote copies, remote signals or barrier semaphores. Data moves between devices by JAX's collectives and lax.ppermute only.
A program may use at most 128 MiB of HBM per device.

v0:
```python
import functools

import jax
import jax.numpy as jnp
from jax import lax
from jax.experimental import pallas as pl
from jax.experimental.pallas import tpu as pltpu
from jax.sharding import PartitionSpec as P

COST = 20
F32, BF16 = jnp.float32, jnp.bfloat16
SMALL, LARGE, WHOLE = 16 * 1024 * 1024, 40 * 1024 * 1024, 60 * 1024 * 1024
BOTH = ("dp", "mp")


def _moves(shift):
    pairs = []
    for i in range(128):
        lo, core, y, z, x = i // 64, (i // 32) % 2, (i // 16) % 2, (i // 4) % 4, i % 4
        lo, core, y, z, x = shift(lo, core, y, z, x)
        pairs.append((i, (lo % 2) * 64 + (core % 2) * 32 + (y % 2) * 16 + (z % 4) * 4 + x % 4))
    return pairs


def _send(a, shift):
    return lax.ppermute(a, BOTH, _moves(shift))


def _first(k):
    return lambda lo, c, y, z, x: (lo, c, y, z + k * c, x + k * (1 - c))


def _second(k):
    return lambda lo, c, y, z, x: (lo, c, y, z + k * (1 - c), x + k * c)


def _over_y(lo, c, y, z, x):
    return lo, c, y + 1, z, x


def _over_core(lo, c, y, z, x):
    return lo, c + 1, y, z, x


def _over_lo(lo, c, y, z, x):
    return lo + 1, c, y, z, x


def encode(u, positive):
    code = jnp.exp2(u * 200.0 - 100.0)
    return jnp.where(positive, code, -code).astype(BF16)


def decode(code):
    wide = code.astype(F32)
    return (jnp.log2(jnp.abs(wide)) + 100.0) * (1.0 / 200.0), wide > 0


def _signed(value, positive):
    return jnp.where(positive, value, -value)


def _call(body, out, room=SMALL, **kw):
    params = pltpu.CompilerParams(vmem_limit_bytes=room)
    return pl.pallas_call(body, out_shape=out, compiler_params=params, **kw)


def _cost(flops, bytes_accessed, transcendentals):
    return pl.CostEstimate(
        flops=flops // COST, bytes_accessed=bytes_accessed // COST, transcendentals=transcendentals // COST
    )


SMEM = pl.BlockSpec(memory_space=pltpu.SMEM)
VMEM = pl.BlockSpec(memory_space=pltpu.VMEM)
ANY = pl.BlockSpec(memory_space=pl.ANY)


def shape(dims, dtype):
    return jax.ShapeDtypeStruct(dims, dtype)


TICK = shape((8, 128), F32)


def _forward_body(width, ids, p0, p1, p2, p3, wg, wu, wd, *rest):
    mine, theirs, (acts, turned, held, last, loads, sems) = rest[:2], rest[2:8], rest[8:]
    weights = [
        pltpu.make_async_copy(weight, held.at[i], loads.at[i]) for i, weight in enumerate((wg, wu))
    ] + [pltpu.make_async_copy(wd, last, loads.at[2])]
    core, y, s1, s2 = ids[0], ids[1], ids[2], ids[3]
    copies = []
    for k2, piece in enumerate((p0, p1, p2, p3)):
        b = lax.rem(s2 + k2, 4)
        for k1 in range(4):
            a = lax.rem(s1 + k1, 4)
            zx = jnp.where(core == 0, b * 4 + a, a * 4 + b)
            for k0 in range(2):
                at = pl.multiple_of((lax.rem(y + k0, 2) * 16 + zx) * 64, 64)
                copies.append(
                    pltpu.make_async_copy(
                        piece.at[k1, k0], acts.at[:, pl.ds(at, 64), :], sems.at[len(copies)]
                    )
                )
    for copy in copies:
        copy.start()
    for copy in weights:
        copy.start()
    for copy in copies:
        copy.wait()
    half = mine[0].shape[0]
    for i in range(2):
        for n, place in enumerate((core, 1 - core)):
            for c in range(2):
                cols = pl.ds(pl.multiple_of((2 * c + place) * half, half), half)
                row = (2 * n + c) * half
                turned[i, row : row + half, :] = acts[i, :, cols].T
    for i in range(3):
        weights[i].wait()
        weight = last if i == 2 else held.at[i]
        dims = (((1,), (0,)), ((), ())) if i < 2 else (((1,), (1,)), ((), ()))
        total = lax.dot_general(turned[i // 2], weight[...], dims, preferred_element_type=F32)
        for c in range(2):
            mine[c][:, i * width : (i + 1) * width] = total[c * half : (c + 1) * half]
            theirs[3 * c + i][...] = total[(2 + c) * half : (3 + c) * half]


def _whole(*dims):
    return pl.BlockSpec(dims, lambda i: (0,) * len(dims))


def forward(ids, pieces, wg, wu, wd):
    depth, width = wg.shape
    tokens = pieces[0].shape[-1]
    mine, other = shape((tokens // 4, 3 * width), F32), shape((tokens // 4, width), F32)
    return _call(
        functools.partial(_forward_body, width),
        (mine,) * 2 + (other,) * 6 + (shape((2, depth, tokens), BF16),),
        WHOLE,
        in_specs=[SMEM] + [ANY] * 7,
        out_specs=(VMEM,) * 9,
        scratch_shapes=[
            pltpu.VMEM((2, tokens, depth), BF16),
            pltpu.VMEM((2, depth, width), BF16),
            pltpu.VMEM((width, depth), BF16),
            pltpu.SemaphoreType.DMA((3,)),
            pltpu.SemaphoreType.DMA((32,)),
        ],
        cost_estimate=_cost(
            flops=6 * tokens * depth * width, bytes_accessed=6 * depth * width + 8 * depth * tokens, transcendentals=0
        ),
    )(ids, *pieces, wg, wu, wd)


def _chip_body(width, mine, o0, o1, o2, chip, code, tick):
    tick[...] = jnp.zeros_like(tick)
    for i in range(3):
        cols = slice(i * width, (i + 1) * width)
        total = mine[:, cols] + (o0, o1, o2)[i][...]
        chip[:, cols] = total
        size = jnp.abs(total)
        top = jnp.max(jnp.max(size, axis=0, keepdims=True), axis=1, keepdims=True)
        top = jnp.maximum(top * 1.01, 1e-35).astype(BF16).astype(F32)
        code[:, cols] = encode(jnp.sqrt(size * (1.0 / top)), total >= 0)
        code[16 * i : 16 * i + 16, 3 * width :] = jnp.broadcast_to(top, (16, 128)).astype(BF16)
    code[48:, 3 * width :] = jnp.zeros((code.shape[0] - 48, 128), BF16)


def chip_sum(mine, others):
    rows, three = mine.shape
    return _call(
        functools.partial(_chip_body, three // 3),
        (shape((rows, three), F32), shape((rows, three + 128), BF16), TICK),
        in_specs=[VMEM] * 4,
        out_specs=(VMEM,) * 3,
        cost_estimate=_cost(
            flops=20 * rows * three, bytes_accessed=14 * rows * three, transcendentals=2 * rows * three
        ),
    )(mine, *others)


def _act_body(width, chip, code, _, o0, o1, o2):
    def whole(i):
        cols = slice(i * width, (i + 1) * width)
        u, positive = decode(code[:, cols])
        top = code[16 * i : 16 * i + 16, 3 * width :].astype(F32)[0:1, 0:1]
        return chip[:, cols] + _signed(u * u * top, positive)

    gate, up, grad_hidden = whole(0), whole(1), whole(2)
    squash = 1.0 / (1.0 + jnp.exp(-gate))
    o0[...] = gate * squash * up
    o1[...] = grad_hidden * up * squash * (1.0 + gate * (1.0 - squash))
    o2[...] = grad_hidden * gate * squash


def activations(chip, code, after):
    rows, three = chip.shape
    return _call(
        functools.partial(_act_body, three // 3),
        (shape((rows, three // 3), F32),) * 3,
        in_specs=[VMEM] * 2 + [ANY],
        out_specs=(VMEM,) * 3,
        cost_estimate=_cost(
            flops=20 * rows * three, bytes_accessed=10 * rows * three, transcendentals=2 * rows * three
        ),
    )(chip, code, after)


def _pack(block):
    size = jnp.abs(block)
    top = jnp.maximum(jnp.max(size, axis=0, keepdims=True) * 1.01, 1e-35)
    top = top.astype(BF16).astype(F32)
    return encode(size * (1.0 / top), block >= 0), top


def _unpack(code, top):
    u, positive = decode(code)
    return _signed(u * top, positive)


def _grad_in_body(width, n_before, ids, wg, wu, m0, m1, m2, o0, o1, o2, *rest):
    before, (pair, own, c1, c2, c3, tick, right, tops, blocks, codes) = rest[:n_before], rest[n_before:]
    core, s1 = ids[0], ids[2]
    half = m0.shape[0]
    tokens = 2 * half
    tick[...] = jnp.zeros_like(tick)
    for parts, place in (((m0, m1, m2), core), ((o0, o1, o2), 1 - core)):
        rows = pl.ds(pl.multiple_of(place * half, half), half)
        rest = pl.ds(pl.multiple_of(tokens + place * half, half), half)
        for i, part in enumerate(parts):
            value = part[...]
            high = value.astype(BF16)
            low = (value - high.astype(F32)).astype(BF16)
            pair[rows, i * width : (i + 1) * width] = high
            pair[rest, i * width : (i + 1) * width] = low
            if i:
                right[rows, (2 * i - 2) * width : (2 * i - 1) * width] = high
                right[rows, (2 * i - 1) * width : 2 * i * width] = low
    for part in range(4):
        some = slice(part * 512, (part + 1) * 512)
        g, u = wg[some, :], wu[some, :]
        total = lax.dot_general(
            jnp.concatenate([g, g, u, u], axis=1), right[...], (((1,), (1,)), ((), ())), preferred_element_type=F32
        )
        for sub in range(8):
            at, x = part * 2 + sub // 4, sub % 4
            y, z = at // 4, at % 4
            block = total[sub * 64 : (sub + 1) * 64]
            k = lax.rem(jnp.where(core == 0, x, z) - s1 + 4, 4)
            j = jnp.where(core == 0, at, y * 4 + x)
            rows = pl.ds(pl.multiple_of(j * 64, 64), 64)
            code, scale = _pack(block)
            tops[pl.ds(k, 1), pl.ds(j, 1), :] = scale[None]
            blocks[pl.ds(k, 1), rows, :] = block[None]
            codes[pl.ds(k, 1), rows, :] = code[None]
    for out, earlier in zip((own, c1, c2, c3), before):
        out[0] = earlier[0]
    c = own.shape[0] - 1
    own[c] = blocks[0]
    for n, out in ((1, c1), (2, c2), (3, c3)):
        out[c, 0:512, :] = codes[n]
        out[c, 512:528, :] = jnp.concatenate([tops[n], tops[n]], axis=0).astype(BF16)


def grad_in(ids, wg, wu, mine, theirs, before):
    half, width = mine[0].shape
    tokens, three = 2 * half, 3 * width
    n = 1 + (len(before) > 0)
    code = shape((n, 528, tokens), BF16)
    return _call(
        functools.partial(_grad_in_body, width, len(before)),
        (shape((2 * tokens, three), BF16), shape((n, 512, tokens), F32), code, code, code, TICK),
        LARGE,
        in_specs=[SMEM] + [VMEM] * (8 + len(before)),
        out_specs=(VMEM,) * 6,
        scratch_shapes=[
            pltpu.VMEM((tokens, 4 * width), BF16),
            pltpu.VMEM((4, 8, tokens), F32),
            pltpu.VMEM((4, 512, tokens), F32),
            pltpu.VMEM((4, 512, tokens), BF16),
        ],
        cost_estimate=_cost(
            flops=8 * tokens * 2048 * width, bytes_accessed=4 * 2048 * width + 16 * tokens * three, transcendentals=2048 * tokens
        ),
    )(ids, wg, wu, *mine, *theirs, *before)


def _twice(rows, c):
    half = rows.shape[1] // 2
    part = rows[:, c * half : (c + 1) * half]
    return jnp.concatenate([part, part], axis=1)


def _grad_up_body(x, d0, d1, out):
    rows = x[0]
    total = jnp.dot(_twice(rows, 0), d0[...], preferred_element_type=F32)
    total = total + jnp.dot(_twice(rows, 1), d1[...], preferred_element_type=F32)
    out[...] = total.astype(BF16)


def grad_weight(acts, pairs, place, width):
    depth, tokens = acts.shape[1:]
    delta = pl.BlockSpec((tokens, width), lambda i: (0, place))
    return _call(
        _grad_up_body,
        shape((depth, width), BF16),
        WHOLE,
        grid=(depth // 512,),
        in_specs=[pl.BlockSpec((1, 512, tokens), lambda i: (0, i, 0))] + [delta] * 2,
        out_specs=pl.BlockSpec((512, width), lambda i: (i, 0)),
        cost_estimate=_cost(
            flops=COST * 4 * tokens * depth * width, bytes_accessed=COST * 4 * depth * width, transcendentals=0
        ),
    )(acts, *pairs)


def _grad_down_body(g, h0, h1, out, turned):
    @pl.when(pl.program_id(0) == 0)
    def _():
        for i, h in enumerate((h0, h1)):
            turned[i] = h[...].T

    rows, dims = g[0], (((1,), (1,)), ((), ()))
    total = lax.dot_general(turned[0], _twice(rows, 0), dims, preferred_element_type=F32)
    total = total + lax.dot_general(turned[1], _twice(rows, 1), dims, preferred_element_type=F32)
    out[...] = total.astype(BF16)


def grad_down_weight(acts, pairs, width):
    depth, tokens = acts.shape[1:]
    hidden = pl.BlockSpec((tokens, width), lambda i: (0, 0))
    return _call(
        _grad_down_body,
        shape((width, depth), BF16),
        WHOLE,
        grid=(depth // 512,),
        in_specs=[pl.BlockSpec((1, 512, tokens), lambda i: (1, i, 0))] + [hidden] * 2,
        out_specs=pl.BlockSpec((width, 512), lambda i: (0, i)),
        scratch_shapes=[pltpu.VMEM((2, width, tokens), BF16)],
        cost_estimate=_cost(
            flops=COST * 4 * tokens * depth * width, bytes_accessed=COST * 4 * depth * width, transcendentals=0
        ),
    )(acts, *pairs)


def _sum_first_body(ids, own, r1, r2, r3, own2, c1, c2, c3, tops):
    s2 = ids[3]
    for c in range(2):
        scales = [r[c, 512:528, :].astype(F32) for r in (r1, r2, r3)]
        for j in range(8):
            rows = slice(j * 64, (j + 1) * 64)
            total = own[c, rows, :]
            for r, scale in zip((r1, r2, r3), scales):
                total = total + _unpack(r[c, rows, :], scale[j : j + 1])
            y, place = j // 4, j % 4
            k = lax.rem(place - s2 + 4, 4)
            code, scale = _pack(total)
            tops[pl.ds(k, 1), y : y + 1, :] = scale[None]
            to = slice(y * 64, (y + 1) * 64)

            @pl.when(k == 0)
            def _():
                own2[c, to, :] = total

            for n, out in ((1, c1), (2, c2), (3, c3)):

                @pl.when(k == n)
                def _():
                    out[c, to, :] = code

        for n, out in ((1, c1), (2, c2), (3, c3)):
            out[c, 128:144, :] = jnp.concatenate([tops[n], tops[n]], axis=0).astype(BF16)


def sum_first(ids, own, received):
    tokens = own.shape[2]
    code = shape((2, 144, tokens), BF16)
    return _call(
        _sum_first_body,
        (shape((2, 128, tokens), F32), code, code, code),
        in_specs=[SMEM] + [VMEM] * 4,
        out_specs=(VMEM,) * 4,
        scratch_shapes=[pltpu.VMEM((4, 8, tokens), F32)],
    )(ids, own, *received)


def _sum_second_body(ids, own, r1, r2, r3, own3, out):
    for c in range(2):
        scales = [r[c, 128:144, :].astype(F32) for r in (r1, r2, r3)]
        for y in range(2):
            rows = slice(y * 64, (y + 1) * 64)
            total = own[c, rows, :]
            for r, scale in zip((r1, r2, r3), scales):
                total = total + _unpack(r[c, rows, :], scale[y : y + 1])

            @pl.when(ids[1] == y)
            def _():
                own3[c] = total

            @pl.when(ids[1] != y)
            def _():
                code, top = _pack(total)
                out[c, 0:64, :] = code
                out[c, 64:80, :] = jnp.broadcast_to(top, (16, top.shape[1])).astype(BF16)


def sum_second(ids, own, received):
    tokens = own.shape[2]
    return _call(
        _sum_second_body,
        (shape((2, 64, tokens), F32), shape((2, 80, tokens), BF16)),
        in_specs=[SMEM] + [VMEM] * 4,
        out_specs=(VMEM,) * 2,
    )(ids, own, *received)


def _sum_last_body(own, r, out):
    tokens = own.shape[2]
    for c in range(2):
        total = own[c] + _unpack(r[c, 0:64, :], r[c, 64:80, :].astype(F32)[0:1])
        out[:, c * tokens : (c + 1) * tokens] = total.astype(BF16)


def sum_last(own, received):
    return _call(
        _sum_last_body, shape((64, 2 * own.shape[2]), BF16), in_specs=[VMEM] * 2, out_specs=VMEM
    )(own, received)


def per_device(inputs, grad_out, gate_weight, up_weight, down_weight):
    width = gate_weight.shape[1]
    mp = lax.axis_index("mp")
    core = lax.axis_index("dp") % 2
    y, z, x = mp // 16, (mp // 4) % 4, mp % 4
    ids = jnp.stack([core, y, jnp.where(core == 0, x, z), jnp.where(core == 0, z, x)]).astype(jnp.int32)
    both = jnp.stack([inputs.T, grad_out.T])
    pair = jnp.stack([both, _send(both, _over_y)])
    some = jnp.stack([pair] + [_send(pair, _first(-k)) for k in (1, 2, 3)])
    pieces = [some] + [_send(some, _second(-k)) for k in (1, 2, 3)]
    mine0, mine1, *theirs, acts = forward(ids, pieces, gate_weight, up_weight, down_weight)
    chips, codes = [], []
    for mine, others in ((mine0, theirs[:3]), (mine1, theirs[3:])):
        chip, code, tick = chip_sum(mine, [_send(v, _over_core) for v in others])
        chips.append(chip)
        codes.append(_send(code, _over_lo))
    pairs, part = [], ()
    for chip, code in zip(chips, codes):
        act = activations(chip, code, tick)
        others = [_send(v, _over_core) for v in act]
        delta, *part, tick = grad_in(ids, gate_weight, up_weight, act, others, part)
        pairs.append(delta)
    own, *rest = part
    own, *rest = sum_first(ids, own, [_send(v, _first(k + 1)) for k, v in enumerate(rest)])
    own, last = sum_second(ids, own, [_send(v, _second(k + 1)) for k, v in enumerate(rest)])
    grad_inputs = sum_last(own, _send(last, _over_y)).T
    grad_gate = grad_weight(acts, pairs, 1, width)
    grad_up = grad_weight(acts, pairs, 2, width)
    grad_down = grad_down_weight(acts, pairs, width)
    return (grad_inputs, grad_gate, grad_up, grad_down)


def solution(mesh):
    placed = (
        P(None, ("dp", "mp")),
        P(None, ("dp", "mp")),
        P("dp", "mp"),
        P("dp", "mp"),
        P("mp", "dp"),
    )
    return jax.shard_map(
        per_device,
        mesh=mesh,
        in_specs=placed,
        out_specs=(P(None, ("dp", "mp")), P("dp", "mp"), P("dp", "mp"), P("mp", "dp")),
        check_vma=False,
    )
```

profile of v0, /device:TPU:0, one launch (start us, length us, event | category | flops | bytes accessed | tf_op | source)
XLA Modules:
  0.0 165.3 jit_solution(3513305797902828255)
XLA Ops:
  0.6 0.9 fusion
  1.5 3.4 %collective-permute-start = (bf16[2,64,512]{2,1,0:T(8,128)(2,1)S(1)}, bf16[2,64,512]{2,1,0:T(8,128)(2,1)S(1)}, u32[]{:S(2)}, u32[]{:S(2)}) collective-permute-start(bf16[2,64,512]{2,1,0:T(8,128)(2,1)S(1)} %get-tuple-element.81), channel_id=1, source_target_pairs={{0,16},{1,17},{2,18},{3,19},{4,20},{5,21},{6,22},{7,23},{8,24},{9,... | collective-permute-start | bytes 393224 | tf_op jit(solution)/shard_map/ppermute | solution.py:26
  4.9 3.5 %collective-permute-done = bf16[2,64,512]{2,1,0:T(8,128)(2,1)S(1)} collective-permute-done((bf16[2,64,512]{2,1,0:T(8,128)(2,1)S(1)}, bf16[2,64,512]{2,1,0:T(8,128)(2,1)S(1)}, u32[]{:S(2)}, u32[]{:S(2)}) %collective-permute-start) | collective-permute-done | bytes 131104 | tf_op jit(solution)/shard_map/ppermute | solution.py:26
  8.4 3.2 %collective-permute-start.2 = (bf16[2,2,64,512]{3,2,1,0:T(8,128)(2,1)S(1)}, bf16[2,2,64,512]{3,2,1,0:T(8,128)(2,1)S(1)}, u32[]{:S(2)}, u32[]{:S(2)}) collective-permute-start(bf16[2,2,64,512]{3,2,1,0:T(8,128)(2,1)S(1)} %get-tuple-element.79), channel_id=1, source_target_pairs={{0,2},{1,3},{2,0},{3,1},{4,6},{5,7},{6,4},{7,5},{8,10},{9,11},{10,... | collective-permute-start | bytes 786440 | tf_op jit(solution)/shard_map/ppermute | solution.py:26
  11.6 1.1 collective-permute-start.1
  12.7 0.9 collective-permute-start.3
  13.6 2.8 %collective-permute-done.2 = bf16[2,2,64,512]{3,2,1,0:T(8,128)(2,1)S(1)} collective-permute-done((bf16[2,2,64,512]{3,2,1,0:T(8,128)(2,1)S(1)}, bf16[2,2,64,512]{3,2,1,0:T(8,128)(2,1)S(1)}, u32[]{:S(2)}, u32[]{:S(2)}) %collective-permute-start.2) | collective-permute-done | bytes 262176 | tf_op jit(solution)/shard_map/ppermute | solution.py:26
  16.4 3.0 %collective-permute-done.1 = bf16[2,2,64,512]{3,2,1,0:T(8,128)(2,1)S(1)} collective-permute-done((bf16[2,2,64,512]{3,2,1,0:T(8,128)(2,1)S(1)}, bf16[2,2,64,512]{3,2,1,0:T(8,128)(2,1)S(1)}, u32[]{:S(2)}, u32[]{:S(2)}) %collective-permute-start.1) | collective-permute-done | bytes 262176 | tf_op jit(solution)/shard_map/ppermute | solution.py:26
  19.3 1.0 collective-permute-done.3
  20.4 2.0 %collective-permute-start.6 = (bf16[4,2,2,64,512]{4,3,2,1,0:T(8,128)(2,1)S(1)}, bf16[4,2,2,64,512]{4,3,2,1,0:T(8,128)(2,1)S(1)}, u32[]{:S(2)}, u32[]{:S(2)}) collective-permute-start(bf16[4,2,2,64,512]{4,3,2,1,0:T(8,128)(2,1)S(1)} %pad_maximum_fusion.p0), channel_id=1, source_target_pairs={{0,4},{1,5},{2,6},{3,7},{4,8},{5,9},{6,10},{7,11},{8,12},{9,13},{1... | collective-permute-start | bytes 3145736 | tf_op jit(solution)/shard_map/ppermute | solution.py:26
  22.4 3.6 %collective-permute-start.5 = (bf16[4,2,2,64,512]{4,3,2,1,0:T(8,128)(2,1)S(1)}, bf16[4,2,2,64,512]{4,3,2,1,0:T(8,128)(2,1)S(1)}, u32[]{:S(2)}, u32[]{:S(2)}) collective-permute-start(bf16[4,2,2,64,512]{4,3,2,1,0:T(8,128)(2,1)S(1)} %pad_maximum_fusion.p0), channel_id=1, source_target_pairs={{0,8},{1,9},{2,10},{3,11},{4,12},{5,13},{6,14},{7,15},{8,0},{9,1},... | collective-permute-start | bytes 3145736 | tf_op jit(solution)/shard_map/ppermute | solution.py:26
  26.0 1.0 collective-permute-start.4
  27.6 9.7 %collective-permute-done.6.p3 = bf16[4,2,2,64,512]{4,3,2,1,0:T(8,128)(2,1)S(1)} collective-permute-done((bf16[4,2,2,64,512]{4,3,2,1,0:T(8,128)(2,1)S(1)}, bf16[4,2,2,64,512]{4,3,2,1,0:T(8,128)(2,1)S(1)}, u32[]{:S(2)}, u32[]{:S(2)}) %collective-permute-start.6) | collective-permute-done | bytes 1048608 | tf_op jit(solution)/shard_map/ppermute | solution.py:26
  37.3 12.7 %collective-permute-done.5.p2 = bf16[4,2,2,64,512]{4,3,2,1,0:T(8,128)(2,1)S(1)} collective-permute-done((bf16[4,2,2,64,512]{4,3,2,1,0:T(8,128)(2,1)S(1)}, bf16[4,2,2,64,512]{4,3,2,1,0:T(8,128)(2,1)S(1)}, u32[]{:S(2)}, u32[]{:S(2)}) %collective-permute-start.5) | collective-permute-done | bytes 1048608 | tf_op jit(solution)/shard_map/ppermute | solution.py:26
  50.0 0.9 copy-done.9
  51.0 15.8 %shard_map.84 = (f32[128,2688]{1,0:T(8,128)}, f32[128,2688]{1,0:T(8,128)}, f32[128,896]{1,0:T(8,128)}, f32[128,896]{1,0:T(8,128)}, f32[128,896]{1,0:T(8,128)}, /...) custom-call(s32[4]{0:T(128)} %pad_add_fusion.ids, ...), custom_call_target="tpu_custom_call" | custom-call | flops 281857216 | bytes 969932 | tf_op jit(solution)/shard_map/pallas_call | solution.py:136
  67.5 1.4 collective-permute-done.11.o0
  70.2 1.3 copy-done.3
  71.6 1.0 shard_map.86
  72.6 1.7 collective-permute-start.14
  74.8 1.5 collective-permute-done.7.o0
  76.3 0.7 collective-permute-done.8.o1
  77.6 1.3 copy-done.2
  78.9 1.1 shard_map.85
  80.5 11.1 %collective-permute-done.14.code = bf16[128,2816]{1,0:T(8,128)(2,1)S(1)} collective-permute-done((bf16[128,2816]{1,0:T(8,128)(2,1)S(1)}, bf16[128,2816]{1,0:T(8,128)(2,1)S(1)}, u32[]{:S(2)}, u32[]{:S(2)}) %collective-permute-start.14) | collective-permute-done | bytes 720928 | tf_op jit(solution)/shard_map/ppermute | solution.py:26
  91.7 1.3 shard_map.87
  93.6 1.2 collective-permute-done.15.o0
  96.1 6.1 %shard_map.88 = (bf16[512,2688]{1,0:T(8,128)(2,1)S(1)}, f32[1,512,256]{2,1,0:T(8,128)S(1)}, bf16[1,528,256]{2,1,0:T(8,128)(2,1)S(1)}, bf16[1,528,256]{2,1,0:T(8,...) custom-call(s32[4]{0:T(128)S(1)} %copy-done.4, bf16[2048,896]{1,0:T(8,128)(2,1)S(1)} %copy-done, ...), custom_call_target="tpu_custom_call" | custom-call | flops 187904816 | bytes 917504 | tf_op jit(solution)/shard_map/pallas_call | solution.py:270
  102.2 1.6 copy-done.5
  103.8 2.5 %collective-permute-done.10.code = bf16[128,2816]{1,0:T(8,128)(2,1)S(1)} collective-permute-done((bf16[128,2816]{1,0:T(8,128)(2,1)S(1)}, bf16[128,2816]{1,0:T(8,128)(2,1)S(1)}, u32[]{:S(2)}, u32[]{:S(2)}) %collective-permute-start.10) | collective-permute-done | bytes 720928 | tf_op jit(solution)/shard_map/ppermute | solution.py:26
  106.3 1.3 shard_map.89
  108.2 1.2 collective-permute-done.18.o0
  110.8 8.4 %shard_map.90 = (bf16[512,2688]{1,0:T(8,128)(2,1)S(1)}, f32[2,512,256]{2,1,0:T(8,128)S(1)}, bf16[2,528,256]{2,1,0:T(8,128)(2,1)}, bf16[2,528,256]{2,1,0:T(8,128)...) custom-call(s32[4]{0:T(128)S(1)} %copy-done.4, bf16[2048,896]{1,0:T(8,128)(2,1)S(1)} %copy-done, ...), custom_call_target="tpu_custom_call" | custom-call | flops 187904816 | bytes 917504 | tf_op jit(solution)/shard_map/pallas_call | solution.py:270
  119.2 1.6 copy-done.6
  121.2 2.7 %collective-permute-start.22 = (bf16[2,528,256]{2,1,0:T(8,128)(2,1)S(1)}, bf16[2,528,256]{2,1,0:T(8,128)(2,1)S(1)}, u32[]{:S(2)}, u32[]{:S(2)}) collective-permute-start(bf16[2,528,256]{2,1,0:T(8,128)(2,1)S(1)} %get-tuple-element.67), channel_id=1, source_target_pairs={{0,2},{1,3},{2,0},{3,1},{4,6},{5,7},{6,4},{7,5},{8,10},{9,11},{10,... | collective-permute-start | bytes 1622024 | tf_op jit(solution)/shard_map/ppermute | solution.py:26
  123.9 1.4 collective-permute-start.23
  125.4 8.0 %shard_map.96 = bf16[896,2048]{1,0:T(8,128)(2,1)} custom-call(bf16[2,2048,512]{2,1,0:T(8,128)(2,1)} %get-tuple-element.75.x.g, bf16[512,2688]{1,0:T(8,128)(2,1)} %copy-done.5, bf16[512,2688]{1,0:T(8,128)(2,1)} %copy-done.6), custom_call_target="tpu_custom_call" | custom-call | flops 3758096384 | bytes 7340032 | tf_op jit(solution)/shard_map/pallas_call | solution.py:332
  133.4 3.9 %collective-permute-done.22.r2 = bf16[2,528,256]{2,1,0:T(8,128)(2,1)S(1)} collective-permute-done((bf16[2,528,256]{2,1,0:T(8,128)(2,1)S(1)}, bf16[2,528,256]{2,1,0:T(8,128)(2,1)S(1)}, u32[]{:S(2)}, u32[]{:S(2)}) %collective-permute-start.22) | collective-permute-done | bytes 540704 | tf_op jit(solution)/shard_map/ppermute | solution.py:26
  137.3 0.7 collective-permute-done.23.r3
  138.0 2.5 %shard_map.91 = (f32[2,128,256]{2,1,0:T(8,128)S(1)}, bf16[2,144,256]{2,1,0:T(8,128)(2,1)S(1)}, bf16[2,144,256]{2,1,0:T(8,128)(2,1)S(1)}, bf16[2,144,256]{2,1,0:T(8,128)(2,1)S(1)}) custom-call(s32[4]{0:T(128)S(1)} %copy-done.4, f32[2,512,256]{2,1,0:T(8,128)S(1)} %get-tuple-element.65.own, bf16[2,528,256]{2,1,0:T(8,128)(2,1)S(1)} %collective-permute-done.21.r1, ...), custom_call_target="tpu_custom_call" | custom-call | tf_op jit(solution)/shard_map/pallas_call | solution.py:378
  140.5 0.7 collective-permute-start.24
  141.2 2.1 %collective-permute-start.25 = (bf16[2,144,256]{2,1,0:T(8,128)(2,1)S(1)}, bf16[2,144,256]{2,1,0:T(8,128)(2,1)S(1)}, u32[]{:S(2)}, u32[]{:S(2)}) collective-permute-start(bf16[2,144,256]{2,1,0:T(8,128)(2,1)S(1)} %get-tuple-element.71), channel_id=1, source_target_pairs={{0,8},{1,9},{2,10},{3,11},{4,12},{5,13},{6,14},{7,15},{8,0},{9,1},... | collective-permute-start | bytes 442376 | tf_op jit(solution)/shard_map/ppermute | solution.py:26
  143.4 1.5 collective-permute-start.26
  144.9 7.7 %shard_map.95 = bf16[2048,896]{1,0:T(8,128)(2,1)} custom-call(bf16[2,2048,512]{2,1,0:T(8,128)(2,1)} %get-tuple-element.75.x.g, bf16[512,2688]{1,0:T(8,128)(2,1)} %copy-done.5, bf16[512,2688]{1,0:T(8,128)(2,1)} %copy-done.6), custom_call_target="tpu_custom_call" | custom-call | flops 3758096384 | bytes 7340032 | tf_op jit(solution)/shard_map/pallas_call | solution.py:304
  152.6 0.9 shard_map.92
  153.6 3.3 %collective-permute-start.27 = (bf16[2,80,256]{2,1,0:T(8,128)(2,1)S(1)}, bf16[2,80,256]{2,1,0:T(8,128)(2,1)S(1)}, u32[]{:S(2)}, u32[]{:S(2)}) collective-permute-start(bf16[2,80,256]{2,1,0:T(8,128)(2,1)S(1)} %get-tuple-element.74), channel_id=1, source_target_pairs={{0,16},{1,17},{2,18},{3,19},{4,20},{5,21},{6,22},{7,23},{8,24},{9,... | collective-permute-start | bytes 245768 | tf_op jit(solution)/shard_map/ppermute | solution.py:26
  156.8 7.7 %shard_map.94 = bf16[2048,896]{1,0:T(8,128)(2,1)} custom-call(bf16[2,2048,512]{2,1,0:T(8,128)(2,1)} %get-tuple-element.75.x.g, bf16[512,2688]{1,0:T(8,128)(2,1)} %copy-done.5, bf16[512,2688]{1,0:T(8,128)(2,1)} %copy-done.6), custom_call_target="tpu_custom_call" | custom-call | flops 3758096384 | bytes 7340032 | tf_op jit(solution)/shard_map/pallas_call | solution.py:304
  164.6 0.7 shard_map.93
  (45 shorter events, 9.0 us)
Async XLA Ops:
  1.5 6.9 %collective-permute-start = (bf16[2,64,512]{2,1,0:T(8,128)(2,1)S(1)}, bf16[2,64,512]{2,1,0:T(8,128)(2,1)S(1)}, u32[]{:S(2)}, u32[]{:S(2)}) collective-permute-start(bf16[2,64,512]{2,1,0:T(8,128)(2,1)S(1)} %get-tuple-element.81), channel_id=1, source_target_pairs={{0,16},{1,17},{2,18},{3,19},{4,20},{5,21},{6,22},{7,23},{8,24},{9,... | collective-permute-start | bytes 393224 | tf_op jit(solution)/shard_map/ppermute | solution.py:26
  8.4 8.0 %collective-permute-start.2 = (bf16[2,2,64,512]{3,2,1,0:T(8,128)(2,1)S(1)}, bf16[2,2,64,512]{3,2,1,0:T(8,128)(2,1)S(1)}, u32[]{:S(2)}, u32[]{:S(2)}) collective-permute-start(bf16[2,2,64,512]{3,2,1,0:T(8,128)(2,1)S(1)} %get-tuple-element.79), channel_id=1, source_target_pairs={{0,2},{1,3},{2,0},{3,1},{4,6},{5,7},{6,4},{7,5},{8,10},{9,11},{10,... | collective-permute-start | bytes 786440 | tf_op jit(solution)/shard_map/ppermute | solution.py:26
  11.6 7.8 %collective-permute-start.1 = (bf16[2,2,64,512]{3,2,1,0:T(8,128)(2,1)S(1)}, bf16[2,2,64,512]{3,2,1,0:T(8,128)(2,1)S(1)}, u32[]{:S(2)}, u32[]{:S(2)}) collective-permute-start(bf16[2,2,64,512]{3,2,1,0:T(8,128)(2,1)S(1)} %get-tuple-element.79), channel_id=1, source_target_pairs={{0,3},{1,0},{2,1},{3,2},{4,7},{5,4},{6,5},{7,6},{8,11},{9,8},{10,9... | collective-permute-start | bytes 786440 | tf_op jit(solution)/shard_map/ppermute | solution.py:26
  12.7 7.6 %collective-permute-start.3 = (bf16[2,2,64,512]{3,2,1,0:T(8,128)(2,1)S(1)}, bf16[2,2,64,512]{3,2,1,0:T(8,128)(2,1)S(1)}, u32[]{:S(2)}, u32[]{:S(2)}) collective-permute-start(bf16[2,2,64,512]{3,2,1,0:T(8,128)(2,1)S(1)} %get-tuple-element.79), channel_id=1, source_target_pairs={{0,1},{1,2},{2,3},{3,0},{4,5},{5,6},{6,7},{7,4},{8,9},{9,10},{10,1... | collective-permute-start | bytes 786440 | tf_op jit(solution)/shard_map/ppermute | solution.py:26
  20.4 29.6 %copy-start.7 = (bf16[4,2,2,64,512]{4,3,2,1,0:T(8,128)(2,1)}, bf16[4,2,2,64,512]{4,3,2,1,0:T(8,128)(2,1)S(1)}, u32[]{:S(2)}) copy-start(bf16[4,2,2,64,512]{4,3,2,1,0:T(8,128)(2,1)S(1)} %pad_maximum_fusion.p0) | copy-start | bytes 3145732
  20.4 16.9 %collective-permute-start.6 = (bf16[4,2,2,64,512]{4,3,2,1,0:T(8,128)(2,1)S(1)}, bf16[4,2,2,64,512]{4,3,2,1,0:T(8,128)(2,1)S(1)}, u32[]{:S(2)}, u32[]{:S(2)}) collective-permute-start(bf16[4,2,2,64,512]{4,3,2,1,0:T(8,128)(2,1)S(1)} %pad_maximum_fusion.p0), channel_id=1, source_target_pairs={{0,4},{1,5},{2,6},{3,7},{4,8},{5,9},{6,10},{7,11},{8,12},{9,13},{1... | collective-permute-start | bytes 3145736 | tf_op jit(solution)/shard_map/ppermute | solution.py:26
  22.4 27.6 %collective-permute-start.5 = (bf16[4,2,2,64,512]{4,3,2,1,0:T(8,128)(2,1)S(1)}, bf16[4,2,2,64,512]{4,3,2,1,0:T(8,128)(2,1)S(1)}, u32[]{:S(2)}, u32[]{:S(2)}) collective-permute-start(bf16[4,2,2,64,512]{4,3,2,1,0:T(8,128)(2,1)S(1)} %pad_maximum_fusion.p0), channel_id=1, source_target_pairs={{0,8},{1,9},{2,10},{3,11},{4,12},{5,13},{6,14},{7,15},{8,0},{9,1},... | collective-permute-start | bytes 3145736 | tf_op jit(solution)/shard_map/ppermute | solution.py:26
  26.0 24.0 %collective-permute-start.4 = (bf16[4,2,2,64,512]{4,3,2,1,0:T(8,128)(2,1)S(1)}, bf16[4,2,2,64,512]{4,3,2,1,0:T(8,128)(2,1)}, u32[]{:S(2)}, u32[]{:S(2)}) collective-permute-start(bf16[4,2,2,64,512]{4,3,2,1,0:T(8,128)(2,1)S(1)} %pad_maximum_fusion.p0), channel_id=1, source_target_pairs={{0,12},{1,13},{2,14},{3,15},{4,0},{5,1},{6,2},{7,3},{8,4},{9,5},{1... | collective-permute-start | bytes 3145736 | tf_op jit(solution)/shard_map/ppermute | solution.py:26
  37.3 12.7 %copy-start.8 = (bf16[4,2,2,64,512]{4,3,2,1,0:T(8,128)(2,1)}, bf16[4,2,2,64,512]{4,3,2,1,0:T(8,128)(2,1)S(1)}, u32[]{:S(2)}) copy-start(bf16[4,2,2,64,512]{4,3,2,1,0:T(8,128)(2,1)S(1)} %collective-permute-done.6.p3) | copy-start | bytes 3145732
  50.0 1.0 copy-start.9
  66.8 2.1 %collective-permute-start.11 = (f32[128,896]{1,0:T(8,128)}, f32[128,896]{1,0:T(8,128)S(1)}, u32[]{:S(2)}, u32[]{:S(2)}) collective-permute-start(f32[128,896]{1,0:T(8,128)} %get-tuple-element.48), channel_id=1, source_target_pairs={{0,32},{1,33},{2,34},{3,35},{4,36},{5,37},{6,38},{7,39},{8,40},{9,... | collective-permute-start | bytes 1376264 | tf_op jit(solution)/shard_map/ppermute | solution.py:26
  66.9 2.7 %collective-permute-start.12 = (f32[128,896]{1,0:T(8,128)}, f32[128,896]{1,0:T(8,128)S(1)}, u32[]{:S(2)}, u32[]{:S(2)}) collective-permute-start(f32[128,896]{1,0:T(8,128)} %get-tuple-element.49), channel_id=1, source_target_pairs={{0,32},{1,33},{2,34},{3,35},{4,36},{5,37},{6,38},{7,39},{8,40},{9,... | collective-permute-start | bytes 1376264 | tf_op jit(solution)/shard_map/ppermute | solution.py:26
  67.4 2.8 %collective-permute-start.13 = (f32[128,896]{1,0:T(8,128)}, f32[128,896]{1,0:T(8,128)S(1)}, u32[]{:S(2)}, u32[]{:S(2)}) collective-permute-start(f32[128,896]{1,0:T(8,128)} %get-tuple-element.50), channel_id=1, source_target_pairs={{0,32},{1,33},{2,34},{3,35},{4,36},{5,37},{6,38},{7,39},{8,40},{9,... | collective-permute-start | bytes 1376264 | tf_op jit(solution)/shard_map/ppermute | solution.py:26
  70.2 25.9 %copy-start.4 = (s32[4]{0:T(128)S(1)}, s32[4]{0:T(128)}, u32[]{:S(2)}) copy-start(s32[4]{0:T(128)} %pad_add_fusion.ids) | copy-start | bytes 52
  70.2 1.3 copy-start.3
  71.6 24.6 %copy-start = (bf16[2048,896]{1,0:T(8,128)(2,1)S(1)}, bf16[2048,896]{1,0:T(8,128)(2,1)}, u32[]{:S(2)}) copy-start(bf16[2048,896]{1,0:T(8,128)(2,1)} %wg.5) | copy-start | bytes 11010052
  71.6 24.6 %copy-start.1 = (bf16[2048,896]{1,0:T(8,128)(2,1)S(1)}, bf16[2048,896]{1,0:T(8,128)(2,1)}, u32[]{:S(2)}) copy-start(bf16[2048,896]{1,0:T(8,128)(2,1)} %wu.5) | copy-start | bytes 11010052
  72.6 19.1 %collective-permute-start.14 = (bf16[128,2816]{1,0:T(8,128)(2,1)S(1)}, bf16[128,2816]{1,0:T(8,128)(2,1)S(1)}, u32[]{:S(2)}, u32[]{:S(2)}) collective-permute-start(bf16[128,2816]{1,0:T(8,128)(2,1)S(1)} %get-tuple-element.52), channel_id=1, source_target_pairs={{0,64},{1,65},{2,66},{3,67},{4,68},{5,69},{6,70},{7,71},{8,72},{9,... | collective-permute-start | bytes 2162696 | tf_op jit(solution)/shard_map/ppermute | solution.py:26
  74.2 2.0 %collective-permute-start.7 = (f32[128,896]{1,0:T(8,128)}, f32[128,896]{1,0:T(8,128)S(1)}, u32[]{:S(2)}, u32[]{:S(2)}) collective-permute-start(f32[128,896]{1,0:T(8,128)} %get-tuple-element.42), channel_id=1, source_target_pairs={{0,32},{1,33},{2,34},{3,35},{4,36},{5,37},{6,38},{7,39},{8,40},{9,... | collective-permute-start | bytes 1376264 | tf_op jit(solution)/shard_map/ppermute | solution.py:26
  74.2 2.7 %collective-permute-start.8 = (f32[128,896]{1,0:T(8,128)}, f32[128,896]{1,0:T(8,128)S(1)}, u32[]{:S(2)}, u32[]{:S(2)}) collective-permute-start(f32[128,896]{1,0:T(8,128)} %get-tuple-element.43), channel_id=1, source_target_pairs={{0,32},{1,33},{2,34},{3,35},{4,36},{5,37},{6,38},{7,39},{8,40},{9,... | collective-permute-start | bytes 1376264 | tf_op jit(solution)/shard_map/ppermute | solution.py:26
  74.8 2.8 %collective-permute-start.9 = (f32[128,896]{1,0:T(8,128)}, f32[128,896]{1,0:T(8,128)S(1)}, u32[]{:S(2)}, u32[]{:S(2)}) collective-permute-start(f32[128,896]{1,0:T(8,128)} %get-tuple-element.44), channel_id=1, source_target_pairs={{0,32},{1,33},{2,34},{3,35},{4,36},{5,37},{6,38},{7,39},{8,40},{9,... | collective-permute-start | bytes 1376264 | tf_op jit(solution)/shard_map/ppermute | solution.py:26
  77.6 1.3 copy-start.2
  80.0 26.3 %collective-permute-start.10 = (bf16[128,2816]{1,0:T(8,128)(2,1)S(1)}, bf16[128,2816]{1,0:T(8,128)(2,1)S(1)}, u32[]{:S(2)}, u32[]{:S(2)}) collective-permute-start(bf16[128,2816]{1,0:T(8,128)(2,1)S(1)} %get-tuple-element.46), channel_id=1, source_target_pairs={{0,64},{1,65},{2,66},{3,67},{4,68},{5,69},{6,70},{7,71},{8,72},{9,... | collective-permute-start | bytes 2162696 | tf_op jit(solution)/shard_map/ppermute | solution.py:26
  92.9 1.9 %collective-permute-start.15 = (f32[128,896]{1,0:T(8,128)S(1)}, f32[128,896]{1,0:T(8,128)S(1)}, u32[]{:S(2)}, u32[]{:S(2)}) collective-permute-start(f32[128,896]{1,0:T(8,128)S(1)} %get-tuple-element.54.m0), channel_id=1, source_target_pairs={{0,32},{1,33},{2,34},{3,35},{4,36},{5,37},{6,38},{7,39},{8,40},{9,... | collective-permute-start | bytes 1376264 | tf_op jit(solution)/shard_map/ppermute | solution.py:26
  93.0 2.5 %collective-permute-start.16 = (f32[128,896]{1,0:T(8,128)S(1)}, f32[128,896]{1,0:T(8,128)S(1)}, u32[]{:S(2)}, u32[]{:S(2)}) collective-permute-start(f32[128,896]{1,0:T(8,128)S(1)} %get-tuple-element.55.m1), channel_id=1, source_target_pairs={{0,32},{1,33},{2,34},{3,35},{4,36},{5,37},{6,38},{7,39},{8,40},{9,... | collective-permute-start | bytes 1376264 | tf_op jit(solution)/shard_map/ppermute | solution.py:26
  93.5 2.6 %collective-permute-start.17 = (f32[128,896]{1,0:T(8,128)S(1)}, f32[128,896]{1,0:T(8,128)S(1)}, u32[]{:S(2)}, u32[]{:S(2)}) collective-permute-start(f32[128,896]{1,0:T(8,128)S(1)} %get-tuple-element.56.m2), channel_id=1, source_target_pairs={{0,32},{1,33},{2,34},{3,35},{4,36},{5,37},{6,38},{7,39},{8,40},{9,... | collective-permute-start | bytes 1376264 | tf_op jit(solution)/shard_map/ppermute | solution.py:26
  102.2 1.6 copy-start.5
  107.6 1.9 %collective-permute-start.18 = (f32[128,896]{1,0:T(8,128)S(1)}, f32[128,896]{1,0:T(8,128)S(1)}, u32[]{:S(2)}, u32[]{:S(2)}) collective-permute-start(f32[128,896]{1,0:T(8,128)S(1)} %get-tuple-element.58.m0), channel_id=1, source_target_pairs={{0,32},{1,33},{2,34},{3,35},{4,36},{5,37},{6,38},{7,39},{8,40},{9,... | collective-permute-start | bytes 1376264 | tf_op jit(solution)/shard_map/ppermute | solution.py:26
  107.7 2.5 %collective-permute-start.19 = (f32[128,896]{1,0:T(8,128)S(1)}, f32[128,896]{1,0:T(8,128)S(1)}, u32[]{:S(2)}, u32[]{:S(2)}) collective-permute-start(f32[128,896]{1,0:T(8,128)S(1)} %get-tuple-element.59.m1), channel_id=1, source_target_pairs={{0,32},{1,33},{2,34},{3,35},{4,36},{5,37},{6,38},{7,39},{8,40},{9,... | collective-permute-start | bytes 1376264 | tf_op jit(solution)/shard_map/ppermute | solution.py:26
  108.2 2.6 %collective-permute-start.20 = (f32[128,896]{1,0:T(8,128)S(1)}, f32[128,896]{1,0:T(8,128)S(1)}, u32[]{:S(2)}, u32[]{:S(2)}) collective-permute-start(f32[128,896]{1,0:T(8,128)S(1)} %get-tuple-element.60.m2), channel_id=1, source_target_pairs={{0,32},{1,33},{2,34},{3,35},{4,36},{5,37},{6,38},{7,39},{8,40},{9,... | collective-permute-start | bytes 1376264 | tf_op jit(solution)/shard_map/ppermute | solution.py:26
  119.2 1.6 copy-start.6
  120.8 12.6 %collective-permute-start.21 = (bf16[2,528,256]{2,1,0:T(8,128)(2,1)}, bf16[2,528,256]{2,1,0:T(8,128)(2,1)S(1)}, u32[]{:S(2)}, u32[]{:S(2)}) collective-permute-start(bf16[2,528,256]{2,1,0:T(8,128)(2,1)} %get-tuple-element.66), channel_id=1, source_target_pairs={{0,1},{1,2},{2,3},{3,0},{4,5},{5,6},{6,7},{7,4},{8,9},{9,10},{10,1... | collective-permute-start | bytes 1622024 | tf_op jit(solution)/shard_map/ppermute | solution.py:26
  121.2 16.1 %collective-permute-start.22 = (bf16[2,528,256]{2,1,0:T(8,128)(2,1)S(1)}, bf16[2,528,256]{2,1,0:T(8,128)(2,1)S(1)}, u32[]{:S(2)}, u32[]{:S(2)}) collective-permute-start(bf16[2,528,256]{2,1,0:T(8,128)(2,1)S(1)} %get-tuple-element.67), channel_id=1, source_target_pairs={{0,2},{1,3},{2,0},{3,1},{4,6},{5,7},{6,4},{7,5},{8,10},{9,11},{10,... | collective-permute-start | bytes 1622024 | tf_op jit(solution)/shard_map/ppermute | solution.py:26
  123.9 14.1 %collective-permute-start.23 = (bf16[2,528,256]{2,1,0:T(8,128)(2,1)S(1)}, bf16[2,528,256]{2,1,0:T(8,128)(2,1)S(1)}, u32[]{:S(2)}, u32[]{:S(2)}) collective-permute-start(bf16[2,528,256]{2,1,0:T(8,128)(2,1)S(1)} %get-tuple-element.68), channel_id=1, source_target_pairs={{0,3},{1,0},{2,1},{3,2},{4,7},{5,4},{6,5},{7,6},{8,11},{9,8},{10,9... | collective-permute-start | bytes 1622024 | tf_op jit(solution)/shard_map/ppermute | solution.py:26
  140.5 12.1 %collective-permute-start.24 = (bf16[2,144,256]{2,1,0:T(8,128)(2,1)S(1)}, bf16[2,144,256]{2,1,0:T(8,128)(2,1)S(1)}, u32[]{:S(2)}, u32[]{:S(2)}) collective-permute-start(bf16[2,144,256]{2,1,0:T(8,128)(2,1)S(1)} %get-tuple-element.70), channel_id=1, source_target_pairs={{0,4},{1,5},{2,6},{3,7},{4,8},{5,9},{6,10},{7,11},{8,12},{9,13},{1... | collective-permute-start | bytes 442376 | tf_op jit(solution)/shard_map/ppermute | solution.py:26
  141.2 11.4 %collective-permute-start.25 = (bf16[2,144,256]{2,1,0:T(8,128)(2,1)S(1)}, bf16[2,144,256]{2,1,0:T(8,128)(2,1)S(1)}, u32[]{:S(2)}, u32[]{:S(2)}) collective-permute-start(bf16[2,144,256]{2,1,0:T(8,128)(2,1)S(1)} %get-tuple-element.71), channel_id=1, source_target_pairs={{0,8},{1,9},{2,10},{3,11},{4,12},{5,13},{6,14},{7,15},{8,0},{9,1},... | collective-permute-start | bytes 442376 | tf_op jit(solution)/shard_map/ppermute | solution.py:26
  143.4 9.3 %collective-permute-start.26 = (bf16[2,144,256]{2,1,0:T(8,128)(2,1)S(1)}, bf16[2,144,256]{2,1,0:T(8,128)(2,1)S(1)}, u32[]{:S(2)}, u32[]{:S(2)}) collective-permute-start(bf16[2,144,256]{2,1,0:T(8,128)(2,1)S(1)} %get-tuple-element.72), channel_id=1, source_target_pairs={{0,12},{1,13},{2,14},{3,15},{4,0},{5,1},{6,2},{7,3},{8,4},{9,5},{1... | collective-permute-start | bytes 442376 | tf_op jit(solution)/shard_map/ppermute | solution.py:26
  153.6 11.0 %collective-permute-start.27 = (bf16[2,80,256]{2,1,0:T(8,128)(2,1)S(1)}, bf16[2,80,256]{2,1,0:T(8,128)(2,1)S(1)}, u32[]{:S(2)}, u32[]{:S(2)}) collective-permute-start(bf16[2,80,256]{2,1,0:T(8,128)(2,1)S(1)} %get-tuple-element.74), channel_id=1, source_target_pairs={{0,16},{1,17},{2,18},{3,19},{4,20},{5,21},{6,22},{7,23},{8,24},{9,... | collective-permute-start | bytes 245768 | tf_op jit(solution)/shard_map/ppermute | solution.py:26
where the time goes:
time: 166 us; the launch traced here: 165 us
  Pallas kernels  62.4 us (38%)
  waiting for transfers between devices  61.5 us (37%)
  starting transfers between devices  32.1 us (19%)
  local copies, waits for them, and re-layouts  6.8 us (4%)
  other arithmetic  1.67 us (1%)
    ppermute x28, waiting for transfers between devices, _send(): return lax.ppermute(a, BOTH, _moves(shift))  61.5 us
    ppermute x28, starting transfers between devices, _send(): return lax.ppermute(a, BOTH, _moves(shift))  32.1 us
    pallas_call x1, Pallas kernels, forward(): _call(functools.partial(_forward_body, width), (mine,) * 2 + (other,) * 6...  15.8 us
    pallas_call x2, Pallas kernels, grad_weight(): _call(_grad_up_body, shape((depth, width), BF16), WHOLE, grid=(depth // 5...  15.5 us
    pallas_call x2, Pallas kernels, grad_in(): _call(functools.partial(_grad_in_body, width, len(before)), (shape((2 * t...  14.5 us
    pallas_call x1, Pallas kernels, grad_down_weight(): _call(_grad_down_body, shape((width, depth), BF16), WHOLE, grid=(depth //...  8.04 us
    unnamed x20, local copies, waits for them, and re-layouts  6.8 us
  transfers between devices with their start and end apart: 28, of which 22 were waited for; matrix products, arithmetic and copies ran while one was open for 0% of the time, Pallas kernels for 19%

commit v1 on v0

--- a/solution.py
+++ b/solution.py
@@ -83,31 +83,35 @@
 TICK = shape((8, 128), F32)
 
 
-def _forward_body(width, ids, p0, p1, p2, p3, wg, wu, wd, *rest):
-    mine, theirs, (acts, turned, held, last, loads, sems) = rest[:2], rest[2:8], rest[8:]
+def _forward_body(width, ids, *rest):
+    xs, gs, (wg, wu, wd), rest = rest[:4], rest[4:8], rest[8:11], rest[11:]
+    mine, theirs, (acts_out, acts, turned, held, last, sums, loads, stores, sems) = rest[:2], rest[2:8], rest[8:]
     weights = [
         pltpu.make_async_copy(weight, held.at[i], loads.at[i]) for i, weight in enumerate((wg, wu))
     ] + [pltpu.make_async_copy(wd, last, loads.at[2])]
     core, y, s1, s2 = ids[0], ids[1], ids[2], ids[3]
     copies = []
-    for k2, piece in enumerate((p0, p1, p2, p3)):
-        b = lax.rem(s2 + k2, 4)
-        for k1 in range(4):
-            a = lax.rem(s1 + k1, 4)
-            zx = jnp.where(core == 0, b * 4 + a, a * 4 + b)
-            for k0 in range(2):
-                at = pl.multiple_of((lax.rem(y + k0, 2) * 16 + zx) * 64, 64)
-                copies.append(
-                    pltpu.make_async_copy(
-                        piece.at[k1, k0], acts.at[:, pl.ds(at, 64), :], sems.at[len(copies)]
+    for i, pieces in enumerate((xs, gs)):
+        for k2, piece in enumerate(pieces):
+            b = lax.rem(s2 + k2, 4)
+            for k1 in range(4):
+                a = lax.rem(s1 + k1, 4)
+                zx = jnp.where(core == 0, b * 4 + a, a * 4 + b)
+                for k0 in range(2):
+                    at = pl.multiple_of((lax.rem(y + k0, 2) * 16 + zx) * 64, 64)
+                    copies.append(
+                        pltpu.make_async_copy(
+                            piece.at[k1, k0], acts.at[i, pl.ds(at, 64), :], sems.at[len(copies)]
+                        )
                     )
-                )
     for copy in copies:
         copy.start()
     for copy in weights:
         copy.start()
     for copy in copies:
         copy.wait()
+    out = [pltpu.make_async_copy(acts, acts_out, stores.at[0])]
+    out[0].start()
     half = mine[0].shape[0]
     for i in range(2):
         for n, place in enumerate((core, 1 - core)):
@@ -119,37 +123,47 @@
         weights[i].wait()
         weight = last if i == 2 else held.at[i]
         dims = (((1,), (0,)), ((), ())) if i < 2 else (((1,), (1,)), ((), ()))
-        total = lax.dot_general(turned[i // 2], weight[...], dims, preferred_element_type=F32)
+        sums[i] = lax.dot_general(turned[i // 2], weight[...], dims, preferred_element_type=F32)
         for c in range(2):
-            mine[c][:, i * width : (i + 1) * width] = total[c * half : (c + 1) * half]
-            theirs[3 * c + i][...] = total[(2 + c) * half : (3 + c) * half]
+            for row, to in (
+                (c * half, mine[c].at[:, pl.ds(i * width, width)]),
+                ((2 + c) * half, theirs[3 * c + i]),
+            ):
+                copy = pltpu.make_async_copy(sums.at[i, pl.ds(row, half), :], to, stores.at[len(out)])
+                copy.start()
+                out.append(copy)
+    for copy in out:
+        copy.wait()
 
 
 def _whole(*dims):
     return pl.BlockSpec(dims, lambda i: (0,) * len(dims))
 
 
-def forward(ids, pieces, wg, wu, wd):
+def forward(ids, xs, gs, wg, wu, wd):
     depth, width = wg.shape
-    tokens = pieces[0].shape[-1]
+    tokens = xs[0].shape[-1]
     mine, other = shape((tokens // 4, 3 * width), F32), shape((tokens // 4, width), F32)
     return _call(
         functools.partial(_forward_body, width),
         (mine,) * 2 + (other,) * 6 + (shape((2, depth, tokens), BF16),),
         WHOLE,
-        in_specs=[SMEM] + [ANY] * 7,
-        out_specs=(VMEM,) * 9,
+        in_specs=[SMEM] + [ANY] * 11,
+        out_specs=(ANY,) * 9,
         scratch_shapes=[
+            pltpu.VMEM((2, depth, tokens), BF16),
             pltpu.VMEM((2, tokens, depth), BF16),
             pltpu.VMEM((2, depth, width), BF16),
             pltpu.VMEM((width, depth), BF16),
+            pltpu.VMEM((3, tokens, width), F32),
             pltpu.SemaphoreType.DMA((3,)),
-            pltpu.SemaphoreType.DMA((32,)),
+            pltpu.SemaphoreType.DMA((13,)),
+            pltpu.SemaphoreType.DMA((64,)),
         ],
         cost_estimate=_cost(
             flops=6 * tokens * depth * width, bytes_accessed=6 * depth * width + 8 * depth * tokens, transcendentals=0
         ),
-    )(ids, *pieces, wg, wu, wd)
+    )(ids, *xs, *gs, wg, wu, wd)
 
 
 def _chip_body(width, mine, o0, o1, o2, chip, code, tick):
@@ -219,7 +233,7 @@
 
 
 def _grad_in_body(width, n_before, ids, wg, wu, m0, m1, m2, o0, o1, o2, *rest):
-    before, (pair, own, c1, c2, c3, tick, right, tops, blocks, codes) = rest[:n_before], rest[n_before:]
+    before, (pair_out, own, c1, c2, c3, tick, pair, right, tops, blocks, codes, sem) = rest[:n_before], rest[n_before:]
     core, s1 = ids[0], ids[2]
     half = m0.shape[0]
     tokens = 2 * half
@@ -236,6 +250,8 @@
             if i:
                 right[rows, (2 * i - 2) * width : (2 * i - 1) * width] = high
                 right[rows, (2 * i - 1) * width : 2 * i * width] = low
+    store = pltpu.make_async_copy(pair, pair_out, sem)
+    store.start()
     for part in range(4):
         some = slice(part * 512, (part + 1) * 512)
         g, u = wg[some, :], wu[some, :]
@@ -260,6 +276,7 @@
     for n, out in ((1, c1), (2, c2), (3, c3)):
         out[c, 0:512, :] = codes[n]
         out[c, 512:528, :] = jnp.concatenate([tops[n], tops[n]], axis=0).astype(BF16)
+    store.wait()
 
 
 def grad_in(ids, wg, wu, mine, theirs, before):
@@ -272,12 +289,14 @@
         (shape((2 * tokens, three), BF16), shape((n, 512, tokens), F32), code, code, code, TICK),
         LARGE,
         in_specs=[SMEM] + [VMEM] * (8 + len(before)),
-        out_specs=(VMEM,) * 6,
+        out_specs=(ANY,) + (VMEM,) * 5,
         scratch_shapes=[
+            pltpu.VMEM((2 * tokens, three), BF16),
             pltpu.VMEM((tokens, 4 * width), BF16),
             pltpu.VMEM((4, 8, tokens), F32),
             pltpu.VMEM((4, 512, tokens), F32),
             pltpu.VMEM((4, 512, tokens), BF16),
+            pltpu.SemaphoreType.DMA,
         ],
         cost_estimate=_cost(
             flops=8 * tokens * 2048 * width, bytes_accessed=4 * 2048 * width + 16 * tokens * three, transcendentals=2048 * tokens
@@ -435,9 +454,14 @@
     ids = jnp.stack([core, y, jnp.where(core == 0, x, z), jnp.where(core == 0, z, x)]).astype(jnp.int32)
     both = jnp.stack([inputs.T, grad_out.T])
     pair = jnp.stack([both, _send(both, _over_y)])
-    some = jnp.stack([pair] + [_send(pair, _first(-k)) for k in (1, 2, 3)])
-    pieces = [some] + [_send(some, _second(-k)) for k in (1, 2, 3)]
-    mine0, mine1, *theirs, acts = forward(ids, pieces, gate_weight, up_weight, down_weight)
+    near = [pair] + [_send(pair, _first(-k)) for k in (1, 2, 3)]
+    x, g = (jnp.stack([p[:, i] for p in near]) for i in range(2))
+    x1, g3 = _send(x, _second(-1)), _send(g, _second(1))
+    g1, x3 = _send(g, _second(-1)), _send(x, _second(1))
+    x2, g2 = _send(x1, _second(-1)), _send(g3, _second(1))
+    mine0, mine1, *theirs, acts = forward(
+        ids, (x, x1, x2, x3), (g, g1, g2, g3), gate_weight, up_weight, down_weight
+    )
     chips, codes = [], []
     for mine, others in ((mine0, theirs[:3]), (mine1, theirs[3:])):
         chip, code, tick = chip_sum(mine, [_send(v, _over_core) for v in others])

time: 166 us -> 159 us (0.958)
  waiting for transfers between devices: 61.5 us -> 53.2 us
  starting transfers between devices: 32.1 us -> 35.6 us
  Pallas kernels: 62.4 us -> 60.6 us
    ppermute x28 -> x31, waiting for transfers between devices: 61.5 us -> 53.2 us  [_send(): return lax.ppermute(a, BOTH, _moves(shift))]
    ppermute x28 -> x31, starting transfers between devices: 32.1 us -> 35.6 us  [_send(): return lax.ppermute(a, BOTH, _moves(shift))]
    pallas_call x1, Pallas kernels: 15.8 us -> 14 us  [forward(): _call(functools.partial(_forward_body, width), (mine,) * 2 + (other,) * 6...]
    unnamed x20 -> x26, local copies, waits for them, and re-layouts: 6.8 us -> 5.85 us
  transfers between devices with their start and end apart: 28 -> 31, of which waited for: 22 -> 25; matrix products, arithmetic and copies ran while one was open for 0% -> 1% of each run, Pallas kernels for 19% -> 20%
where the time goes in v1:
time: 159 us; the launch traced here: 158 us
  Pallas kernels  60.6 us (38%)
  waiting for transfers between devices  53.2 us (33%)
  starting transfers between devices  35.6 us (22%)
  local copies, waits for them, and re-layouts  5.9 us (4%)
  other arithmetic  1.8 us (1%)
    ppermute x31, waiting for transfers between devices, _send(): return lax.ppermute(a, BOTH, _moves(shift))  53.2 us
    ppermute x31, starting transfers between devices, _send(): return lax.ppermute(a, BOTH, _moves(shift))  35.6 us
    pallas_call x2, Pallas kernels, grad_weight(): _call(_grad_up_body, shape((depth, width), BF16), WHOLE, grid=(depth // 5...  15.5 us
    pallas_call x2, Pallas kernels, grad_in(): _call(functools.partial(_grad_in_body, width, len(before)), (shape((2 * t...  14.5 us
    pallas_call x1, Pallas kernels, forward(): _call(functools.partial(_forward_body, width), (mine,) * 2 + (other,) * 6...  14 us
    pallas_call x1, Pallas kernels, grad_down_weight(): _call(_grad_down_body, shape((width, depth), BF16), WHOLE, grid=(depth //...  7.95 us
    unnamed x26, local copies, waits for them, and re-layouts  5.85 us
  transfers between devices with their start and end apart: 31, of which 25 were waited for; matrix products, arithmetic and copies ran while one was open for 1% of the time, Pallas kernels for 20%

profile of v1, /device:TPU:0, one launch (start us, length us, event | category | flops | bytes accessed | tf_op | source)
XLA Modules:
  0.0 158.0 jit_solution(8257096186171941505)
XLA Ops:
  0.6 0.9 fusion.4
  1.5 3.4 %collective-permute-start = (bf16[2,64,512]{2,1,0:T(8,128)(2,1)S(1)}, bf16[2,64,512]{2,1,0:T(8,128)(2,1)S(1)}, u32[]{:S(2)}, u32[]{:S(2)}) collective-permute-start(bf16[2,64,512]{2,1,0:T(8,128)(2,1)S(1)} %get-tuple-element.87), channel_id=1, source_target_pairs={{0,16},{1,17},{2,18},{3,19},{4,20},{5,21},{6,22},{7,23},{8,24},{9,... | collective-permute-start | bytes 393224 | tf_op jit(solution)/shard_map/ppermute | solution.py:26
  4.9 3.5 %collective-permute-done = bf16[2,64,512]{2,1,0:T(8,128)(2,1)S(1)} collective-permute-done((bf16[2,64,512]{2,1,0:T(8,128)(2,1)S(1)}, bf16[2,64,512]{2,1,0:T(8,128)(2,1)S(1)}, u32[]{:S(2)}, u32[]{:S(2)}) %collective-permute-start) | collective-permute-done | bytes 131104 | tf_op jit(solution)/shard_map/ppermute | solution.py:26
  8.4 3.2 %collective-permute-start.2 = (bf16[2,2,64,512]{3,2,0,1:T(8,128)(2,1)S(1)}, bf16[2,2,64,512]{3,2,0,1:T(8,128)(2,1)S(1)}, u32[]{:S(2)}, u32[]{:S(2)}) collective-permute-start(bf16[2,2,64,512]{3,2,0,1:T(8,128)(2,1)S(1)} %pad_maximum_fusion.2), channel_id=1, source_target_pairs={{0,2},{1,3},{2,0},{3,1},{4,6},{5,7},{6,4},{7,5},{8,10},{9,11},{10,... | collective-permute-start | bytes 786440 | tf_op jit(solution)/shard_map/ppermute | solution.py:26
  11.6 1.1 collective-permute-start.1
  12.7 1.0 collective-permute-start.3
  13.7 2.7 %collective-permute-done.2 = bf16[2,2,64,512]{3,2,0,1:T(8,128)(2,1)S(1)} collective-permute-done((bf16[2,2,64,512]{3,2,0,1:T(8,128)(2,1)S(1)}, bf16[2,2,64,512]{3,2,0,1:T(8,128)(2,1)S(1)}, u32[]{:S(2)}, u32[]{:S(2)}) %collective-permute-start.2) | collective-permute-done | bytes 262176 | tf_op jit(solution)/shard_map/ppermute | solution.py:26
  16.4 2.9 %collective-permute-done.1 = bf16[2,2,64,512]{3,2,0,1:T(8,128)(2,1)S(1)} collective-permute-done((bf16[2,2,64,512]{3,2,0,1:T(8,128)(2,1)S(1)}, bf16[2,2,64,512]{3,2,0,1:T(8,128)(2,1)S(1)}, u32[]{:S(2)}, u32[]{:S(2)}) %collective-permute-start.1) | collective-permute-done | bytes 262176 | tf_op jit(solution)/shard_map/ppermute | solution.py:26
  19.4 1.0 collective-permute-done.3
  20.5 4.1 %collective-permute-start.4 = (bf16[4,2,64,512]{3,2,1,0:T(8,128)(2,1)S(1)}, bf16[4,2,64,512]{3,2,1,0:T(8,128)(2,1)S(1)}, u32[]{:S(2)}, u32[]{:S(2)}) collective-permute-start(bf16[4,2,64,512]{3,2,1,0:T(8,128)(2,1)S(1)} %pad_maximum_fusion.rest_0_), channel_id=1, source_target_pairs={{0,12},{1,13},{2,14},{3,15},{4,0},{5,1},{6,2},{7,3},{8,4},{9,5},{1... | collective-permute-start | bytes 1572872 | tf_op jit(solution)/shard_map/ppermute | solution.py:26
  24.8 3.2 %collective-permute-start.7 = (bf16[4,2,64,512]{3,2,1,0:T(8,128)(2,1)S(1)}, bf16[4,2,64,512]{3,2,1,0:T(8,128)(2,1)S(1)}, u32[]{:S(2)}, u32[]{:S(2)}) collective-permute-start(bf16[4,2,64,512]{3,2,1,0:T(8,128)(2,1)S(1)} %pad_maximum_fusion.1.rest_4_), channel_id=1, source_target_pairs={{0,12},{1,13},{2,14},{3,15},{4,0},{5,1},{6,2},{7,3},{8,4},{9,5},{1... | collective-permute-start | bytes 1572872 | tf_op jit(solution)/shard_map/ppermute | solution.py:26
  28.1 3.2 %collective-permute-done.4.rest_1_ = bf16[4,2,64,512]{3,2,1,0:T(8,128)(2,1)S(1)} collective-permute-done((bf16[4,2,64,512]{3,2,1,0:T(8,128)(2,1)S(1)}, bf16[4,2,64,512]{3,2,1,0:T(8,128)(2,1)S(1)}, u32[]{:S(2)}, u32[]{:S(2)}) %collective-permute-start.4) | collective-permute-done | bytes 524320 | tf_op jit(solution)/shard_map/ppermute | solution.py:26
  31.3 3.7 %collective-permute-start.5 = (bf16[4,2,64,512]{3,2,1,0:T(8,128)(2,1)S(1)}, bf16[4,2,64,512]{3,2,1,0:T(8,128)(2,1)}, u32[]{:S(2)}, u32[]{:S(2)}) collective-permute-start(bf16[4,2,64,512]{3,2,1,0:T(8,128)(2,1)S(1)} %collective-permute-done.4.rest_1_), channel_id=1, source_target_pairs={{0,12},{1,13},{2,14},{3,15},{4,0},{5,1},{6,2},{7,3},{8,4},{9,5},{1... | collective-permute-start | bytes 1572872 | tf_op jit(solution)/shard_map/ppermute | solution.py:26
  35.1 0.7 pad_add_fusion.ids
  35.9 4.9 %collective-permute-done.6.rest_3_ = bf16[4,2,64,512]{3,2,1,0:T(8,128)(2,1)S(1)} collective-permute-done((bf16[4,2,64,512]{3,2,1,0:T(8,128)(2,1)S(1)}, bf16[4,2,64,512]{3,2,1,0:T(8,128)(2,1)S(1)}, u32[]{:S(2)}, u32[]{:S(2)}) %collective-permute-start.6) | collective-permute-done | bytes 524320 | tf_op jit(solution)/shard_map/ppermute | solution.py:26
  40.8 1.8 %collective-permute-done.5.rest_2_ = bf16[4,2,64,512]{3,2,1,0:T(8,128)(2,1)} collective-permute-done((bf16[4,2,64,512]{3,2,1,0:T(8,128)(2,1)S(1)}, bf16[4,2,64,512]{3,2,1,0:T(8,128)(2,1)}, u32[]{:S(2)}, u32[]{:S(2)}) %collective-permute-start.5) | collective-permute-done | bytes 524320 | tf_op jit(solution)/shard_map/ppermute | solution.py:26
  42.5 3.9 %collective-permute-done.9.rest_6_ = bf16[4,2,64,512]{3,2,1,0:T(8,128)(2,1)} collective-permute-done((bf16[4,2,64,512]{3,2,1,0:T(8,128)(2,1)S(1)}, bf16[4,2,64,512]{3,2,1,0:T(8,128)(2,1)}, u32[]{:S(2)}, u32[]{:S(2)}) %collective-permute-start.9) | collective-permute-done | bytes 524320 | tf_op jit(solution)/shard_map/ppermute | solution.py:26
  46.5 14.0 %shard_map.84 = (f32[128,2688]{1,0:T(8,128)}, f32[128,2688]{1,0:T(8,128)}, f32[128,896]{1,0:T(8,128)}, f32[128,896]{1,0:T(8,128)}, f32[128,896]{1,0:T(8,128)}, /...) custom-call(s32[4]{0:T(128)} %pad_add_fusion.ids, ...), custom_call_target="tpu_custom_call" | custom-call | flops 281857216 | bytes 969932 | tf_op jit(solution)/shard_map/pallas_call | solution.py:147
  61.3 1.4 collective-permute-done.14.o0
  64.0 1.3 copy-done.3
  65.3 1.0 shard_map.86
  66.4 1.7 %collective-permute-start.17 = (bf16[128,2816]{1,0:T(8,128)(2,1)S(1)}, bf16[128,2816]{1,0:T(8,128)(2,1)S(1)}, u32[]{:S(2)}, u32[]{:S(2)}) collective-permute-start(bf16[128,2816]{1,0:T(8,128)(2,1)S(1)} %get-tuple-element.52), channel_id=1, source_target_pairs={{0,64},{1,65},{2,66},{3,67},{4,68},{5,69},{6,70},{7,71},{8,72},{9,... | collective-permute-start | bytes 2162696 | tf_op jit(solution)/shard_map/ppermute | solution.py:26
  68.5 1.5 collective-permute-done.10.o0
  71.4 1.3 copy-done.2
  72.7 1.1 shard_map.85
  74.3 11.1 %collective-permute-done.17.code = bf16[128,2816]{1,0:T(8,128)(2,1)S(1)} collective-permute-done((bf16[128,2816]{1,0:T(8,128)(2,1)S(1)}, bf16[128,2816]{1,0:T(8,128)(2,1)S(1)}, u32[]{:S(2)}, u32[]{:S(2)}) %collective-permute-start.17) | collective-permute-done | bytes 720928 | tf_op jit(solution)/shard_map/ppermute | solution.py:26
  85.4 1.3 shard_map.87
  87.4 1.2 collective-permute-done.18.o0
  89.9 6.1 %shard_map.88 = (bf16[512,2688]{1,0:T(8,128)(2,1)S(1)}, f32[1,512,256]{2,1,0:T(8,128)S(1)}, bf16[1,528,256]{2,1,0:T(8,128)(2,1)S(1)}, bf16[1,528,256]{2,1,0:T(8,...) custom-call(s32[4]{0:T(128)S(1)} %copy-done.4, bf16[2048,896]{1,0:T(8,128)(2,1)S(1)} %copy-done, ...), custom_call_target="tpu_custom_call" | custom-call | flops 187904816 | bytes 917504 | tf_op jit(solution)/shard_map/pallas_call | solution.py:287
  96.0 1.5 copy-done.5
  97.6 2.5 %collective-permute-done.13.code = bf16[128,2816]{1,0:T(8,128)(2,1)S(1)} collective-permute-done((bf16[128,2816]{1,0:T(8,128)(2,1)S(1)}, bf16[128,2816]{1,0:T(8,128)(2,1)S(1)}, u32[]{:S(2)}, u32[]{:S(2)}) %collective-permute-start.13) | collective-permute-done | bytes 720928 | tf_op jit(solution)/shard_map/ppermute | solution.py:26
  100.1 1.3 shard_map.89
  102.0 1.2 collective-permute-done.21.o0
  104.5 8.5 %shard_map.90 = (bf16[512,2688]{1,0:T(8,128)(2,1)S(1)}, f32[2,512,256]{2,1,0:T(8,128)S(1)}, bf16[2,528,256]{2,1,0:T(8,128)(2,1)}, bf16[2,528,256]{2,1,0:T(8,128)...) custom-call(s32[4]{0:T(128)S(1)} %copy-done.4, bf16[2048,896]{1,0:T(8,128)(2,1)S(1)} %copy-done, ...), custom_call_target="tpu_custom_call" | custom-call | flops 187904816 | bytes 917504 | tf_op jit(solution)/shard_map/pallas_call | solution.py:287
  113.0 1.6 %copy-done.6 = bf16[512,2688]{1,0:T(8,128)(2,1)} copy-done((bf16[512,2688]{1,0:T(8,128)(2,1)}, bf16[512,2688]{1,0:T(8,128)(2,1)S(1)}, u32[]{:S(2)}) %copy-start.6) | copy-done | bytes 2752536
  115.0 2.7 %collective-permute-start.25 = (bf16[2,528,256]{2,1,0:T(8,128)(2,1)S(1)}, bf16[2,528,256]{2,1,0:T(8,128)(2,1)S(1)}, u32[]{:S(2)}, u32[]{:S(2)}) collective-permute-start(bf16[2,528,256]{2,1,0:T(8,128)(2,1)S(1)} %get-tuple-element.67), channel_id=1, source_target_pairs={{0,2},{1,3},{2,0},{3,1},{4,6},{5,7},{6,4},{7,5},{8,10},{9,11},{10,... | collective-permute-start | bytes 1622024 | tf_op jit(solution)/shard_map/ppermute | solution.py:26
  117.7 1.4 collective-permute-start.26
  119.1 8.0 %shard_map.96 = bf16[896,2048]{1,0:T(8,128)(2,1)} custom-call(bf16[2,2048,512]{2,1,0:T(8,128)(2,1)} %get-tuple-element.75.x.g, bf16[512,2688]{1,0:T(8,128)(2,1)} %copy-done.5, bf16[512,2688]{1,0:T(8,128)(2,1)} %copy-done.6), custom_call_target="tpu_custom_call" | custom-call | flops 3758096384 | bytes 7340032 | tf_op jit(solution)/shard_map/pallas_call | solution.py:351
  127.1 4.1 %collective-permute-done.24.r1 = bf16[2,528,256]{2,1,0:T(8,128)(2,1)S(1)} collective-permute-done((bf16[2,528,256]{2,1,0:T(8,128)(2,1)}, bf16[2,528,256]{2,1,0:T(8,128)(2,1)S(1)}, u32[]{:S(2)}, u32[]{:S(2)}) %collective-permute-start.24) | collective-permute-done | bytes 540704 | tf_op jit(solution)/shard_map/ppermute | solution.py:26
  131.2 0.7 collective-permute-done.26.r3
  131.9 2.5 %shard_map.91 = (f32[2,128,256]{2,1,0:T(8,128)S(1)}, bf16[2,144,256]{2,1,0:T(8,128)(2,1)S(1)}, bf16[2,144,256]{2,1,0:T(8,128)(2,1)S(1)}, bf16[2,144,256]{2,1,0:T(8,128)(2,1)S(1)}) custom-call(s32[4]{0:T(128)S(1)} %copy-done.4, f32[2,512,256]{2,1,0:T(8,128)S(1)} %get-tuple-element.65.own, bf16[2,528,256]{2,1,0:T(8,128)(2,1)S(1)} %collective-permute-done.24.r1, ...), custom_call_target="tpu_custom_call" | custom-call | tf_op jit(solution)/shard_map/pallas_call | solution.py:397
  134.4 1.3 collective-permute-start.28
  135.7 1.9 %collective-permute-start.29 = (bf16[2,144,256]{2,1,0:T(8,128)(2,1)S(1)}, bf16[2,144,256]{2,1,0:T(8,128)(2,1)S(1)}, u32[]{:S(2)}, u32[]{:S(2)}) collective-permute-start(bf16[2,144,256]{2,1,0:T(8,128)(2,1)S(1)} %get-tuple-element.72), channel_id=1, source_target_pairs={{0,12},{1,13},{2,14},{3,15},{4,0},{5,1},{6,2},{7,3},{8,4},{9,5},{1... | collective-permute-start | bytes 442376 | tf_op jit(solution)/shard_map/ppermute | solution.py:26
  137.6 7.7 %shard_map.95 = bf16[2048,896]{1,0:T(8,128)(2,1)} custom-call(bf16[2,2048,512]{2,1,0:T(8,128)(2,1)} %get-tuple-element.75.x.g, bf16[512,2688]{1,0:T(8,128)(2,1)} %copy-done.5, bf16[512,2688]{1,0:T(8,128)(2,1)} %copy-done.6), custom_call_target="tpu_custom_call" | custom-call | flops 3758096384 | bytes 7340032 | tf_op jit(solution)/shard_map/pallas_call | solution.py:323
  145.4 0.9 shard_map.92
  146.3 3.3 %collective-permute-start.30 = (bf16[2,80,256]{2,1,0:T(8,128)(2,1)S(1)}, bf16[2,80,256]{2,1,0:T(8,128)(2,1)S(1)}, u32[]{:S(2)}, u32[]{:S(2)}) collective-permute-start(bf16[2,80,256]{2,1,0:T(8,128)(2,1)S(1)} %get-tuple-element.74), channel_id=1, source_target_pairs={{0,16},{1,17},{2,18},{3,19},{4,20},{5,21},{6,22},{7,23},{8,24},{9,... | collective-permute-start | bytes 245768 | tf_op jit(solution)/shard_map/ppermute | solution.py:26
  149.6 7.7 %shard_map.94 = bf16[2048,896]{1,0:T(8,128)(2,1)} custom-call(bf16[2,2048,512]{2,1,0:T(8,128)(2,1)} %get-tuple-element.75.x.g, bf16[512,2688]{1,0:T(8,128)(2,1)} %copy-done.5, bf16[512,2688]{1,0:T(8,128)(2,1)} %copy-done.6), custom_call_target="tpu_custom_call" | custom-call | flops 3758096384 | bytes 7340032 | tf_op jit(solution)/shard_map/pallas_call | solution.py:323
  157.3 0.7 shard_map.93
  (62 shorter events, 9.4 us)
Async XLA Ops:
  1.5 6.9 %collective-permute-start = (bf16[2,64,512]{2,1,0:T(8,128)(2,1)S(1)}, bf16[2,64,512]{2,1,0:T(8,128)(2,1)S(1)}, u32[]{:S(2)}, u32[]{:S(2)}) collective-permute-start(bf16[2,64,512]{2,1,0:T(8,128)(2,1)S(1)} %get-tuple-element.87), channel_id=1, source_target_pairs={{0,16},{1,17},{2,18},{3,19},{4,20},{5,21},{6,22},{7,23},{8,24},{9,... | collective-permute-start | bytes 393224 | tf_op jit(solution)/shard_map/ppermute | solution.py:26
  8.4 8.0 %collective-permute-start.2 = (bf16[2,2,64,512]{3,2,0,1:T(8,128)(2,1)S(1)}, bf16[2,2,64,512]{3,2,0,1:T(8,128)(2,1)S(1)}, u32[]{:S(2)}, u32[]{:S(2)}) collective-permute-start(bf16[2,2,64,512]{3,2,0,1:T(8,128)(2,1)S(1)} %pad_maximum_fusion.2), channel_id=1, source_target_pairs={{0,2},{1,3},{2,0},{3,1},{4,6},{5,7},{6,4},{7,5},{8,10},{9,11},{10,... | collective-permute-start | bytes 786440 | tf_op jit(solution)/shard_map/ppermute | solution.py:26
  11.6 7.8 %collective-permute-start.1 = (bf16[2,2,64,512]{3,2,0,1:T(8,128)(2,1)S(1)}, bf16[2,2,64,512]{3,2,0,1:T(8,128)(2,1)S(1)}, u32[]{:S(2)}, u32[]{:S(2)}) collective-permute-start(bf16[2,2,64,512]{3,2,0,1:T(8,128)(2,1)S(1)} %pad_maximum_fusion.2), channel_id=1, source_target_pairs={{0,3},{1,0},{2,1},{3,2},{4,7},{5,4},{6,5},{7,6},{8,11},{9,8},{10,9... | collective-permute-start | bytes 786440 | tf_op jit(solution)/shard_map/ppermute | solution.py:26
  12.7 7.7 %collective-permute-start.3 = (bf16[2,2,64,512]{3,2,0,1:T(8,128)(2,1)S(1)}, bf16[2,2,64,512]{3,2,0,1:T(8,128)(2,1)S(1)}, u32[]{:S(2)}, u32[]{:S(2)}) collective-permute-start(bf16[2,2,64,512]{3,2,0,1:T(8,128)(2,1)S(1)} %pad_maximum_fusion.2), channel_id=1, source_target_pairs={{0,1},{1,2},{2,3},{3,0},{4,5},{5,6},{6,7},{7,4},{8,9},{9,10},{10,1... | collective-permute-start | bytes 786440 | tf_op jit(solution)/shard_map/ppermute | solution.py:26
  20.5 26.0 %copy-start.7 = (bf16[4,2,64,512]{3,2,1,0:T(8,128)(2,1)}, bf16[4,2,64,512]{3,2,1,0:T(8,128)(2,1)S(1)}, u32[]{:S(2)}) copy-start(bf16[4,2,64,512]{3,2,1,0:T(8,128)(2,1)S(1)} %pad_maximum_fusion.rest_0_) | copy-start | bytes 1572868
  20.5 10.8 %collective-permute-start.4 = (bf16[4,2,64,512]{3,2,1,0:T(8,128)(2,1)S(1)}, bf16[4,2,64,512]{3,2,1,0:T(8,128)(2,1)S(1)}, u32[]{:S(2)}, u32[]{:S(2)}) collective-permute-start(bf16[4,2,64,512]{3,2,1,0:T(8,128)(2,1)S(1)} %pad_maximum_fusion.rest_0_), channel_id=1, source_target_pairs={{0,12},{1,13},{2,14},{3,15},{4,0},{5,1},{6,2},{7,3},{8,4},{9,5},{1... | collective-permute-start | bytes 1572872 | tf_op jit(solution)/shard_map/ppermute | solution.py:26
  24.7 21.8 %copy-start.8 = (bf16[4,2,64,512]{3,2,1,0:T(8,128)(2,1)}, bf16[4,2,64,512]{3,2,1,0:T(8,128)(2,1)S(1)}, u32[]{:S(2)}) copy-start(bf16[4,2,64,512]{3,2,1,0:T(8,128)(2,1)S(1)} %pad_maximum_fusion.1.rest_4_) | copy-start | bytes 1572868
  24.7 10.5 %collective-permute-start.8 = (bf16[4,2,64,512]{3,2,1,0:T(8,128)(2,1)S(1)}, bf16[4,2,64,512]{3,2,1,0:T(8,128)(2,1)S(1)}, u32[]{:S(2)}, u32[]{:S(2)}) collective-permute-start(bf16[4,2,64,512]{3,2,1,0:T(8,128)(2,1)S(1)} %pad_maximum_fusion.1.rest_4_), channel_id=1, source_target_pairs={{0,4},{1,5},{2,6},{3,7},{4,8},{5,9},{6,10},{7,11},{8,12},{9,13},{1... | collective-permute-start | bytes 1572872 | tf_op jit(solution)/shard_map/ppermute | solution.py:26
  24.8 16.0 %collective-permute-start.6 = (bf16[4,2,64,512]{3,2,1,0:T(8,128)(2,1)S(1)}, bf16[4,2,64,512]{3,2,1,0:T(8,128)(2,1)S(1)}, u32[]{:S(2)}, u32[]{:S(2)}) collective-permute-start(bf16[4,2,64,512]{3,2,1,0:T(8,128)(2,1)S(1)} %pad_maximum_fusion.rest_0_), channel_id=1, source_target_pairs={{0,4},{1,5},{2,6},{3,7},{4,8},{5,9},{6,10},{7,11},{8,12},{9,13},{1... | collective-permute-start | bytes 1572872 | tf_op jit(solution)/shard_map/ppermute | solution.py:26
  24.8 15.9 %collective-permute-start.7 = (bf16[4,2,64,512]{3,2,1,0:T(8,128)(2,1)S(1)}, bf16[4,2,64,512]{3,2,1,0:T(8,128)(2,1)S(1)}, u32[]{:S(2)}, u32[]{:S(2)}) collective-permute-start(bf16[4,2,64,512]{3,2,1,0:T(8,128)(2,1)S(1)} %pad_maximum_fusion.1.rest_4_), channel_id=1, source_target_pairs={{0,12},{1,13},{2,14},{3,15},{4,0},{5,1},{6,2},{7,3},{8,4},{9,5},{1... | collective-permute-start | bytes 1572872 | tf_op jit(solution)/shard_map/ppermute | solution.py:26
  31.3 15.2 %copy-start.9 = (bf16[4,2,64,512]{3,2,1,0:T(8,128)(2,1)}, bf16[4,2,64,512]{3,2,1,0:T(8,128)(2,1)S(1)}, u32[]{:S(2)}) copy-start(bf16[4,2,64,512]{3,2,1,0:T(8,128)(2,1)S(1)} %collective-permute-done.4.rest_1_) | copy-start | bytes 1572868
  31.3 11.2 %collective-permute-start.5 = (bf16[4,2,64,512]{3,2,1,0:T(8,128)(2,1)S(1)}, bf16[4,2,64,512]{3,2,1,0:T(8,128)(2,1)}, u32[]{:S(2)}, u32[]{:S(2)}) collective-permute-start(bf16[4,2,64,512]{3,2,1,0:T(8,128)(2,1)S(1)} %collective-permute-done.4.rest_1_), channel_id=1, source_target_pairs={{0,12},{1,13},{2,14},{3,15},{4,0},{5,1},{6,2},{7,3},{8,4},{9,5},{1... | collective-permute-start | bytes 1572872 | tf_op jit(solution)/shard_map/ppermute | solution.py:26
  35.1 11.4 %copy-start.10 = (bf16[4,2,64,512]{3,2,1,0:T(8,128)(2,1)}, bf16[4,2,64,512]{3,2,1,0:T(8,128)(2,1)S(1)}, u32[]{:S(2)}) copy-start(bf16[4,2,64,512]{3,2,1,0:T(8,128)(2,1)S(1)} %collective-permute-done.8.rest_7_) | copy-start | bytes 1572868
  35.1 11.3 %collective-permute-start.9 = (bf16[4,2,64,512]{3,2,1,0:T(8,128)(2,1)S(1)}, bf16[4,2,64,512]{3,2,1,0:T(8,128)(2,1)}, u32[]{:S(2)}, u32[]{:S(2)}) collective-permute-start(bf16[4,2,64,512]{3,2,1,0:T(8,128)(2,1)S(1)} %collective-permute-done.8.rest_7_), channel_id=1, source_target_pairs={{0,4},{1,5},{2,6},{3,7},{4,8},{5,9},{6,10},{7,11},{8,12},{9,13},{1... | collective-permute-start | bytes 1572872 | tf_op jit(solution)/shard_map/ppermute | solution.py:26
  40.8 5.7 %copy-start.11 = (bf16[4,2,64,512]{3,2,1,0:T(8,128)(2,1)}, bf16[4,2,64,512]{3,2,1,0:T(8,128)(2,1)S(1)}, u32[]{:S(2)}) copy-start(bf16[4,2,64,512]{3,2,1,0:T(8,128)(2,1)S(1)} %collective-permute-done.6.rest_3_) | copy-start | bytes 1572868
  40.8 5.8 %copy-start.12 = (bf16[4,2,64,512]{3,2,1,0:T(8,128)(2,1)}, bf16[4,2,64,512]{3,2,1,0:T(8,128)(2,1)S(1)}, u32[]{:S(2)}) copy-start(bf16[4,2,64,512]{3,2,1,0:T(8,128)(2,1)S(1)} %collective-permute-done.7.rest_5_) | copy-start | bytes 1572868
  60.6 2.1 %collective-permute-start.14 = (f32[128,896]{1,0:T(8,128)}, f32[128,896]{1,0:T(8,128)S(1)}, u32[]{:S(2)}, u32[]{:S(2)}) collective-permute-start(f32[128,896]{1,0:T(8,128)} %get-tuple-element.48), channel_id=1, source_target_pairs={{0,32},{1,33},{2,34},{3,35},{4,36},{5,37},{6,38},{7,39},{8,40},{9,... | collective-permute-start | bytes 1376264 | tf_op jit(solution)/shard_map/ppermute | solution.py:26
  60.7 2.7 %collective-permute-start.15 = (f32[128,896]{1,0:T(8,128)}, f32[128,896]{1,0:T(8,128)S(1)}, u32[]{:S(2)}, u32[]{:S(2)}) collective-permute-start(f32[128,896]{1,0:T(8,128)} %get-tuple-element.49), channel_id=1, source_target_pairs={{0,32},{1,33},{2,34},{3,35},{4,36},{5,37},{6,38},{7,39},{8,40},{9,... | collective-permute-start | bytes 1376264 | tf_op jit(solution)/shard_map/ppermute | solution.py:26
  61.2 2.8 %collective-permute-start.16 = (f32[128,896]{1,0:T(8,128)}, f32[128,896]{1,0:T(8,128)S(1)}, u32[]{:S(2)}, u32[]{:S(2)}) collective-permute-start(f32[128,896]{1,0:T(8,128)} %get-tuple-element.50), channel_id=1, source_target_pairs={{0,32},{1,33},{2,34},{3,35},{4,36},{5,37},{6,38},{7,39},{8,40},{9,... | collective-permute-start | bytes 1376264 | tf_op jit(solution)/shard_map/ppermute | solution.py:26
  64.0 25.9 %copy-start.4 = (s32[4]{0:T(128)S(1)}, s32[4]{0:T(128)}, u32[]{:S(2)}) copy-start(s32[4]{0:T(128)} %pad_add_fusion.ids) | copy-start | bytes 52
  64.0 1.3 copy-start.3
  65.3 24.6 %copy-start = (bf16[2048,896]{1,0:T(8,128)(2,1)S(1)}, bf16[2048,896]{1,0:T(8,128)(2,1)}, u32[]{:S(2)}) copy-start(bf16[2048,896]{1,0:T(8,128)(2,1)} %wg.3) | copy-start | bytes 11010052
  65.3 24.6 %copy-start.1 = (bf16[2048,896]{1,0:T(8,128)(2,1)S(1)}, bf16[2048,896]{1,0:T(8,128)(2,1)}, u32[]{:S(2)}) copy-start(bf16[2048,896]{1,0:T(8,128)(2,1)} %wu.3) | copy-start | bytes 11010052
  66.4 19.1 %collective-permute-start.17 = (bf16[128,2816]{1,0:T(8,128)(2,1)S(1)}, bf16[128,2816]{1,0:T(8,128)(2,1)S(1)}, u32[]{:S(2)}, u32[]{:S(2)}) collective-permute-start(bf16[128,2816]{1,0:T(8,128)(2,1)S(1)} %get-tuple-element.52), channel_id=1, source_target_pairs={{0,64},{1,65},{2,66},{3,67},{4,68},{5,69},{6,70},{7,71},{8,72},{9,... | collective-permute-start | bytes 2162696 | tf_op jit(solution)/shard_map/ppermute | solution.py:26
  68.0 2.0 %collective-permute-start.10 = (f32[128,896]{1,0:T(8,128)}, f32[128,896]{1,0:T(8,128)S(1)}, u32[]{:S(2)}, u32[]{:S(2)}) collective-permute-start(f32[128,896]{1,0:T(8,128)} %get-tuple-element.42), channel_id=1, source_target_pairs={{0,32},{1,33},{2,34},{3,35},{4,36},{5,37},{6,38},{7,39},{8,40},{9,... | collective-permute-start | bytes 1376264 | tf_op jit(solution)/shard_map/ppermute | solution.py:26
  68.0 2.7 %collective-permute-start.11 = (f32[128,896]{1,0:T(8,128)}, f32[128,896]{1,0:T(8,128)S(1)}, u32[]{:S(2)}, u32[]{:S(2)}) collective-permute-start(f32[128,896]{1,0:T(8,128)} %get-tuple-element.43), channel_id=1, source_target_pairs={{0,32},{1,33},{2,34},{3,35},{4,36},{5,37},{6,38},{7,39},{8,40},{9,... | collective-permute-start | bytes 1376264 | tf_op jit(solution)/shard_map/ppermute | solution.py:26
  68.5 2.8 %collective-permute-start.12 = (f32[128,896]{1,0:T(8,128)}, f32[128,896]{1,0:T(8,128)S(1)}, u32[]{:S(2)}, u32[]{:S(2)}) collective-permute-start(f32[128,896]{1,0:T(8,128)} %get-tuple-element.44), channel_id=1, source_target_pairs={{0,32},{1,33},{2,34},{3,35},{4,36},{5,37},{6,38},{7,39},{8,40},{9,... | collective-permute-start | bytes 1376264 | tf_op jit(solution)/shard_map/ppermute | solution.py:26
  71.4 1.3 copy-start.2
  73.8 26.3 %collective-permute-start.13 = (bf16[128,2816]{1,0:T(8,128)(2,1)S(1)}, bf16[128,2816]{1,0:T(8,128)(2,1)S(1)}, u32[]{:S(2)}, u32[]{:S(2)}) collective-permute-start(bf16[128,2816]{1,0:T(8,128)(2,1)S(1)} %get-tuple-element.46), channel_id=1, source_target_pairs={{0,64},{1,65},{2,66},{3,67},{4,68},{5,69},{6,70},{7,71},{8,72},{9,... | collective-permute-start | bytes 2162696 | tf_op jit(solution)/shard_map/ppermute | solution.py:26
  86.7 1.9 %collective-permute-start.18 = (f32[128,896]{1,0:T(8,128)S(1)}, f32[128,896]{1,0:T(8,128)S(1)}, u32[]{:S(2)}, u32[]{:S(2)}) collective-permute-start(f32[128,896]{1,0:T(8,128)S(1)} %get-tuple-element.54.m0), channel_id=1, source_target_pairs={{0,32},{1,33},{2,34},{3,35},{4,36},{5,37},{6,38},{7,39},{8,40},{9,... | collective-permute-start | bytes 1376264 | tf_op jit(solution)/shard_map/ppermute | solution.py:26
  86.8 2.5 %collective-permute-start.19 = (f32[128,896]{1,0:T(8,128)S(1)}, f32[128,896]{1,0:T(8,128)S(1)}, u32[]{:S(2)}, u32[]{:S(2)}) collective-permute-start(f32[128,896]{1,0:T(8,128)S(1)} %get-tuple-element.55.m1), channel_id=1, source_target_pairs={{0,32},{1,33},{2,34},{3,35},{4,36},{5,37},{6,38},{7,39},{8,40},{9,... | collective-permute-start | bytes 1376264 | tf_op jit(solution)/shard_map/ppermute | solution.py:26
  87.3 2.6 %collective-permute-start.20 = (f32[128,896]{1,0:T(8,128)S(1)}, f32[128,896]{1,0:T(8,128)S(1)}, u32[]{:S(2)}, u32[]{:S(2)}) collective-permute-start(f32[128,896]{1,0:T(8,128)S(1)} %get-tuple-element.56.m2), channel_id=1, source_target_pairs={{0,32},{1,33},{2,34},{3,35},{4,36},{5,37},{6,38},{7,39},{8,40},{9,... | collective-permute-start | bytes 1376264 | tf_op jit(solution)/shard_map/ppermute | solution.py:26
  96.0 1.6 copy-start.5
  101.3 1.9 %collective-permute-start.21 = (f32[128,896]{1,0:T(8,128)S(1)}, f32[128,896]{1,0:T(8,128)S(1)}, u32[]{:S(2)}, u32[]{:S(2)}) collective-permute-start(f32[128,896]{1,0:T(8,128)S(1)} %get-tuple-element.58.m0), channel_id=1, source_target_pairs={{0,32},{1,33},{2,34},{3,35},{4,36},{5,37},{6,38},{7,39},{8,40},{9,... | collective-permute-start | bytes 1376264 | tf_op jit(solution)/shard_map/ppermute | solution.py:26
  101.4 2.5 %collective-permute-start.22 = (f32[128,896]{1,0:T(8,128)S(1)}, f32[128,896]{1,0:T(8,128)S(1)}, u32[]{:S(2)}, u32[]{:S(2)}) collective-permute-start(f32[128,896]{1,0:T(8,128)S(1)} %get-tuple-element.59.m1), channel_id=1, source_target_pairs={{0,32},{1,33},{2,34},{3,35},{4,36},{5,37},{6,38},{7,39},{8,40},{9,... | collective-permute-start | bytes 1376264 | tf_op jit(solution)/shard_map/ppermute | solution.py:26
  101.9 2.6 %collective-permute-start.23 = (f32[128,896]{1,0:T(8,128)S(1)}, f32[128,896]{1,0:T(8,128)S(1)}, u32[]{:S(2)}, u32[]{:S(2)}) collective-permute-start(f32[128,896]{1,0:T(8,128)S(1)} %get-tuple-element.60.m2), channel_id=1, source_target_pairs={{0,32},{1,33},{2,34},{3,35},{4,36},{5,37},{6,38},{7,39},{8,40},{9,... | collective-permute-start | bytes 1376264 | tf_op jit(solution)/shard_map/ppermute | solution.py:26
  113.0 1.6 %copy-start.6 = (bf16[512,2688]{1,0:T(8,128)(2,1)}, bf16[512,2688]{1,0:T(8,128)(2,1)S(1)}, u32[]{:S(2)}) copy-start(bf16[512,2688]{1,0:T(8,128)(2,1)S(1)} %get-tuple-element.77.d1.h1) | copy-start | bytes 8257540
  114.6 16.6 %collective-permute-start.24 = (bf16[2,528,256]{2,1,0:T(8,128)(2,1)}, bf16[2,528,256]{2,1,0:T(8,128)(2,1)S(1)}, u32[]{:S(2)}, u32[]{:S(2)}) collective-permute-start(bf16[2,528,256]{2,1,0:T(8,128)(2,1)} %get-tuple-element.66), channel_id=1, source_target_pairs={{0,1},{1,2},{2,3},{3,0},{4,5},{5,6},{6,7},{7,4},{8,9},{9,10},{10,1... | collective-permute-start | bytes 1622024 | tf_op jit(solution)/shard_map/ppermute | solution.py:26
  115.0 16.2 %collective-permute-start.25 = (bf16[2,528,256]{2,1,0:T(8,128)(2,1)S(1)}, bf16[2,528,256]{2,1,0:T(8,128)(2,1)S(1)}, u32[]{:S(2)}, u32[]{:S(2)}) collective-permute-start(bf16[2,528,256]{2,1,0:T(8,128)(2,1)S(1)} %get-tuple-element.67), channel_id=1, source_target_pairs={{0,2},{1,3},{2,0},{3,1},{4,6},{5,7},{6,4},{7,5},{8,10},{9,11},{10,... | collective-permute-start | bytes 1622024 | tf_op jit(solution)/shard_map/ppermute | solution.py:26
  117.7 14.2 %collective-permute-start.26 = (bf16[2,528,256]{2,1,0:T(8,128)(2,1)S(1)}, bf16[2,528,256]{2,1,0:T(8,128)(2,1)S(1)}, u32[]{:S(2)}, u32[]{:S(2)}) collective-permute-start(bf16[2,528,256]{2,1,0:T(8,128)(2,1)S(1)} %get-tuple-element.68), channel_id=1, source_target_pairs={{0,3},{1,0},{2,1},{3,2},{4,7},{5,4},{6,5},{7,6},{8,11},{9,8},{10,9... | collective-permute-start | bytes 1622024 | tf_op jit(solution)/shard_map/ppermute | solution.py:26
  134.3 11.0 %collective-permute-start.27 = (bf16[2,144,256]{2,1,0:T(8,128)(2,1)S(1)}, bf16[2,144,256]{2,1,0:T(8,128)(2,1)S(1)}, u32[]{:S(2)}, u32[]{:S(2)}) collective-permute-start(bf16[2,144,256]{2,1,0:T(8,128)(2,1)S(1)} %get-tuple-element.70), channel_id=1, source_target_pairs={{0,4},{1,5},{2,6},{3,7},{4,8},{5,9},{6,10},{7,11},{8,12},{9,13},{1... | collective-permute-start | bytes 442376 | tf_op jit(solution)/shard_map/ppermute | solution.py:26
  134.4 11.0 %collective-permute-start.28 = (bf16[2,144,256]{2,1,0:T(8,128)(2,1)S(1)}, bf16[2,144,256]{2,1,0:T(8,128)(2,1)S(1)}, u32[]{:S(2)}, u32[]{:S(2)}) collective-permute-start(bf16[2,144,256]{2,1,0:T(8,128)(2,1)S(1)} %get-tuple-element.71), channel_id=1, source_target_pairs={{0,8},{1,9},{2,10},{3,11},{4,12},{5,13},{6,14},{7,15},{8,0},{9,1},... | collective-permute-start | bytes 442376 | tf_op jit(solution)/shard_map/ppermute | solution.py:26
  135.7 9.7 %collective-permute-start.29 = (bf16[2,144,256]{2,1,0:T(8,128)(2,1)S(1)}, bf16[2,144,256]{2,1,0:T(8,128)(2,1)S(1)}, u32[]{:S(2)}, u32[]{:S(2)}) collective-permute-start(bf16[2,144,256]{2,1,0:T(8,128)(2,1)S(1)} %get-tuple-element.72), channel_id=1, source_target_pairs={{0,12},{1,13},{2,14},{3,15},{4,0},{5,1},{6,2},{7,3},{8,4},{9,5},{1... | collective-permute-start | bytes 442376 | tf_op jit(solution)/shard_map/ppermute | solution.py:26
  146.3 11.0 %collective-permute-start.30 = (bf16[2,80,256]{2,1,0:T(8,128)(2,1)S(1)}, bf16[2,80,256]{2,1,0:T(8,128)(2,1)S(1)}, u32[]{:S(2)}, u32[]{:S(2)}) collective-permute-start(bf16[2,80,256]{2,1,0:T(8,128)(2,1)S(1)} %get-tuple-element.74), channel_id=1, source_target_pairs={{0,16},{1,17},{2,18},{3,19},{4,20},{5,21},{6,22},{7,23},{8,24},{9,... | collective-permute-start | bytes 245768 | tf_op jit(solution)/shard_map/ppermute | solution.py:26

commit v2 on v0

--- a/solution.py
+++ b/solution.py
@@ -83,14 +83,14 @@
 TICK = shape((8, 128), F32)
 
 
-def _forward_body(width, ids, p0, p1, p2, p3, wg, wu, wd, *rest):
-    mine, theirs, (acts, turned, held, last, loads, sems) = rest[:2], rest[2:8], rest[8:]
-    weights = [
-        pltpu.make_async_copy(weight, held.at[i], loads.at[i]) for i, weight in enumerate((wg, wu))
-    ] + [pltpu.make_async_copy(wd, last, loads.at[2])]
+def _forward_body(n, width, ids, *rest):
+    pieces, weights, rest = rest[:4], rest[4 : 4 + n], rest[4 + n :]
+    mine, theirs, rest = rest[:2], rest[2 : 2 + 2 * n], rest[2 + 2 * n :]
+    acts_out, acts, turned, held, sums, loads, stores, sems = rest
+    loading = [pltpu.make_async_copy(weight, held.at[i], loads.at[i]) for i, weight in enumerate(weights)]
     core, y, s1, s2 = ids[0], ids[1], ids[2], ids[3]
     copies = []
-    for k2, piece in enumerate((p0, p1, p2, p3)):
+    for k2, piece in enumerate(pieces):
         b = lax.rem(s2 + k2, 4)
         for k1 in range(4):
             a = lax.rem(s1 + k1, 4)
@@ -98,112 +98,121 @@
             for k0 in range(2):
                 at = pl.multiple_of((lax.rem(y + k0, 2) * 16 + zx) * 64, 64)
                 copies.append(
-                    pltpu.make_async_copy(
-                        piece.at[k1, k0], acts.at[:, pl.ds(at, 64), :], sems.at[len(copies)]
-                    )
+                    pltpu.make_async_copy(piece.at[k1, k0], acts.at[pl.ds(at, 64), :], sems.at[len(copies)])
                 )
     for copy in copies:
         copy.start()
-    for copy in weights:
+    for copy in loading:
         copy.start()
     for copy in copies:
         copy.wait()
+    out = [pltpu.make_async_copy(acts, acts_out, stores.at[0])]
+    out[0].start()
     half = mine[0].shape[0]
-    for i in range(2):
-        for n, place in enumerate((core, 1 - core)):
-            for c in range(2):
-                cols = pl.ds(pl.multiple_of((2 * c + place) * half, half), half)
-                row = (2 * n + c) * half
-                turned[i, row : row + half, :] = acts[i, :, cols].T
-    for i in range(3):
-        weights[i].wait()
-        weight = last if i == 2 else held.at[i]
-        dims = (((1,), (0,)), ((), ())) if i < 2 else (((1,), (1,)), ((), ()))
-        total = lax.dot_general(turned[i // 2], weight[...], dims, preferred_element_type=F32)
+    for m, place in enumerate((core, 1 - core)):
         for c in range(2):
-            mine[c][:, i * width : (i + 1) * width] = total[c * half : (c + 1) * half]
-            theirs[3 * c + i][...] = total[(2 + c) * half : (3 + c) * half]
+            cols = pl.ds(pl.multiple_of((2 * c + place) * half, half), half)
+            row = (2 * m + c) * half
+            turned[row : row + half, :] = acts[:, cols].T
+    for i in range(n):
+        loading[i].wait()
+        dims = (((1,), (0,)), ((), ())) if n == 2 else (((1,), (1,)), ((), ()))
+        sums[i] = lax.dot_general(turned[...], held[i], dims, preferred_element_type=F32)
+        for c in range(2):
+            for row, to in (
+                (c * half, mine[c].at[:, pl.ds(i * width, width)]),
+                ((2 + c) * half, theirs[n * c + i]),
+            ):
+                copy = pltpu.make_async_copy(sums.at[i, pl.ds(row, half), :], to, stores.at[len(out)])
+                copy.start()
+                out.append(copy)
+    for copy in out:
+        copy.wait()
 
 
 def _whole(*dims):
     return pl.BlockSpec(dims, lambda i: (0,) * len(dims))
 
 
-def forward(ids, pieces, wg, wu, wd):
-    depth, width = wg.shape
-    tokens = pieces[0].shape[-1]
-    mine, other = shape((tokens // 4, 3 * width), F32), shape((tokens // 4, width), F32)
-    return _call(
-        functools.partial(_forward_body, width),
-        (mine,) * 2 + (other,) * 6 + (shape((2, depth, tokens), BF16),),
+def forward(ids, pieces, weights, width):
+    n, tokens = len(weights), pieces[0].shape[-1]
+    depth = 32 * 64
+    mine, other = shape((tokens // 4, n * width), F32), shape((tokens // 4, width), F32)
+    *out, acts = _call(
+        functools.partial(_forward_body, n, width),
+        (mine,) * 2 + (other,) * (2 * n) + (shape((depth, tokens), BF16),),
         WHOLE,
-        in_specs=[SMEM] + [ANY] * 7,
-        out_specs=(VMEM,) * 9,
+        in_specs=[SMEM] + [ANY] * (4 + n),
+        out_specs=(ANY,) * (3 + 2 * n),
         scratch_shapes=[
-            pltpu.VMEM((2, tokens, depth), BF16),
-            pltpu.VMEM((2, depth, width), BF16),
-            pltpu.VMEM((width, depth), BF16),
-            pltpu.SemaphoreType.DMA((3,)),
+            pltpu.VMEM((depth, tokens), BF16),
+            pltpu.VMEM((tokens, depth), BF16),
+            pltpu.VMEM((n, *weights[0].shape), BF16),
+            pltpu.VMEM((n, tokens, width), F32),
+            pltpu.SemaphoreType.DMA((n,)),
+            pltpu.SemaphoreType.DMA((1 + 4 * n,)),
             pltpu.SemaphoreType.DMA((32,)),
         ],
         cost_estimate=_cost(
-            flops=6 * tokens * depth * width, bytes_accessed=6 * depth * width + 8 * depth * tokens, transcendentals=0
-        ),
-    )(ids, *pieces, wg, wu, wd)
-
-
-def _chip_body(width, mine, o0, o1, o2, chip, code, tick):
+            flops=2 * n * tokens * depth * width, bytes_accessed=2 * n * depth * width + 4 * depth * tokens, transcendentals=0
+        ),
+    )(ids, *pieces, *weights)
+    return (out[0], out[2 : 2 + n]), (out[1], out[2 + n :]), acts
+
+
+def _chip_body(n, width, mine, *rest):
+    others, (chip, code, tick) = rest[:n], rest[n:]
     tick[...] = jnp.zeros_like(tick)
-    for i in range(3):
+    for i in range(n):
         cols = slice(i * width, (i + 1) * width)
-        total = mine[:, cols] + (o0, o1, o2)[i][...]
+        total = mine[:, cols] + others[i][...]
         chip[:, cols] = total
         size = jnp.abs(total)
         top = jnp.max(jnp.max(size, axis=0, keepdims=True), axis=1, keepdims=True)
         top = jnp.maximum(top * 1.01, 1e-35).astype(BF16).astype(F32)
         code[:, cols] = encode(jnp.sqrt(size * (1.0 / top)), total >= 0)
-        code[16 * i : 16 * i + 16, 3 * width :] = jnp.broadcast_to(top, (16, 128)).astype(BF16)
-    code[48:, 3 * width :] = jnp.zeros((code.shape[0] - 48, 128), BF16)
+        code[16 * i : 16 * i + 16, n * width :] = jnp.broadcast_to(top, (16, 128)).astype(BF16)
+    code[16 * n :, n * width :] = jnp.zeros((code.shape[0] - 16 * n, 128), BF16)
 
 
 def chip_sum(mine, others):
-    rows, three = mine.shape
-    return _call(
-        functools.partial(_chip_body, three // 3),
-        (shape((rows, three), F32), shape((rows, three + 128), BF16), TICK),
-        in_specs=[VMEM] * 4,
+    (rows, whole), n = mine.shape, len(others)
+    return _call(
+        functools.partial(_chip_body, n, whole // n),
+        (shape((rows, whole), F32), shape((rows, whole + 128), BF16), TICK),
+        in_specs=[VMEM] * (1 + n),
         out_specs=(VMEM,) * 3,
         cost_estimate=_cost(
-            flops=20 * rows * three, bytes_accessed=14 * rows * three, transcendentals=2 * rows * three
+            flops=20 * rows * whole, bytes_accessed=14 * rows * whole, transcendentals=2 * rows * whole
         ),
     )(mine, *others)
 
 
-def _act_body(width, chip, code, _, o0, o1, o2):
-    def whole(i):
+def _act_body(width, chip, code, chip_h, code_h, _, o0, o1, o2):
+    def total(part, coded, i, n):
         cols = slice(i * width, (i + 1) * width)
-        u, positive = decode(code[:, cols])
-        top = code[16 * i : 16 * i + 16, 3 * width :].astype(F32)[0:1, 0:1]
-        return chip[:, cols] + _signed(u * u * top, positive)
-
-    gate, up, grad_hidden = whole(0), whole(1), whole(2)
+        u, positive = decode(coded[:, cols])
+        top = coded[16 * i : 16 * i + 16, n * width :].astype(F32)[0:1, 0:1]
+        return part[:, cols] + _signed(u * u * top, positive)
+
+    gate, up, grad_hidden = total(chip, code, 0, 2), total(chip, code, 1, 2), total(chip_h, code_h, 0, 1)
     squash = 1.0 / (1.0 + jnp.exp(-gate))
     o0[...] = gate * squash * up
     o1[...] = grad_hidden * up * squash * (1.0 + gate * (1.0 - squash))
     o2[...] = grad_hidden * gate * squash
 
 
-def activations(chip, code, after):
-    rows, three = chip.shape
-    return _call(
-        functools.partial(_act_body, three // 3),
-        (shape((rows, three // 3), F32),) * 3,
-        in_specs=[VMEM] * 2 + [ANY],
+def activations(chip, code, chip_h, code_h, after):
+    rows, width = chip_h.shape
+    return _call(
+        functools.partial(_act_body, width),
+        (shape((rows, width), F32),) * 3,
+        in_specs=[VMEM] * 4 + [ANY],
         out_specs=(VMEM,) * 3,
         cost_estimate=_cost(
-            flops=20 * rows * three, bytes_accessed=10 * rows * three, transcendentals=2 * rows * three
-        ),
-    )(chip, code, after)
+            flops=60 * rows * width, bytes_accessed=30 * rows * width, transcendentals=6 * rows * width
+        ),
+    )(chip, code, chip_h, code_h, after)
 
 
 def _pack(block):
@@ -219,7 +228,7 @@
 
 
 def _grad_in_body(width, n_before, ids, wg, wu, m0, m1, m2, o0, o1, o2, *rest):
-    before, (pair, own, c1, c2, c3, tick, right, tops, blocks, codes) = rest[:n_before], rest[n_before:]
+    before, (pair_out, own, c1, c2, c3, tick, pair, right, tops, blocks, codes, sem) = rest[:n_before], rest[n_before:]
     core, s1 = ids[0], ids[2]
     half = m0.shape[0]
     tokens = 2 * half
@@ -236,6 +245,8 @@
             if i:
                 right[rows, (2 * i - 2) * width : (2 * i - 1) * width] = high
                 right[rows, (2 * i - 1) * width : 2 * i * width] = low
+    store = pltpu.make_async_copy(pair, pair_out, sem)
+    store.start()
     for part in range(4):
         some = slice(part * 512, (part + 1) * 512)
         g, u = wg[some, :], wu[some, :]
@@ -260,6 +271,7 @@
     for n, out in ((1, c1), (2, c2), (3, c3)):
         out[c, 0:512, :] = codes[n]
         out[c, 512:528, :] = jnp.concatenate([tops[n], tops[n]], axis=0).astype(BF16)
+    store.wait()
 
 
 def grad_in(ids, wg, wu, mine, theirs, before):
@@ -272,12 +284,14 @@
         (shape((2 * tokens, three), BF16), shape((n, 512, tokens), F32), code, code, code, TICK),
         LARGE,
         in_specs=[SMEM] + [VMEM] * (8 + len(before)),
-        out_specs=(VMEM,) * 6,
+        out_specs=(ANY,) + (VMEM,) * 5,
         scratch_shapes=[
+            pltpu.VMEM((2 * tokens, three), BF16),
             pltpu.VMEM((tokens, 4 * width), BF16),
             pltpu.VMEM((4, 8, tokens), F32),
             pltpu.VMEM((4, 512, tokens), F32),
             pltpu.VMEM((4, 512, tokens), BF16),
+            pltpu.SemaphoreType.DMA,
         ],
         cost_estimate=_cost(
             flops=8 * tokens * 2048 * width, bytes_accessed=4 * 2048 * width + 16 * tokens * three, transcendentals=2048 * tokens
@@ -292,26 +306,26 @@
 
 
 def _grad_up_body(x, d0, d1, out):
-    rows = x[0]
+    rows = x[...]
     total = jnp.dot(_twice(rows, 0), d0[...], preferred_element_type=F32)
     total = total + jnp.dot(_twice(rows, 1), d1[...], preferred_element_type=F32)
     out[...] = total.astype(BF16)
 
 
-def grad_weight(acts, pairs, place, width):
-    depth, tokens = acts.shape[1:]
+def grad_weight(part, pairs, place, width):
+    depth, tokens = part.shape
     delta = pl.BlockSpec((tokens, width), lambda i: (0, place))
     return _call(
         _grad_up_body,
         shape((depth, width), BF16),
         WHOLE,
         grid=(depth // 512,),
-        in_specs=[pl.BlockSpec((1, 512, tokens), lambda i: (0, i, 0))] + [delta] * 2,
+        in_specs=[pl.BlockSpec((512, tokens), lambda i: (i, 0))] + [delta] * 2,
         out_specs=pl.BlockSpec((512, width), lambda i: (i, 0)),
         cost_estimate=_cost(
             flops=COST * 4 * tokens * depth * width, bytes_accessed=COST * 4 * depth * width, transcendentals=0
         ),
-    )(acts, *pairs)
+    )(part, *pairs)
 
 
 def _grad_down_body(g, h0, h1, out, turned):
@@ -320,27 +334,27 @@
         for i, h in enumerate((h0, h1)):
             turned[i] = h[...].T
 
-    rows, dims = g[0], (((1,), (1,)), ((), ()))
+    rows, dims = g[...], (((1,), (1,)), ((), ()))
     total = lax.dot_general(turned[0], _twice(rows, 0), dims, preferred_element_type=F32)
     total = total + lax.dot_general(turned[1], _twice(rows, 1), dims, preferred_element_type=F32)
     out[...] = total.astype(BF16)
 
 
-def grad_down_weight(acts, pairs, width):
-    depth, tokens = acts.shape[1:]
+def grad_down_weight(part, pairs, width):
+    depth, tokens = part.shape
     hidden = pl.BlockSpec((tokens, width), lambda i: (0, 0))
     return _call(
         _grad_down_body,
         shape((width, depth), BF16),
         WHOLE,
         grid=(depth // 512,),
-        in_specs=[pl.BlockSpec((1, 512, tokens), lambda i: (1, i, 0))] + [hidden] * 2,
+        in_specs=[pl.BlockSpec((512, tokens), lambda i: (i, 0))] + [hidden] * 2,
         out_specs=pl.BlockSpec((width, 512), lambda i: (0, i)),
         scratch_shapes=[pltpu.VMEM((2, width, tokens), BF16)],
         cost_estimate=_cost(
             flops=COST * 4 * tokens * depth * width, bytes_accessed=COST * 4 * depth * width, transcendentals=0
         ),
-    )(acts, *pairs)
+    )(part, *pairs)
 
 
 def _sum_first_body(ids, own, r1, r2, r3, own2, c1, c2, c3, tops):
@@ -435,17 +449,25 @@
     ids = jnp.stack([core, y, jnp.where(core == 0, x, z), jnp.where(core == 0, z, x)]).astype(jnp.int32)
     both = jnp.stack([inputs.T, grad_out.T])
     pair = jnp.stack([both, _send(both, _over_y)])
-    some = jnp.stack([pair] + [_send(pair, _first(-k)) for k in (1, 2, 3)])
-    pieces = [some] + [_send(some, _second(-k)) for k in (1, 2, 3)]
-    mine0, mine1, *theirs, acts = forward(ids, pieces, gate_weight, up_weight, down_weight)
-    chips, codes = [], []
-    for mine, others in ((mine0, theirs[:3]), (mine1, theirs[3:])):
+    near = [pair] + [_send(pair, _first(-k)) for k in (1, 2, 3)]
+    x, g = (jnp.stack([p[:, i] for p in near]) for i in range(2))
+    x1, x3 = _send(x, _second(-1)), _send(x, _second(1))
+    x2 = _send(x1, _second(-1))
+    g3, g1 = _send(g, _second(1)), _send(g, _second(-1))
+    g2 = _send(g3, _second(1))
+
+    def exchange(mine, others):
         chip, code, tick = chip_sum(mine, [_send(v, _over_core) for v in others])
-        chips.append(chip)
-        codes.append(_send(code, _over_lo))
+        return (chip, _send(code, _over_lo)), tick
+
+    *ups, x_acts = forward(ids, (x, x1, x2, x3), (gate_weight, up_weight), width)
+    ups = [exchange(*part)[0] for part in ups]
+    *downs, g_acts = forward(ids, (g, g1, g2, g3), (down_weight,), width)
+    downs = [exchange(*part) for part in downs]
+    tick = downs[1][1]
     pairs, part = [], ()
-    for chip, code in zip(chips, codes):
-        act = activations(chip, code, tick)
+    for c in range(2):
+        act = activations(*ups[c], *downs[c][0], tick)
         others = [_send(v, _over_core) for v in act]
         delta, *part, tick = grad_in(ids, gate_weight, up_weight, act, others, part)
         pairs.append(delta)
@@ -453,9 +475,9 @@
     own, *rest = sum_first(ids, own, [_send(v, _first(k + 1)) for k, v in enumerate(rest)])
     own, last = sum_second(ids, own, [_send(v, _second(k + 1)) for k, v in enumerate(rest)])
     grad_inputs = sum_last(own, _send(last, _over_y)).T
-    grad_gate = grad_weight(acts, pairs, 1, width)
-    grad_up = grad_weight(acts, pairs, 2, width)
-    grad_down = grad_down_weight(acts, pairs, width)
+    grad_gate = grad_weight(x_acts, pairs, 1, width)
+    grad_up = grad_weight(x_acts, pairs, 2, width)
+    grad_down = grad_down_weight(g_acts, pairs, width)
     return (grad_inputs, grad_gate, grad_up, grad_down)
 
 

time: 166 us -> 158 us (0.952)
  waiting for transfers between devices: 61.5 us -> 44.4 us
  starting transfers between devices: 32.1 us -> 39.4 us
  Pallas kernels: 62.4 us -> 65.3 us
    ppermute x28 -> x33, waiting for transfers between devices: 61.5 us -> 44.4 us  [_send(): return lax.ppermute(a, BOTH, _moves(shift))]
    ppermute x28 -> x33, starting transfers between devices: 32.1 us -> 39.4 us  [_send(): return lax.ppermute(a, BOTH, _moves(shift))]
    pallas_call x5 -> x8, Pallas kernels: 20.4 us -> 23.3 us  [the longest x2 18.2 us: forward(): _call(functools.partial(_forward_body, n, width), (mine,) * 2 + (other,)...]
    unnamed x20 -> x30, local copies, waits for them, and re-layouts: 6.8 us -> 5.92 us
  transfers between devices with their start and end apart: 28 -> 33, of which waited for: 22 -> 17; matrix products, arithmetic and copies ran while one was open for 0% -> 0% of each run, Pallas kernels for 19% -> 33%
where the time goes in v2:
time: 158 us
  Pallas kernels  65.3 us (41%)
  waiting for transfers between devices  44.4 us (28%)
  starting transfers between devices  39.4 us (25%)
  local copies, waits for them, and re-layouts  5.97 us (4%)
  other arithmetic  1.68 us (1%)
    ppermute x33, waiting for transfers between devices, _send(): return lax.ppermute(a, BOTH, _moves(shift))  44.4 us
    ppermute x33, starting transfers between devices, _send(): return lax.ppermute(a, BOTH, _moves(shift))  39.4 us
    pallas_call x2, Pallas kernels, forward(): _call(functools.partial(_forward_body, n, width), (mine,) * 2 + (other,)...  18.2 us
    pallas_call x2, Pallas kernels, grad_weight(): _call(_grad_up_body, shape((depth, width), BF16), WHOLE, grid=(depth // 5...  15.5 us
    pallas_call x2, Pallas kernels, grad_in(): _call(functools.partial(_grad_in_body, width, len(before)), (shape((2 * t...  14.5 us
    pallas_call x1, Pallas kernels, grad_down_weight(): _call(_grad_down_body, shape((width, depth), BF16), WHOLE, grid=(depth //...  7.96 us
    unnamed x30, local copies, waits for them, and re-layouts  5.92 us
  transfers between devices with their start and end apart: 33, of which 17 were waited for; matrix products, arithmetic and copies ran while one was open for 0% of the time, Pallas kernels for 33%

profile of v2, /device:TPU:0, one launch (start us, length us, event | category | flops | bytes accessed | tf_op | source)
XLA Modules:
  0.0 157.7 jit_solution(13452105726780194021)
XLA Ops:
  0.6 0.9 fusion.4
  1.5 3.4 %collective-permute-start = (bf16[2,64,512]{2,1,0:T(8,128)(2,1)S(1)}, bf16[2,64,512]{2,1,0:T(8,128)(2,1)S(1)}, u32[]{:S(2)}, u32[]{:S(2)}) collective-permute-start(bf16[2,64,512]{2,1,0:T(8,128)(2,1)S(1)} %get-tuple-element.101), channel_id=1, source_target_pairs={{0,16},{1,17},{2,18},{3,19},{4,20},{5,21},{6,22},{7,23},{8,24},{9,... | collective-permute-start | bytes 393224 | tf_op jit(solution)/shard_map/ppermute | solution.py:26
  4.9 3.5 %collective-permute-done = bf16[2,64,512]{2,1,0:T(8,128)(2,1)S(1)} collective-permute-done((bf16[2,64,512]{2,1,0:T(8,128)(2,1)S(1)}, bf16[2,64,512]{2,1,0:T(8,128)(2,1)S(1)}, u32[]{:S(2)}, u32[]{:S(2)}) %collective-permute-start) | collective-permute-done | bytes 131104 | tf_op jit(solution)/shard_map/ppermute | solution.py:26
  8.4 3.2 %collective-permute-start.2 = (bf16[2,2,64,512]{3,2,0,1:T(8,128)(2,1)S(1)}, bf16[2,2,64,512]{3,2,0,1:T(8,128)(2,1)S(1)}, u32[]{:S(2)}, u32[]{:S(2)}) collective-permute-start(bf16[2,2,64,512]{3,2,0,1:T(8,128)(2,1)S(1)} %pad_maximum_fusion.2), channel_id=1, source_target_pairs={{0,2},{1,3},{2,0},{3,1},{4,6},{5,7},{6,4},{7,5},{8,10},{9,11},{10,... | collective-permute-start | bytes 786440 | tf_op jit(solution)/shard_map/ppermute | solution.py:26
  11.6 1.1 collective-permute-start.1
  12.7 1.0 collective-permute-start.3
  13.7 2.7 %collective-permute-done.2 = bf16[2,2,64,512]{3,2,0,1:T(8,128)(2,1)S(1)} collective-permute-done((bf16[2,2,64,512]{3,2,0,1:T(8,128)(2,1)S(1)}, bf16[2,2,64,512]{3,2,0,1:T(8,128)(2,1)S(1)}, u32[]{:S(2)}, u32[]{:S(2)}) %collective-permute-start.2) | collective-permute-done | bytes 262176 | tf_op jit(solution)/shard_map/ppermute | solution.py:26
  16.4 2.9 %collective-permute-done.1 = bf16[2,2,64,512]{3,2,0,1:T(8,128)(2,1)S(1)} collective-permute-done((bf16[2,2,64,512]{3,2,0,1:T(8,128)(2,1)S(1)}, bf16[2,2,64,512]{3,2,0,1:T(8,128)(2,1)S(1)}, u32[]{:S(2)}, u32[]{:S(2)}) %collective-permute-start.1) | collective-permute-done | bytes 262176 | tf_op jit(solution)/shard_map/ppermute | solution.py:26
  19.4 1.0 collective-permute-done.3
  20.5 4.1 %collective-permute-start.4 = (bf16[4,2,64,512]{3,2,1,0:T(8,128)(2,1)S(1)}, bf16[4,2,64,512]{3,2,1,0:T(8,128)(2,1)S(1)}, u32[]{:S(2)}, u32[]{:S(2)}) collective-permute-start(bf16[4,2,64,512]{3,2,1,0:T(8,128)(2,1)S(1)} %pad_maximum_fusion.rest_0_), channel_id=1, source_target_pairs={{0,12},{1,13},{2,14},{3,15},{4,0},{5,1},{6,2},{7,3},{8,4},{9,5},{1... | collective-permute-start | bytes 1572872 | tf_op jit(solution)/shard_map/ppermute | solution.py:26
  24.8 6.5 %collective-permute-done.4.rest_1_ = bf16[4,2,64,512]{3,2,1,0:T(8,128)(2,1)S(1)} collective-permute-done((bf16[4,2,64,512]{3,2,1,0:T(8,128)(2,1)S(1)}, bf16[4,2,64,512]{3,2,1,0:T(8,128)(2,1)S(1)}, u32[]{:S(2)}, u32[]{:S(2)}) %collective-permute-start.4) | collective-permute-done | bytes 524320 | tf_op jit(solution)/shard_map/ppermute | solution.py:26
  31.3 3.7 %collective-permute-start.5 = (bf16[4,2,64,512]{3,2,1,0:T(8,128)(2,1)S(1)}, bf16[4,2,64,512]{3,2,1,0:T(8,128)(2,1)S(1)}, u32[]{:S(2)}, u32[]{:S(2)}) collective-permute-start(bf16[4,2,64,512]{3,2,1,0:T(8,128)(2,1)S(1)} %collective-permute-done.4.rest_1_), channel_id=1, source_target_pairs={{0,12},{1,13},{2,14},{3,15},{4,0},{5,1},{6,2},{7,3},{8,4},{9,5},{1... | collective-permute-start | bytes 1572872 | tf_op jit(solution)/shard_map/ppermute | solution.py:26
  35.1 1.9 %collective-permute-start.12 = (bf16[4,2,64,512]{3,2,1,0:T(8,128)(2,1)S(1)}, bf16[4,2,64,512]{3,2,1,0:T(8,128)(2,1)}, u32[]{:S(2)}, u32[]{:S(2)}) collective-permute-start(bf16[4,2,64,512]{3,2,1,0:T(8,128)(2,1)S(1)} %collective-permute-done.11.rest_3_), channel_id=1, source_target_pairs={{0,4},{1,5},{2,6},{3,7},{4,8},{5,9},{6,10},{7,11},{8,12},{9,13},{1... | collective-permute-start | bytes 1572872 | tf_op jit(solution)/shard_map/ppermute | solution.py:26
  37.6 3.1 %collective-permute-done.6.rest_3_ = bf16[4,2,64,512]{3,2,1,0:T(8,128)(2,1)S(1)} collective-permute-done((bf16[4,2,64,512]{3,2,1,0:T(8,128)(2,1)S(1)}, bf16[4,2,64,512]{3,2,1,0:T(8,128)(2,1)S(1)}, u32[]{:S(2)}, u32[]{:S(2)}) %collective-permute-start.6) | collective-permute-done | bytes 524320 | tf_op jit(solution)/shard_map/ppermute | solution.py:26
  40.8 0.9 collective-permute-done.5.rest_2_
  41.7 0.8 copy-done.14
  42.5 10.3 %shard_map.84 = (f32[128,1792]{1,0:T(8,128)}, f32[128,1792]{1,0:T(8,128)}, f32[128,896]{1,0:T(8,128)}, f32[128,896]{1,0:T(8,128)}, f32[128,896]{1,0:T(8,128)}, /...) custom-call(s32[4]{0:T(128)} %pad_add_fusion.ids, bf16[4,2,64,512]{3,2,1,0:T(8,128)(2,1)} %copy-done.10, ...), custom_call_target="tpu_custom_call" | custom-call | flops 187904816 | bytes 576716 | tf_op jit(solution)/shard_map/pallas_call | solution.py:141
  53.4 8.0 %shard_map.86 = (f32[128,896]{1,0:T(8,128)}, f32[128,896]{1,0:T(8,128)}, f32[128,896]{1,0:T(8,128)}, f32[128,896]{1,0:T(8,128)}, bf16[2048,512]{1,0:T(8,128)(2,1)}) custom-call(s32[4]{0:T(128)} %pad_add_fusion.ids, bf16[4,2,64,512]{3,2,1,0:T(8,128)(2,1)} %copy-done.9, bf16[4,2,64,512]{3,2,1,0:T(8,128)(2,1)} %collective-permute-done.10.rest_1_, ...), custom_call_target="tpu_custom_call" | custom-call | flops 93952408 | bytes 393216 | tf_op jit(solution)/shard_map/pallas_call | solution.py:141
  61.7 0.8 shard_map.88
  62.5 1.6 collective-permute-start.17
  64.6 1.0 copy-done.5
  66.2 0.8 collective-permute-start.19
  67.1 0.8 shard_map.85
  67.9 1.2 collective-permute-start.9
  69.1 1.0 copy-done.4
  70.5 11.7 %collective-permute-done.19.code_h = bf16[128,1024]{1,0:T(8,128)(2,1)S(1)} collective-permute-done((bf16[128,1024]{1,0:T(8,128)(2,1)S(1)}, bf16[128,1024]{1,0:T(8,128)(2,1)S(1)}, u32[]{:S(2)}, u32[]{:S(2)}) %collective-permute-start.19) | collective-permute-done | bytes 262176 | tf_op jit(solution)/shard_map/ppermute | solution.py:26
  82.2 1.2 shard_map.90
  84.1 1.6 collective-permute-start.14
  86.6 6.1 %shard_map.91 = (bf16[512,2688]{1,0:T(8,128)(2,1)S(1)}, f32[1,512,256]{2,1,0:T(8,128)S(1)}, bf16[1,528,256]{2,1,0:T(8,128)(2,1)S(1)}, bf16[1,528,256]{2,1,0:T(8,...) custom-call(s32[4]{0:T(128)S(1)} %copy-done.6, bf16[2048,896]{1,0:T(8,128)(2,1)S(1)} %copy-done, ...), custom_call_target="tpu_custom_call" | custom-call | flops 187904816 | bytes 917504 | tf_op jit(solution)/shard_map/pallas_call | solution.py:282
  92.7 1.5 copy-done.7
  94.2 3.5 %collective-permute-done.14.code_h = bf16[128,1024]{1,0:T(8,128)(2,1)S(1)} collective-permute-done((bf16[128,1024]{1,0:T(8,128)(2,1)S(1)}, bf16[128,1024]{1,0:T(8,128)(2,1)S(1)}, u32[]{:S(2)}, u32[]{:S(2)}) %collective-permute-start.14) | collective-permute-done | bytes 262176 | tf_op jit(solution)/shard_map/ppermute | solution.py:26
  97.7 1.2 shard_map.92
  99.6 1.2 collective-permute-done.23.o0
  100.8 0.7 collective-permute-done.24.o1
  102.1 8.4 %shard_map.93 = (bf16[512,2688]{1,0:T(8,128)(2,1)S(1)}, f32[2,512,256]{2,1,0:T(8,128)S(1)}, bf16[2,528,256]{2,1,0:T(8,128)(2,1)}, bf16[2,528,256]{2,1,0:T(8,128)...) custom-call(s32[4]{0:T(128)S(1)} %copy-done.6, bf16[2048,896]{1,0:T(8,128)(2,1)S(1)} %copy-done, ...), custom_call_target="tpu_custom_call" | custom-call | flops 187904816 | bytes 917504 | tf_op jit(solution)/shard_map/pallas_call | solution.py:282
  110.6 1.5 copy-done.8
  112.5 2.7 %collective-permute-start.27 = (bf16[2,528,256]{2,1,0:T(8,128)(2,1)S(1)}, bf16[2,528,256]{2,1,0:T(8,128)(2,1)S(1)}, u32[]{:S(2)}, u32[]{:S(2)}) collective-permute-start(bf16[2,528,256]{2,1,0:T(8,128)(2,1)S(1)} %get-tuple-element.80), channel_id=1, source_target_pairs={{0,2},{1,3},{2,0},{3,1},{4,6},{5,7},{6,4},{7,5},{8,10},{9,11},{10,... | collective-permute-start | bytes 1622024 | tf_op jit(solution)/shard_map/ppermute | solution.py:26
  115.2 1.4 collective-permute-start.28
  116.6 7.7 %shard_map.98 = bf16[2048,896]{1,0:T(8,128)(2,1)} custom-call(bf16[2048,512]{1,0:T(8,128)(2,1)} %get-tuple-element.88.x, bf16[512,2688]{1,0:T(8,128)(2,1)} %copy-done.7, bf16[512,2688]{1,0:T(8,128)(2,1)} %copy-done.8), custom_call_target="tpu_custom_call" | custom-call | flops 3758096384 | bytes 7340032 | tf_op jit(solution)/shard_map/pallas_call | solution.py:318
  124.4 4.3 %collective-permute-done.26.r1 = bf16[2,528,256]{2,1,0:T(8,128)(2,1)S(1)} collective-permute-done((bf16[2,528,256]{2,1,0:T(8,128)(2,1)}, bf16[2,528,256]{2,1,0:T(8,128)(2,1)S(1)}, u32[]{:S(2)}, u32[]{:S(2)}) %collective-permute-start.26) | collective-permute-done | bytes 540704 | tf_op jit(solution)/shard_map/ppermute | solution.py:26
  128.7 0.7 collective-permute-done.28.r3
  129.4 2.5 %shard_map.94 = (f32[2,128,256]{2,1,0:T(8,128)S(1)}, bf16[2,144,256]{2,1,0:T(8,128)(2,1)S(1)}, bf16[2,144,256]{2,1,0:T(8,128)(2,1)S(1)}, bf16[2,144,256]{2,1,0:T(8,128)(2,1)S(1)}) custom-call(s32[4]{0:T(128)S(1)} %copy-done.6, f32[2,512,256]{2,1,0:T(8,128)S(1)} %get-tuple-element.78.own, bf16[2,528,256]{2,1,0:T(8,128)(2,1)S(1)} %collective-permute-done.26.r1, ...), custom_call_target="tpu_custom_call" | custom-call | tf_op jit(solution)/shard_map/pallas_call | solution.py:392
  132.0 5.2 %collective-permute-start.30 = (bf16[2,144,256]{2,1,0:T(8,128)(2,1)S(1)}, bf16[2,144,256]{2,1,0:T(8,128)(2,1)S(1)}, u32[]{:S(2)}, u32[]{:S(2)}) collective-permute-start(bf16[2,144,256]{2,1,0:T(8,128)(2,1)S(1)} %get-tuple-element.84), channel_id=1, source_target_pairs={{0,8},{1,9},{2,10},{3,11},{4,12},{5,13},{6,14},{7,15},{8,0},{9,1},... | collective-permute-start | bytes 442376 | tf_op jit(solution)/shard_map/ppermute | solution.py:26
  137.1 7.7 %shard_map.97 = bf16[2048,896]{1,0:T(8,128)(2,1)} custom-call(bf16[2048,512]{1,0:T(8,128)(2,1)} %get-tuple-element.88.x, bf16[512,2688]{1,0:T(8,128)(2,1)} %copy-done.7, bf16[512,2688]{1,0:T(8,128)(2,1)} %copy-done.8), custom_call_target="tpu_custom_call" | custom-call | flops 3758096384 | bytes 7340032 | tf_op jit(solution)/shard_map/pallas_call | solution.py:318
  144.9 0.9 shard_map.95
  145.8 3.3 %collective-permute-start.32 = (bf16[2,80,256]{2,1,0:T(8,128)(2,1)S(1)}, bf16[2,80,256]{2,1,0:T(8,128)(2,1)S(1)}, u32[]{:S(2)}, u32[]{:S(2)}) collective-permute-start(bf16[2,80,256]{2,1,0:T(8,128)(2,1)S(1)} %get-tuple-element.87), channel_id=1, source_target_pairs={{0,16},{1,17},{2,18},{3,19},{4,20},{5,21},{6,22},{7,23},{8,24},{9,... | collective-permute-start | bytes 245768 | tf_op jit(solution)/shard_map/ppermute | solution.py:26
  149.1 8.0 %shard_map.99 = bf16[896,2048]{1,0:T(8,128)(2,1)} custom-call(bf16[2048,512]{1,0:T(8,128)(2,1)} %get-tuple-element.91.g, bf16[512,2688]{1,0:T(8,128)(2,1)} %copy-done.7, bf16[512,2688]{1,0:T(8,128)(2,1)} %copy-done.8), custom_call_target="tpu_custom_call" | custom-call | flops 3758096384 | bytes 7340032 | tf_op jit(solution)/shard_map/pallas_call | solution.py:346
  157.0 0.7 shard_map.96
  (73 shorter events, 7.1 us)
Async XLA Ops:
  1.5 6.9 %collective-permute-start = (bf16[2,64,512]{2,1,0:T(8,128)(2,1)S(1)}, bf16[2,64,512]{2,1,0:T(8,128)(2,1)S(1)}, u32[]{:S(2)}, u32[]{:S(2)}) collective-permute-start(bf16[2,64,512]{2,1,0:T(8,128)(2,1)S(1)} %get-tuple-element.101), channel_id=1, source_target_pairs={{0,16},{1,17},{2,18},{3,19},{4,20},{5,21},{6,22},{7,23},{8,24},{9,... | collective-permute-start | bytes 393224 | tf_op jit(solution)/shard_map/ppermute | solution.py:26
  8.4 8.0 %collective-permute-start.2 = (bf16[2,2,64,512]{3,2,0,1:T(8,128)(2,1)S(1)}, bf16[2,2,64,512]{3,2,0,1:T(8,128)(2,1)S(1)}, u32[]{:S(2)}, u32[]{:S(2)}) collective-permute-start(bf16[2,2,64,512]{3,2,0,1:T(8,128)(2,1)S(1)} %pad_maximum_fusion.2), channel_id=1, source_target_pairs={{0,2},{1,3},{2,0},{3,1},{4,6},{5,7},{6,4},{7,5},{8,10},{9,11},{10,... | collective-permute-start | bytes 786440 | tf_op jit(solution)/shard_map/ppermute | solution.py:26
  11.6 7.8 %collective-permute-start.1 = (bf16[2,2,64,512]{3,2,0,1:T(8,128)(2,1)S(1)}, bf16[2,2,64,512]{3,2,0,1:T(8,128)(2,1)S(1)}, u32[]{:S(2)}, u32[]{:S(2)}) collective-permute-start(bf16[2,2,64,512]{3,2,0,1:T(8,128)(2,1)S(1)} %pad_maximum_fusion.2), channel_id=1, source_target_pairs={{0,3},{1,0},{2,1},{3,2},{4,7},{5,4},{6,5},{7,6},{8,11},{9,8},{10,9... | collective-permute-start | bytes 786440 | tf_op jit(solution)/shard_map/ppermute | solution.py:26
  12.7 7.7 %collective-permute-start.3 = (bf16[2,2,64,512]{3,2,0,1:T(8,128)(2,1)S(1)}, bf16[2,2,64,512]{3,2,0,1:T(8,128)(2,1)S(1)}, u32[]{:S(2)}, u32[]{:S(2)}) collective-permute-start(bf16[2,2,64,512]{3,2,0,1:T(8,128)(2,1)S(1)} %pad_maximum_fusion.2), channel_id=1, source_target_pairs={{0,1},{1,2},{2,3},{3,0},{4,5},{5,6},{6,7},{7,4},{8,9},{9,10},{10,1... | collective-permute-start | bytes 786440 | tf_op jit(solution)/shard_map/ppermute | solution.py:26
  20.5 21.2 %copy-start.10 = (bf16[4,2,64,512]{3,2,1,0:T(8,128)(2,1)}, bf16[4,2,64,512]{3,2,1,0:T(8,128)(2,1)S(1)}, u32[]{:S(2)}) copy-start(bf16[4,2,64,512]{3,2,1,0:T(8,128)(2,1)S(1)} %pad_maximum_fusion.rest_0_) | copy-start | bytes 1572868
  20.5 10.8 %collective-permute-start.4 = (bf16[4,2,64,512]{3,2,1,0:T(8,128)(2,1)S(1)}, bf16[4,2,64,512]{3,2,1,0:T(8,128)(2,1)S(1)}, u32[]{:S(2)}, u32[]{:S(2)}) collective-permute-start(bf16[4,2,64,512]{3,2,1,0:T(8,128)(2,1)S(1)} %pad_maximum_fusion.rest_0_), channel_id=1, source_target_pairs={{0,12},{1,13},{2,14},{3,15},{4,0},{5,1},{6,2},{7,3},{8,4},{9,5},{1... | collective-permute-start | bytes 1572872 | tf_op jit(solution)/shard_map/ppermute | solution.py:26
  24.7 28.1 %copy-start.9 = (bf16[4,2,64,512]{3,2,1,0:T(8,128)(2,1)}, bf16[4,2,64,512]{3,2,1,0:T(8,128)(2,1)S(1)}, u32[]{:S(2)}) copy-start(bf16[4,2,64,512]{3,2,1,0:T(8,128)(2,1)S(1)} %pad_maximum_fusion.1.rest_0_) | copy-start | bytes 1572868
  24.7 10.5 %collective-permute-start.11 = (bf16[4,2,64,512]{3,2,1,0:T(8,128)(2,1)S(1)}, bf16[4,2,64,512]{3,2,1,0:T(8,128)(2,1)S(1)}, u32[]{:S(2)}, u32[]{:S(2)}) collective-permute-start(bf16[4,2,64,512]{3,2,1,0:T(8,128)(2,1)S(1)} %pad_maximum_fusion.1.rest_0_), channel_id=1, source_target_pairs={{0,4},{1,5},{2,6},{3,7},{4,8},{5,9},{6,10},{7,11},{8,12},{9,13},{1... | collective-permute-start | bytes 1572872 | tf_op jit(solution)/shard_map/ppermute | solution.py:26
  24.8 16.0 %collective-permute-start.6 = (bf16[4,2,64,512]{3,2,1,0:T(8,128)(2,1)S(1)}, bf16[4,2,64,512]{3,2,1,0:T(8,128)(2,1)S(1)}, u32[]{:S(2)}, u32[]{:S(2)}) collective-permute-start(bf16[4,2,64,512]{3,2,1,0:T(8,128)(2,1)S(1)} %pad_maximum_fusion.rest_0_), channel_id=1, source_target_pairs={{0,4},{1,5},{2,6},{3,7},{4,8},{5,9},{6,10},{7,11},{8,12},{9,13},{1... | collective-permute-start | bytes 1572872 | tf_op jit(solution)/shard_map/ppermute | solution.py:26
  31.3 10.4 %copy-start.12 = (bf16[4,2,64,512]{3,2,1,0:T(8,128)(2,1)}, bf16[4,2,64,512]{3,2,1,0:T(8,128)(2,1)S(1)}, u32[]{:S(2)}) copy-start(bf16[4,2,64,512]{3,2,1,0:T(8,128)(2,1)S(1)} %collective-permute-done.4.rest_1_) | copy-start | bytes 1572868
  31.3 10.4 %collective-permute-start.5 = (bf16[4,2,64,512]{3,2,1,0:T(8,128)(2,1)S(1)}, bf16[4,2,64,512]{3,2,1,0:T(8,128)(2,1)S(1)}, u32[]{:S(2)}, u32[]{:S(2)}) collective-permute-start(bf16[4,2,64,512]{3,2,1,0:T(8,128)(2,1)S(1)} %collective-permute-done.4.rest_1_), channel_id=1, source_target_pairs={{0,12},{1,13},{2,14},{3,15},{4,0},{5,1},{6,2},{7,3},{8,4},{9,5},{1... | collective-permute-start | bytes 1572872 | tf_op jit(solution)/shard_map/ppermute | solution.py:26
  35.0 18.4 %collective-permute-start.10 = (bf16[4,2,64,512]{3,2,1,0:T(8,128)(2,1)S(1)}, bf16[4,2,64,512]{3,2,1,0:T(8,128)(2,1)}, u32[]{:S(2)}, u32[]{:S(2)}) collective-permute-start(bf16[4,2,64,512]{3,2,1,0:T(8,128)(2,1)S(1)} %pad_maximum_fusion.1.rest_0_), channel_id=1, source_target_pairs={{0,12},{1,13},{2,14},{3,15},{4,0},{5,1},{6,2},{7,3},{8,4},{9,5},{1... | collective-permute-start | bytes 1572872 | tf_op jit(solution)/shard_map/ppermute | solution.py:26
  35.1 17.6 %copy-start.11 = (bf16[4,2,64,512]{3,2,1,0:T(8,128)(2,1)}, bf16[4,2,64,512]{3,2,1,0:T(8,128)(2,1)S(1)}, u32[]{:S(2)}) copy-start(bf16[4,2,64,512]{3,2,1,0:T(8,128)(2,1)S(1)} %collective-permute-done.11.rest_3_) | copy-start | bytes 1572868
  35.1 18.2 %collective-permute-start.12 = (bf16[4,2,64,512]{3,2,1,0:T(8,128)(2,1)S(1)}, bf16[4,2,64,512]{3,2,1,0:T(8,128)(2,1)}, u32[]{:S(2)}, u32[]{:S(2)}) collective-permute-start(bf16[4,2,64,512]{3,2,1,0:T(8,128)(2,1)S(1)} %collective-permute-done.11.rest_3_), channel_id=1, source_target_pairs={{0,4},{1,5},{2,6},{3,7},{4,8},{5,9},{6,10},{7,11},{8,12},{9,13},{1... | collective-permute-start | bytes 1572872 | tf_op jit(solution)/shard_map/ppermute | solution.py:26
  40.8 0.9 copy-start.13
  41.7 0.8 copy-start.14
  52.8 8.9 %copy-start.3 = (f32[128,1792]{1,0:T(8,128)S(1)}, f32[128,1792]{1,0:T(8,128)}, u32[]{:S(2)}) copy-start(f32[128,1792]{1,0:T(8,128)} %get-tuple-element.57.mine) | copy-start | bytes 2752516
  52.8 8.9 %collective-permute-start.15 = (f32[128,896]{1,0:T(8,128)}, f32[128,896]{1,0:T(8,128)S(1)}, u32[]{:S(2)}, u32[]{:S(2)}) collective-permute-start(f32[128,896]{1,0:T(8,128)} %get-tuple-element.58), channel_id=1, source_target_pairs={{0,32},{1,33},{2,34},{3,35},{4,36},{5,37},{6,38},{7,39},{8,40},{9,... | collective-permute-start | bytes 1376264 | tf_op jit(solution)/shard_map/ppermute | solution.py:26
  52.9 14.2 %copy-start.2 = (f32[128,1792]{1,0:T(8,128)S(1)}, f32[128,1792]{1,0:T(8,128)}, u32[]{:S(2)}) copy-start(f32[128,1792]{1,0:T(8,128)} %get-tuple-element.48.mine) | copy-start | bytes 2752516
  52.9 8.8 %collective-permute-start.16 = (f32[128,896]{1,0:T(8,128)}, f32[128,896]{1,0:T(8,128)S(1)}, u32[]{:S(2)}, u32[]{:S(2)}) collective-permute-start(f32[128,896]{1,0:T(8,128)} %get-tuple-element.59), channel_id=1, source_target_pairs={{0,32},{1,33},{2,34},{3,35},{4,36},{5,37},{6,38},{7,39},{8,40},{9,... | collective-permute-start | bytes 1376264 | tf_op jit(solution)/shard_map/ppermute | solution.py:26
  61.4 3.2 %collective-permute-start.18 = (f32[128,896]{1,0:T(8,128)}, f32[128,896]{1,0:T(8,128)S(1)}, u32[]{:S(2)}, u32[]{:S(2)}) collective-permute-start(f32[128,896]{1,0:T(8,128)} %get-tuple-element.63), channel_id=1, source_target_pairs={{0,32},{1,33},{2,34},{3,35},{4,36},{5,37},{6,38},{7,39},{8,40},{9,... | collective-permute-start | bytes 1376264 | tf_op jit(solution)/shard_map/ppermute | solution.py:26
  61.7 24.9 %copy-start.6 = (s32[4]{0:T(128)S(1)}, s32[4]{0:T(128)}, u32[]{:S(2)}) copy-start(s32[4]{0:T(128)} %pad_add_fusion.ids) | copy-start | bytes 52
  61.7 24.9 %copy-start = (bf16[2048,896]{1,0:T(8,128)(2,1)S(1)}, bf16[2048,896]{1,0:T(8,128)(2,1)}, u32[]{:S(2)}) copy-start(bf16[2048,896]{1,0:T(8,128)(2,1)} %wg.3) | copy-start | bytes 11010052
  61.7 24.9 %copy-start.1 = (bf16[2048,896]{1,0:T(8,128)(2,1)S(1)}, bf16[2048,896]{1,0:T(8,128)(2,1)}, u32[]{:S(2)}) copy-start(bf16[2048,896]{1,0:T(8,128)(2,1)} %wu.3) | copy-start | bytes 11010052
  62.5 19.7 %collective-permute-start.17 = (bf16[128,1920]{1,0:T(8,128)(2,1)S(1)}, bf16[128,1920]{1,0:T(8,128)(2,1)S(1)}, u32[]{:S(2)}, u32[]{:S(2)}) collective-permute-start(bf16[128,1920]{1,0:T(8,128)(2,1)S(1)} %get-tuple-element.61), channel_id=1, source_target_pairs={{0,64},{1,65},{2,66},{3,67},{4,68},{5,69},{6,70},{7,71},{8,72},{9,... | collective-permute-start | bytes 1474568 | tf_op jit(solution)/shard_map/ppermute | solution.py:26
  64.1 3.0 %collective-permute-start.7 = (f32[128,896]{1,0:T(8,128)}, f32[128,896]{1,0:T(8,128)S(1)}, u32[]{:S(2)}, u32[]{:S(2)}) collective-permute-start(f32[128,896]{1,0:T(8,128)} %get-tuple-element.49), channel_id=1, source_target_pairs={{0,32},{1,33},{2,34},{3,35},{4,36},{5,37},{6,38},{7,39},{8,40},{9,... | collective-permute-start | bytes 1376264 | tf_op jit(solution)/shard_map/ppermute | solution.py:26
  64.1 3.0 %collective-permute-start.8 = (f32[128,896]{1,0:T(8,128)}, f32[128,896]{1,0:T(8,128)S(1)}, u32[]{:S(2)}, u32[]{:S(2)}) collective-permute-start(f32[128,896]{1,0:T(8,128)} %get-tuple-element.50), channel_id=1, source_target_pairs={{0,32},{1,33},{2,34},{3,35},{4,36},{5,37},{6,38},{7,39},{8,40},{9,... | collective-permute-start | bytes 1376264 | tf_op jit(solution)/shard_map/ppermute | solution.py:26
  64.6 4.5 %collective-permute-start.13 = (f32[128,896]{1,0:T(8,128)}, f32[128,896]{1,0:T(8,128)S(1)}, u32[]{:S(2)}, u32[]{:S(2)}) collective-permute-start(f32[128,896]{1,0:T(8,128)} %get-tuple-element.54), channel_id=1, source_target_pairs={{0,32},{1,33},{2,34},{3,35},{4,36},{5,37},{6,38},{7,39},{8,40},{9,... | collective-permute-start | bytes 1376264 | tf_op jit(solution)/shard_map/ppermute | solution.py:26
  64.6 1.0 copy-start.5
  66.2 16.0 %collective-permute-start.19 = (bf16[128,1024]{1,0:T(8,128)(2,1)S(1)}, bf16[128,1024]{1,0:T(8,128)(2,1)S(1)}, u32[]{:S(2)}, u32[]{:S(2)}) collective-permute-start(bf16[128,1024]{1,0:T(8,128)(2,1)S(1)} %get-tuple-element.65), channel_id=1, source_target_pairs={{0,64},{1,65},{2,66},{3,67},{4,68},{5,69},{6,70},{7,71},{8,72},{9,... | collective-permute-start | bytes 786440 | tf_op jit(solution)/shard_map/ppermute | solution.py:26
  67.9 29.8 %collective-permute-start.9 = (bf16[128,1920]{1,0:T(8,128)(2,1)S(1)}, bf16[128,1920]{1,0:T(8,128)(2,1)S(1)}, u32[]{:S(2)}, u32[]{:S(2)}) collective-permute-start(bf16[128,1920]{1,0:T(8,128)(2,1)S(1)} %get-tuple-element.52), channel_id=1, source_target_pairs={{0,64},{1,65},{2,66},{3,67},{4,68},{5,69},{6,70},{7,71},{8,72},{9,... | collective-permute-start | bytes 1474568 | tf_op jit(solution)/shard_map/ppermute | solution.py:26
  69.1 1.0 copy-start.4
  83.4 2.3 %collective-permute-start.20 = (f32[128,896]{1,0:T(8,128)S(1)}, f32[128,896]{1,0:T(8,128)S(1)}, u32[]{:S(2)}, u32[]{:S(2)}) collective-permute-start(f32[128,896]{1,0:T(8,128)S(1)} %get-tuple-element.67.m0), channel_id=1, source_target_pairs={{0,32},{1,33},{2,34},{3,35},{4,36},{5,37},{6,38},{7,39},{8,40},{9,... | collective-permute-start | bytes 1376264 | tf_op jit(solution)/shard_map/ppermute | solution.py:26
  83.5 2.5 %collective-permute-start.21 = (f32[128,896]{1,0:T(8,128)S(1)}, f32[128,896]{1,0:T(8,128)S(1)}, u32[]{:S(2)}, u32[]{:S(2)}) collective-permute-start(f32[128,896]{1,0:T(8,128)S(1)} %get-tuple-element.68.m1), channel_id=1, source_target_pairs={{0,32},{1,33},{2,34},{3,35},{4,36},{5,37},{6,38},{7,39},{8,40},{9,... | collective-permute-start | bytes 1376264 | tf_op jit(solution)/shard_map/ppermute | solution.py:26
  84.0 2.6 %collective-permute-start.22 = (f32[128,896]{1,0:T(8,128)S(1)}, f32[128,896]{1,0:T(8,128)S(1)}, u32[]{:S(2)}, u32[]{:S(2)}) collective-permute-start(f32[128,896]{1,0:T(8,128)S(1)} %get-tuple-element.69.m2), channel_id=1, source_target_pairs={{0,32},{1,33},{2,34},{3,35},{4,36},{5,37},{6,38},{7,39},{8,40},{9,... | collective-permute-start | bytes 1376264 | tf_op jit(solution)/shard_map/ppermute | solution.py:26
  84.1 13.6 %collective-permute-start.14 = (bf16[128,1024]{1,0:T(8,128)(2,1)S(1)}, bf16[128,1024]{1,0:T(8,128)(2,1)S(1)}, u32[]{:S(2)}, u32[]{:S(2)}) collective-permute-start(bf16[128,1024]{1,0:T(8,128)(2,1)S(1)} %get-tuple-element.56), channel_id=1, source_target_pairs={{0,64},{1,65},{2,66},{3,67},{4,68},{5,69},{6,70},{7,71},{8,72},{9,... | collective-permute-start | bytes 786440 | tf_op jit(solution)/shard_map/ppermute | solution.py:26
  92.7 1.5 copy-start.7
  98.9 1.9 %collective-permute-start.23 = (f32[128,896]{1,0:T(8,128)S(1)}, f32[128,896]{1,0:T(8,128)S(1)}, u32[]{:S(2)}, u32[]{:S(2)}) collective-permute-start(f32[128,896]{1,0:T(8,128)S(1)} %get-tuple-element.71.m0), channel_id=1, source_target_pairs={{0,32},{1,33},{2,34},{3,35},{4,36},{5,37},{6,38},{7,39},{8,40},{9,... | collective-permute-start | bytes 1376264 | tf_op jit(solution)/shard_map/ppermute | solution.py:26
  99.0 2.5 %collective-permute-start.24 = (f32[128,896]{1,0:T(8,128)S(1)}, f32[128,896]{1,0:T(8,128)S(1)}, u32[]{:S(2)}, u32[]{:S(2)}) collective-permute-start(f32[128,896]{1,0:T(8,128)S(1)} %get-tuple-element.72.m1), channel_id=1, source_target_pairs={{0,32},{1,33},{2,34},{3,35},{4,36},{5,37},{6,38},{7,39},{8,40},{9,... | collective-permute-start | bytes 1376264 | tf_op jit(solution)/shard_map/ppermute | solution.py:26
  99.5 2.6 %collective-permute-start.25 = (f32[128,896]{1,0:T(8,128)S(1)}, f32[128,896]{1,0:T(8,128)S(1)}, u32[]{:S(2)}, u32[]{:S(2)}) collective-permute-start(f32[128,896]{1,0:T(8,128)S(1)} %get-tuple-element.73.m2), channel_id=1, source_target_pairs={{0,32},{1,33},{2,34},{3,35},{4,36},{5,37},{6,38},{7,39},{8,40},{9,... | collective-permute-start | bytes 1376264 | tf_op jit(solution)/shard_map/ppermute | solution.py:26
  110.6 1.6 copy-start.8
  112.1 16.6 %collective-permute-start.26 = (bf16[2,528,256]{2,1,0:T(8,128)(2,1)}, bf16[2,528,256]{2,1,0:T(8,128)(2,1)S(1)}, u32[]{:S(2)}, u32[]{:S(2)}) collective-permute-start(bf16[2,528,256]{2,1,0:T(8,128)(2,1)} %get-tuple-element.79), channel_id=1, source_target_pairs={{0,1},{1,2},{2,3},{3,0},{4,5},{5,6},{6,7},{7,4},{8,9},{9,10},{10,1... | collective-permute-start | bytes 1622024 | tf_op jit(solution)/shard_map/ppermute | solution.py:26
  112.5 16.2 %collective-permute-start.27 = (bf16[2,528,256]{2,1,0:T(8,128)(2,1)S(1)}, bf16[2,528,256]{2,1,0:T(8,128)(2,1)S(1)}, u32[]{:S(2)}, u32[]{:S(2)}) collective-permute-start(bf16[2,528,256]{2,1,0:T(8,128)(2,1)S(1)} %get-tuple-element.80), channel_id=1, source_target_pairs={{0,2},{1,3},{2,0},{3,1},{4,6},{5,7},{6,4},{7,5},{8,10},{9,11},{10,... | collective-permute-start | bytes 1622024 | tf_op jit(solution)/shard_map/ppermute | solution.py:26
  115.2 14.1 %collective-permute-start.28 = (bf16[2,528,256]{2,1,0:T(8,128)(2,1)S(1)}, bf16[2,528,256]{2,1,0:T(8,128)(2,1)S(1)}, u32[]{:S(2)}, u32[]{:S(2)}) collective-permute-start(bf16[2,528,256]{2,1,0:T(8,128)(2,1)S(1)} %get-tuple-element.81), channel_id=1, source_target_pairs={{0,3},{1,0},{2,1},{3,2},{4,7},{5,4},{6,5},{7,6},{8,11},{9,8},{10,9... | collective-permute-start | bytes 1622024 | tf_op jit(solution)/shard_map/ppermute | solution.py:26
  131.9 13.0 %collective-permute-start.29 = (bf16[2,144,256]{2,1,0:T(8,128)(2,1)S(1)}, bf16[2,144,256]{2,1,0:T(8,128)(2,1)S(1)}, u32[]{:S(2)}, u32[]{:S(2)}) collective-permute-start(bf16[2,144,256]{2,1,0:T(8,128)(2,1)S(1)} %get-tuple-element.83), channel_id=1, source_target_pairs={{0,4},{1,5},{2,6},{3,7},{4,8},{5,9},{6,10},{7,11},{8,12},{9,13},{1... | collective-permute-start | bytes 442376 | tf_op jit(solution)/shard_map/ppermute | solution.py:26
  132.0 12.9 %collective-permute-start.30 = (bf16[2,144,256]{2,1,0:T(8,128)(2,1)S(1)}, bf16[2,144,256]{2,1,0:T(8,128)(2,1)S(1)}, u32[]{:S(2)}, u32[]{:S(2)}) collective-permute-start(bf16[2,144,256]{2,1,0:T(8,128)(2,1)S(1)} %get-tuple-element.84), channel_id=1, source_target_pairs={{0,8},{1,9},{2,10},{3,11},{4,12},{5,13},{6,14},{7,15},{8,0},{9,1},... | collective-permute-start | bytes 442376 | tf_op jit(solution)/shard_map/ppermute | solution.py:26
  137.1 7.7 %collective-permute-start.31 = (bf16[2,144,256]{2,1,0:T(8,128)(2,1)S(1)}, bf16[2,144,256]{2,1,0:T(8,128)(2,1)S(1)}, u32[]{:S(2)}, u32[]{:S(2)}) collective-permute-start(bf16[2,144,256]{2,1,0:T(8,128)(2,1)S(1)} %get-tuple-element.85), channel_id=1, source_target_pairs={{0,12},{1,13},{2,14},{3,15},{4,0},{5,1},{6,2},{7,3},{8,4},{9,5},{1... | collective-permute-start | bytes 442376 | tf_op jit(solution)/shard_map/ppermute | solution.py:26
  145.8 11.2 %collective-permute-start.32 = (bf16[2,80,256]{2,1,0:T(8,128)(2,1)S(1)}, bf16[2,80,256]{2,1,0:T(8,128)(2,1)S(1)}, u32[]{:S(2)}, u32[]{:S(2)}) collective-permute-start(bf16[2,80,256]{2,1,0:T(8,128)(2,1)S(1)} %get-tuple-element.87), channel_id=1, source_target_pairs={{0,16},{1,17},{2,18},{3,19},{4,20},{5,21},{6,22},{7,23},{8,24},{9,... | collective-permute-start | bytes 245768 | tf_op jit(solution)/shard_map/ppermute | solution.py:26

commit v3 on v2

--- a/solution.py
+++ b/solution.py
@@ -9,7 +9,7 @@
 
 COST = 20
 F32, BF16 = jnp.float32, jnp.bfloat16
-SMALL, LARGE, WHOLE = 16 * 1024 * 1024, 40 * 1024 * 1024, 60 * 1024 * 1024
+SMALL, DELTA, WHOLE = 16 * 1024 * 1024, 40 * 1024 * 1024, 60 * 1024 * 1024
 BOTH = ("dp", "mp")
 
 
@@ -282,7 +282,7 @@
     return _call(
         functools.partial(_grad_in_body, width, len(before)),
         (shape((2 * tokens, three), BF16), shape((n, 512, tokens), F32), code, code, code, TICK),
-        LARGE,
+        DELTA,
         in_specs=[SMEM] + [VMEM] * (8 + len(before)),
         out_specs=(ANY,) + (VMEM,) * 5,
         scratch_shapes=[
@@ -305,30 +305,47 @@
     return jnp.concatenate([part, part], axis=1)
 
 
-def _grad_up_body(x, d0, d1, out):
+def _grad_up_body(steps, x, d0, d1, gate, up, tick):
+    tick[...] = jnp.zeros_like(tick)
     rows = x[...]
     total = jnp.dot(_twice(rows, 0), d0[...], preferred_element_type=F32)
     total = total + jnp.dot(_twice(rows, 1), d1[...], preferred_element_type=F32)
-    out[...] = total.astype(BF16)
-
-
-def grad_weight(part, pairs, place, width):
+    first = pl.program_id(0) < steps
+
+    @pl.when(first)
+    def _():
+        gate[...] = total.astype(BF16)
+
+    @pl.when(jnp.logical_not(first))
+    def _():
+        up[...] = total.astype(BF16)
+
+
+def grad_weights(part, pairs, width):
     depth, tokens = part.shape
-    delta = pl.BlockSpec((tokens, width), lambda i: (0, place))
-    return _call(
-        _grad_up_body,
-        shape((depth, width), BF16),
+    steps = depth // 512
+    delta = pl.BlockSpec((tokens, width), lambda i: (0, 1 + i // steps))
+    out = shape((depth, width), BF16)
+    return _call(
+        functools.partial(_grad_up_body, steps),
+        (out, out, TICK),
         WHOLE,
-        grid=(depth // 512,),
-        in_specs=[pl.BlockSpec((512, tokens), lambda i: (i, 0))] + [delta] * 2,
-        out_specs=pl.BlockSpec((512, width), lambda i: (i, 0)),
+        grid=(2 * steps,),
+        in_specs=[pl.BlockSpec((512, tokens), lambda i: (lax.rem(i, steps), 0))] + [delta] * 2,
+        out_specs=(
+            pl.BlockSpec((512, width), lambda i: (jnp.minimum(i, steps - 1), 0)),
+            pl.BlockSpec((512, width), lambda i: (jnp.maximum(i - steps, 0), 0)),
+            _whole(8, 128),
+        ),
         cost_estimate=_cost(
-            flops=COST * 4 * tokens * depth * width, bytes_accessed=COST * 4 * depth * width, transcendentals=0
+            flops=COST * 8 * tokens * depth * width, bytes_accessed=COST * 8 * depth * width, transcendentals=0
         ),
     )(part, *pairs)
 
 
-def _grad_down_body(g, h0, h1, out, turned):
+def _grad_down_body(g, h0, h1, out, tick, turned):
+    tick[...] = jnp.zeros_like(tick)
+
     @pl.when(pl.program_id(0) == 0)
     def _():
         for i, h in enumerate((h0, h1)):
@@ -345,11 +362,11 @@
     hidden = pl.BlockSpec((tokens, width), lambda i: (0, 0))
     return _call(
         _grad_down_body,
-        shape((width, depth), BF16),
+        (shape((width, depth), BF16), TICK),
         WHOLE,
         grid=(depth // 512,),
         in_specs=[pl.BlockSpec((512, tokens), lambda i: (i, 0))] + [hidden] * 2,
-        out_specs=pl.BlockSpec((width, 512), lambda i: (0, i)),
+        out_specs=(pl.BlockSpec((width, 512), lambda i: (0, i)), _whole(8, 128)),
         scratch_shapes=[pltpu.VMEM((2, width, tokens), BF16)],
         cost_estimate=_cost(
             flops=COST * 4 * tokens * depth * width, bytes_accessed=COST * 4 * depth * width, transcendentals=0
@@ -357,7 +374,7 @@
     )(part, *pairs)
 
 
-def _sum_first_body(ids, own, r1, r2, r3, own2, c1, c2, c3, tops):
+def _sum_first_body(ids, own, r1, r2, r3, _, own2, c1, c2, c3, tops):
     s2 = ids[3]
     for c in range(2):
         scales = [r[c, 512:528, :].astype(F32) for r in (r1, r2, r3)]
@@ -386,19 +403,19 @@
             out[c, 128:144, :] = jnp.concatenate([tops[n], tops[n]], axis=0).astype(BF16)
 
 
-def sum_first(ids, own, received):
+def sum_first(ids, own, received, after):
     tokens = own.shape[2]
     code = shape((2, 144, tokens), BF16)
     return _call(
         _sum_first_body,
         (shape((2, 128, tokens), F32), code, code, code),
-        in_specs=[SMEM] + [VMEM] * 4,
+        in_specs=[SMEM] + [VMEM] * 4 + [ANY],
         out_specs=(VMEM,) * 4,
         scratch_shapes=[pltpu.VMEM((4, 8, tokens), F32)],
-    )(ids, own, *received)
-
-
-def _sum_second_body(ids, own, r1, r2, r3, own3, out):
+    )(ids, own, *received, after)
+
+
+def _sum_second_body(ids, own, r1, r2, r3, _, own3, out):
     for c in range(2):
         scales = [r[c, 128:144, :].astype(F32) for r in (r1, r2, r3)]
         for y in range(2):
@@ -418,14 +435,14 @@
                 out[c, 64:80, :] = jnp.broadcast_to(top, (16, top.shape[1])).astype(BF16)
 
 
-def sum_second(ids, own, received):
+def sum_second(ids, own, received, after):
     tokens = own.shape[2]
     return _call(
         _sum_second_body,
         (shape((2, 64, tokens), F32), shape((2, 80, tokens), BF16)),
-        in_specs=[SMEM] + [VMEM] * 4,
+        in_specs=[SMEM] + [VMEM] * 4 + [ANY],
         out_specs=(VMEM,) * 2,
-    )(ids, own, *received)
+    )(ids, own, *received, after)
 
 
 def _sum_last_body(own, r, out):
@@ -472,12 +489,11 @@
         delta, *part, tick = grad_in(ids, gate_weight, up_weight, act, others, part)
         pairs.append(delta)
     own, *rest = part
-    own, *rest = sum_first(ids, own, [_send(v, _first(k + 1)) for k, v in enumerate(rest)])
-    own, last = sum_second(ids, own, [_send(v, _second(k + 1)) for k, v in enumerate(rest)])
+    grad_gate, grad_up, tick = grad_weights(x_acts, pairs, width)
+    own, *rest = sum_first(ids, own, [_send(v, _first(k + 1)) for k, v in enumerate(rest)], tick)
+    grad_down, tick = grad_down_weight(g_acts, pairs, width)
+    own, last = sum_second(ids, own, [_send(v, _second(k + 1)) for k, v in enumerate(rest)], tick)
     grad_inputs = sum_last(own, _send(last, _over_y)).T
-    grad_gate = grad_weight(x_acts, pairs, 1, width)
-    grad_up = grad_weight(x_acts, pairs, 2, width)
-    grad_down = grad_down_weight(g_acts, pairs, width)
     return (grad_inputs, grad_gate, grad_up, grad_down)
 
 

time: 158 us -> 157 us (level)
  waiting for transfers between devices: 44.4 us -> 41.1 us
    ppermute x33, waiting for transfers between devices: 44.4 us -> 41.1 us  [_send(): return lax.ppermute(a, BOTH, _moves(shift))]
    unnamed x30 -> x34, local copies, waits for them, and re-layouts: 5.92 us -> 7.34 us
    pallas_call x3 -> x2, Pallas kernels: 23.4 us -> 22.5 us  [the longest x1 14.5 us: grad_weights(): _call(functools.partial(_grad_up_body, steps), (out, out, TICK), WHOLE, g...]
  transfers between devices with their start and end apart: 33 -> 33, of which waited for: 17 -> 15; matrix products, arithmetic and copies ran while one was open for 0% -> 1% of each run, Pallas kernels for 33% -> 32%
where the time goes in v3:
time: 157 us
  Pallas kernels  64.4 us (41%)
  waiting for transfers between devices  41.1 us (26%)
  starting transfers between devices  40.9 us (26%)
  local copies, waits for them, and re-layouts  7.4 us (5%)
  other arithmetic  1.74 us (1%)
    ppermute x33, waiting for transfers between devices, _send(): return lax.ppermute(a, BOTH, _moves(shift))  41.1 us
    ppermute x33, starting transfers between devices, _send(): return lax.ppermute(a, BOTH, _moves(shift))  40.9 us
    pallas_call x2, Pallas kernels, forward(): _call(functools.partial(_forward_body, n, width), (mine,) * 2 + (other,)...  18.2 us
    pallas_call x2, Pallas kernels, grad_in(): _call(functools.partial(_grad_in_body, width, len(before)), (shape((2 * t...  14.6 us
    pallas_call x1, Pallas kernels, grad_weights(): _call(functools.partial(_grad_up_body, steps), (out, out, TICK), WHOLE, g...  14.5 us
    pallas_call x1, Pallas kernels, grad_down_weight(): _call(_grad_down_body, (shape((width, depth), BF16), TICK), WHOLE, grid=(...  7.96 us
    unnamed x34, local copies, waits for them, and re-layouts  7.34 us
  transfers between devices with their start and end apart: 33, of which 15 were waited for; matrix products, arithmetic and copies ran while one was open for 1% of the time, Pallas kernels for 32%

profile of v3, /device:TPU:0, one launch (start us, length us, event | category | flops | bytes accessed | tf_op | source)
XLA Modules:
  0.0 156.6 jit_solution(16039531187338180778)
XLA Ops:
  0.6 0.9 fusion.4
  1.5 3.4 %collective-permute-start = (bf16[2,64,512]{2,1,0:T(8,128)(2,1)S(1)}, bf16[2,64,512]{2,1,0:T(8,128)(2,1)S(1)}, u32[]{:S(2)}, u32[]{:S(2)}) collective-permute-start(bf16[2,64,512]{2,1,0:T(8,128)(2,1)S(1)} %get-tuple-element.111), channel_id=1, source_target_pairs={{0,16},{1,17},{2,18},{3,19},{4,20},{5,21},{6,22},{7,23},{8,24},{9,... | collective-permute-start | bytes 393224 | tf_op jit(solution)/shard_map/ppermute | solution.py:26
  4.9 3.5 %collective-permute-done = bf16[2,64,512]{2,1,0:T(8,128)(2,1)S(1)} collective-permute-done((bf16[2,64,512]{2,1,0:T(8,128)(2,1)S(1)}, bf16[2,64,512]{2,1,0:T(8,128)(2,1)S(1)}, u32[]{:S(2)}, u32[]{:S(2)}) %collective-permute-start) | collective-permute-done | bytes 131104 | tf_op jit(solution)/shard_map/ppermute | solution.py:26
  8.4 1.6 %collective-permute-start.3 = (bf16[2,2,64,512]{3,2,0,1:T(8,128)(2,1)S(1)}, bf16[2,2,64,512]{3,2,0,1:T(8,128)(2,1)S(1)}, u32[]{:S(2)}, u32[]{:S(2)}) collective-permute-start(bf16[2,2,64,512]{3,2,0,1:T(8,128)(2,1)S(1)} %pad_maximum_fusion.2), channel_id=1, source_target_pairs={{0,1},{1,2},{2,3},{3,0},{4,5},{5,6},{6,7},{7,4},{8,9},{9,10},{10,1... | collective-permute-start | bytes 786440 | tf_op jit(solution)/shard_map/ppermute | solution.py:26
  10.0 2.7 %collective-permute-start.2 = (bf16[2,2,64,512]{3,2,0,1:T(8,128)(2,1)S(1)}, bf16[2,2,64,512]{3,2,0,1:T(8,128)(2,1)S(1)}, u32[]{:S(2)}, u32[]{:S(2)}) collective-permute-start(bf16[2,2,64,512]{3,2,0,1:T(8,128)(2,1)S(1)} %pad_maximum_fusion.2), channel_id=1, source_target_pairs={{0,2},{1,3},{2,0},{3,1},{4,6},{5,7},{6,4},{7,5},{8,10},{9,11},{10,... | collective-permute-start | bytes 786440 | tf_op jit(solution)/shard_map/ppermute | solution.py:26
  12.7 1.4 collective-permute-start.1
  14.2 1.8 %collective-permute-done.3 = bf16[2,2,64,512]{3,2,0,1:T(8,128)(2,1)S(1)} collective-permute-done((bf16[2,2,64,512]{3,2,0,1:T(8,128)(2,1)S(1)}, bf16[2,2,64,512]{3,2,0,1:T(8,128)(2,1)S(1)}, u32[]{:S(2)}, u32[]{:S(2)}) %collective-permute-start.3) | collective-permute-done | bytes 262176 | tf_op jit(solution)/shard_map/ppermute | solution.py:26
  16.1 3.8 %collective-permute-done.2 = bf16[2,2,64,512]{3,2,0,1:T(8,128)(2,1)S(1)} collective-permute-done((bf16[2,2,64,512]{3,2,0,1:T(8,128)(2,1)S(1)}, bf16[2,2,64,512]{3,2,0,1:T(8,128)(2,1)S(1)}, u32[]{:S(2)}, u32[]{:S(2)}) %collective-permute-start.2) | collective-permute-done | bytes 262176 | tf_op jit(solution)/shard_map/ppermute | solution.py:26
  20.1 4.1 %collective-permute-start.4 = (bf16[4,2,64,512]{3,2,1,0:T(8,128)(2,1)S(1)}, bf16[4,2,64,512]{3,2,1,0:T(8,128)(2,1)S(1)}, u32[]{:S(2)}, u32[]{:S(2)}) collective-permute-start(bf16[4,2,64,512]{3,2,1,0:T(8,128)(2,1)S(1)} %pad_maximum_fusion.rest_0_), channel_id=1, source_target_pairs={{0,12},{1,13},{2,14},{3,15},{4,0},{5,1},{6,2},{7,3},{8,4},{9,5},{1... | collective-permute-start | bytes 1572872 | tf_op jit(solution)/shard_map/ppermute | solution.py:26
  24.4 6.5 %collective-permute-done.4.rest_1_ = bf16[4,2,64,512]{3,2,1,0:T(8,128)(2,1)S(1)} collective-permute-done((bf16[4,2,64,512]{3,2,1,0:T(8,128)(2,1)S(1)}, bf16[4,2,64,512]{3,2,1,0:T(8,128)(2,1)S(1)}, u32[]{:S(2)}, u32[]{:S(2)}) %collective-permute-start.4) | collective-permute-done | bytes 524320 | tf_op jit(solution)/shard_map/ppermute | solution.py:26
  30.9 3.7 %collective-permute-start.5 = (bf16[4,2,64,512]{3,2,1,0:T(8,128)(2,1)S(1)}, bf16[4,2,64,512]{3,2,1,0:T(8,128)(2,1)S(1)}, u32[]{:S(2)}, u32[]{:S(2)}) collective-permute-start(bf16[4,2,64,512]{3,2,1,0:T(8,128)(2,1)S(1)} %collective-permute-done.4.rest_1_), channel_id=1, source_target_pairs={{0,12},{1,13},{2,14},{3,15},{4,0},{5,1},{6,2},{7,3},{8,4},{9,5},{1... | collective-permute-start | bytes 1572872 | tf_op jit(solution)/shard_map/ppermute | solution.py:26
  34.7 1.9 %collective-permute-start.12 = (bf16[4,2,64,512]{3,2,1,0:T(8,128)(2,1)S(1)}, bf16[4,2,64,512]{3,2,1,0:T(8,128)(2,1)}, u32[]{:S(2)}, u32[]{:S(2)}) collective-permute-start(bf16[4,2,64,512]{3,2,1,0:T(8,128)(2,1)S(1)} %collective-permute-done.11.rest_3_), channel_id=1, source_target_pairs={{0,4},{1,5},{2,6},{3,7},{4,8},{5,9},{6,10},{7,11},{8,12},{9,13},{1... | collective-permute-start | bytes 1572872 | tf_op jit(solution)/shard_map/ppermute | solution.py:26
  37.2 3.1 %collective-permute-done.6.rest_3_ = bf16[4,2,64,512]{3,2,1,0:T(8,128)(2,1)S(1)} collective-permute-done((bf16[4,2,64,512]{3,2,1,0:T(8,128)(2,1)S(1)}, bf16[4,2,64,512]{3,2,1,0:T(8,128)(2,1)S(1)}, u32[]{:S(2)}, u32[]{:S(2)}) %collective-permute-start.6) | collective-permute-done | bytes 524320 | tf_op jit(solution)/shard_map/ppermute | solution.py:26
  40.3 0.9 collective-permute-done.5.rest_2_
  41.3 0.8 copy-done.16
  42.1 10.3 %shard_map.84 = (f32[128,1792]{1,0:T(8,128)}, f32[128,1792]{1,0:T(8,128)}, f32[128,896]{1,0:T(8,128)}, f32[128,896]{1,0:T(8,128)}, f32[128,896]{1,0:T(8,128)}, /...) custom-call(s32[4]{0:T(128)} %pad_add_fusion.ids, bf16[4,2,64,512]{3,2,1,0:T(8,128)(2,1)} %copy-done.12, ...), custom_call_target="tpu_custom_call" | custom-call | flops 187904816 | bytes 576716 | tf_op jit(solution)/shard_map/pallas_call | solution.py:141
  53.0 8.0 %shard_map.86 = (f32[128,896]{1,0:T(8,128)}, f32[128,896]{1,0:T(8,128)}, f32[128,896]{1,0:T(8,128)}, f32[128,896]{1,0:T(8,128)}, bf16[2048,512]{1,0:T(8,128)(2,1)}) custom-call(s32[4]{0:T(128)} %pad_add_fusion.ids, bf16[4,2,64,512]{3,2,1,0:T(8,128)(2,1)} %copy-done.11, bf16[4,2,64,512]{3,2,1,0:T(8,128)(2,1)} %collective-permute-done.10.rest_1_, ...), custom_call_target="tpu_custom_call" | custom-call | flops 93952408 | bytes 393216 | tf_op jit(solution)/shard_map/pallas_call | solution.py:141
  61.3 0.8 shard_map.88
  62.1 1.6 %collective-permute-start.17 = (bf16[128,1920]{1,0:T(8,128)(2,1)S(1)}, bf16[128,1920]{1,0:T(8,128)(2,1)S(1)}, u32[]{:S(2)}, u32[]{:S(2)}) collective-permute-start(bf16[128,1920]{1,0:T(8,128)(2,1)S(1)} %get-tuple-element.66), channel_id=1, source_target_pairs={{0,64},{1,65},{2,66},{3,67},{4,68},{5,69},{6,70},{7,71},{8,72},{9,... | collective-permute-start | bytes 1474568 | tf_op jit(solution)/shard_map/ppermute | solution.py:26
  64.2 1.0 copy-done.5
  65.8 0.8 collective-permute-start.19
  66.6 0.8 shard_map.85
  67.4 1.2 collective-permute-start.9
  68.6 1.0 copy-done.4
  70.1 11.7 %collective-permute-done.19.code_h = bf16[128,1024]{1,0:T(8,128)(2,1)S(1)} collective-permute-done((bf16[128,1024]{1,0:T(8,128)(2,1)S(1)}, bf16[128,1024]{1,0:T(8,128)(2,1)S(1)}, u32[]{:S(2)}, u32[]{:S(2)}) %collective-permute-start.19) | collective-permute-done | bytes 262176 | tf_op jit(solution)/shard_map/ppermute | solution.py:26
  81.8 1.2 shard_map.90
  83.7 1.6 %collective-permute-start.14 = (bf16[128,1024]{1,0:T(8,128)(2,1)S(1)}, bf16[128,1024]{1,0:T(8,128)(2,1)S(1)}, u32[]{:S(2)}, u32[]{:S(2)}) collective-permute-start(bf16[128,1024]{1,0:T(8,128)(2,1)S(1)} %get-tuple-element.61), channel_id=1, source_target_pairs={{0,64},{1,65},{2,66},{3,67},{4,68},{5,69},{6,70},{7,71},{8,72},{9,... | collective-permute-start | bytes 786440 | tf_op jit(solution)/shard_map/ppermute | solution.py:26
  86.2 6.1 %shard_map.91 = (bf16[512,2688]{1,0:T(8,128)(2,1)S(1)}, f32[1,512,256]{2,1,0:T(8,128)S(1)}, bf16[1,528,256]{2,1,0:T(8,128)(2,1)S(1)}, bf16[1,528,256]{2,1,0:T(8,...) custom-call(s32[4]{0:T(128)S(1)} %copy-done.6, bf16[2048,896]{1,0:T(8,128)(2,1)S(1)} %copy-done, ...), custom_call_target="tpu_custom_call" | custom-call | flops 187904816 | bytes 917504 | tf_op jit(solution)/shard_map/pallas_call | solution.py:282
  92.3 1.5 copy-done.9
  93.8 3.5 %collective-permute-done.14.code_h = bf16[128,1024]{1,0:T(8,128)(2,1)S(1)} collective-permute-done((bf16[128,1024]{1,0:T(8,128)(2,1)S(1)}, bf16[128,1024]{1,0:T(8,128)(2,1)S(1)}, u32[]{:S(2)}, u32[]{:S(2)}) %collective-permute-start.14) | collective-permute-done | bytes 262176 | tf_op jit(solution)/shard_map/ppermute | solution.py:26
  97.3 1.2 shard_map.92
  99.2 1.2 collective-permute-done.23.o0
  100.4 0.7 collective-permute-done.24.o1
  101.7 8.5 %shard_map.93 = (bf16[512,2688]{1,0:T(8,128)(2,1)S(1)}, f32[2,512,256]{2,1,0:T(8,128)S(1)}, bf16[2,528,256]{2,1,0:T(8,128)(2,1)}, bf16[2,528,256]{2,1,0:T(8,128)...) custom-call(s32[4]{0:T(128)S(1)} %copy-done.6, bf16[2048,896]{1,0:T(8,128)(2,1)S(1)} %copy-done, ...), custom_call_target="tpu_custom_call" | custom-call | flops 187904816 | bytes 917504 | tf_op jit(solution)/shard_map/pallas_call | solution.py:282
  110.2 1.6 %copy-done.10 = bf16[512,2688]{1,0:T(8,128)(2,1)} copy-done((bf16[512,2688]{1,0:T(8,128)(2,1)}, bf16[512,2688]{1,0:T(8,128)(2,1)S(1)}, u32[]{:S(2)}) %copy-start.10) | copy-done | bytes 2752536
  111.8 2.1 %collective-permute-start.26 = (bf16[2,528,256]{2,1,0:T(8,128)(2,1)}, bf16[2,528,256]{2,1,0:T(8,128)(2,1)S(1)}, u32[]{:S(2)}, u32[]{:S(2)}) collective-permute-start(bf16[2,528,256]{2,1,0:T(8,128)(2,1)} %get-tuple-element.84), channel_id=1, source_target_pairs={{0,1},{1,2},{2,3},{3,0},{4,5},{5,6},{6,7},{7,4},{8,9},{9,10},{10,1... | collective-permute-start | bytes 1622024 | tf_op jit(solution)/shard_map/ppermute | solution.py:26
  113.9 1.9 %collective-permute-start.27 = (bf16[2,528,256]{2,1,0:T(8,128)(2,1)S(1)}, bf16[2,528,256]{2,1,0:T(8,128)(2,1)S(1)}, u32[]{:S(2)}, u32[]{:S(2)}) collective-permute-start(bf16[2,528,256]{2,1,0:T(8,128)(2,1)S(1)} %get-tuple-element.85), channel_id=1, source_target_pairs={{0,2},{1,3},{2,0},{3,1},{4,6},{5,7},{6,4},{7,5},{8,10},{9,11},{10,... | collective-permute-start | bytes 1622024 | tf_op jit(solution)/shard_map/ppermute | solution.py:26
  115.8 1.6 collective-permute-start.28
  117.3 14.5 %shard_map.94 = (bf16[2048,896]{1,0:T(8,128)(2,1)}, bf16[2048,896]{1,0:T(8,128)(2,1)}, f32[8,128]{1,0:T(8,128)}) custom-call(bf16[2048,512]{1,0:T(8,128)(2,1)} %get-tuple-element.87.x, bf16[512,2688]{1,0:T(8,128)(2,1)} %copy-done.9, bf16[512,2688]{1,0:T(8,128)(2,1)} %copy-done.10), custom_call_target="tpu_custom_call" | custom-call | flops 7516192768 | bytes 14680064 | tf_op jit(solution)/shard_map/pallas_call | solution.py:329
  131.9 0.7 copy-done.7
  132.6 2.5 %shard_map.95 = (f32[2,128,256]{2,1,0:T(8,128)S(1)}, bf16[2,144,256]{2,1,0:T(8,128)(2,1)S(1)}, bf16[2,144,256]{2,1,0:T(8,128)(2,1)S(1)}, bf16[2,144,256]{2,1,0:T(8,128)(2,1)S(1)}) custom-call(s32[4]{0:T(128)S(1)} %copy-done.6, f32[2,512,256]{2,1,0:T(8,128)S(1)} %get-tuple-element.83.own, bf16[2,528,256]{2,1,0:T(8,128)(2,1)S(1)} %collective-permute-done.26.r1, ...), custom_call_target="tpu_custom_call" | custom-call | tf_op jit(solution)/shard_map/pallas_call | solution.py:409
  135.1 5.1 %collective-permute-start.30 = (bf16[2,144,256]{2,1,0:T(8,128)(2,1)S(1)}, bf16[2,144,256]{2,1,0:T(8,128)(2,1)S(1)}, u32[]{:S(2)}, u32[]{:S(2)}) collective-permute-start(bf16[2,144,256]{2,1,0:T(8,128)(2,1)S(1)} %get-tuple-element.93), channel_id=1, source_target_pairs={{0,8},{1,9},{2,10},{3,11},{4,12},{5,13},{6,14},{7,15},{8,0},{9,1},... | collective-permute-start | bytes 442376 | tf_op jit(solution)/shard_map/ppermute | solution.py:26
  140.3 8.0 %shard_map.96 = (bf16[896,2048]{1,0:T(8,128)(2,1)}, f32[8,128]{1,0:T(8,128)}) custom-call(bf16[2048,512]{1,0:T(8,128)(2,1)} %get-tuple-element.95.g, bf16[512,2688]{1,0:T(8,128)(2,1)} %copy-done.9, bf16[512,2688]{1,0:T(8,128)(2,1)} %copy-done.10), custom_call_target="tpu_custom_call" | custom-call | flops 3758096384 | bytes 7340032 | tf_op jit(solution)/shard_map/pallas_call | solution.py:363
  148.3 0.7 copy-done.8
  149.0 0.9 shard_map.97
  149.9 3.3 %collective-permute-start.32 = (bf16[2,80,256]{2,1,0:T(8,128)(2,1)S(1)}, bf16[2,80,256]{2,1,0:T(8,128)(2,1)S(1)}, u32[]{:S(2)}, u32[]{:S(2)}) collective-permute-start(bf16[2,80,256]{2,1,0:T(8,128)(2,1)S(1)} %get-tuple-element.98), channel_id=1, source_target_pairs={{0,16},{1,17},{2,18},{3,19},{4,20},{5,21},{6,22},{7,23},{8,24},{9,... | collective-permute-start | bytes 245768 | tf_op jit(solution)/shard_map/ppermute | solution.py:26
  153.2 2.7 %collective-permute-done.32.r = bf16[2,80,256]{2,1,0:T(8,128)(2,1)S(1)} collective-permute-done((bf16[2,80,256]{2,1,0:T(8,128)(2,1)S(1)}, bf16[2,80,256]{2,1,0:T(8,128)(2,1)S(1)}, u32[]{:S(2)}, u32[]{:S(2)}) %collective-permute-start.32) | collective-permute-done | bytes 81952 | tf_op jit(solution)/shard_map/ppermute | solution.py:26
  155.9 0.7 shard_map.98
  (76 shorter events, 6.8 us)
Async XLA Ops:
  1.5 6.9 %collective-permute-start = (bf16[2,64,512]{2,1,0:T(8,128)(2,1)S(1)}, bf16[2,64,512]{2,1,0:T(8,128)(2,1)S(1)}, u32[]{:S(2)}, u32[]{:S(2)}) collective-permute-start(bf16[2,64,512]{2,1,0:T(8,128)(2,1)S(1)} %get-tuple-element.111), channel_id=1, source_target_pairs={{0,16},{1,17},{2,18},{3,19},{4,20},{5,21},{6,22},{7,23},{8,24},{9,... | collective-permute-start | bytes 393224 | tf_op jit(solution)/shard_map/ppermute | solution.py:26
  8.4 7.7 %collective-permute-start.3 = (bf16[2,2,64,512]{3,2,0,1:T(8,128)(2,1)S(1)}, bf16[2,2,64,512]{3,2,0,1:T(8,128)(2,1)S(1)}, u32[]{:S(2)}, u32[]{:S(2)}) collective-permute-start(bf16[2,2,64,512]{3,2,0,1:T(8,128)(2,1)S(1)} %pad_maximum_fusion.2), channel_id=1, source_target_pairs={{0,1},{1,2},{2,3},{3,0},{4,5},{5,6},{6,7},{7,4},{8,9},{9,10},{10,1... | collective-permute-start | bytes 786440 | tf_op jit(solution)/shard_map/ppermute | solution.py:26
  10.0 9.9 %collective-permute-start.2 = (bf16[2,2,64,512]{3,2,0,1:T(8,128)(2,1)S(1)}, bf16[2,2,64,512]{3,2,0,1:T(8,128)(2,1)S(1)}, u32[]{:S(2)}, u32[]{:S(2)}) collective-permute-start(bf16[2,2,64,512]{3,2,0,1:T(8,128)(2,1)S(1)} %pad_maximum_fusion.2), channel_id=1, source_target_pairs={{0,2},{1,3},{2,0},{3,1},{4,6},{5,7},{6,4},{7,5},{8,10},{9,11},{10,... | collective-permute-start | bytes 786440 | tf_op jit(solution)/shard_map/ppermute | solution.py:26
  12.7 7.2 %collective-permute-start.1 = (bf16[2,2,64,512]{3,2,0,1:T(8,128)(2,1)S(1)}, bf16[2,2,64,512]{3,2,0,1:T(8,128)(2,1)S(1)}, u32[]{:S(2)}, u32[]{:S(2)}) collective-permute-start(bf16[2,2,64,512]{3,2,0,1:T(8,128)(2,1)S(1)} %pad_maximum_fusion.2), channel_id=1, source_target_pairs={{0,3},{1,0},{2,1},{3,2},{4,7},{5,4},{6,5},{7,6},{8,11},{9,8},{10,9... | collective-permute-start | bytes 786440 | tf_op jit(solution)/shard_map/ppermute | solution.py:26
  20.0 21.2 %copy-start.12 = (bf16[4,2,64,512]{3,2,1,0:T(8,128)(2,1)}, bf16[4,2,64,512]{3,2,1,0:T(8,128)(2,1)S(1)}, u32[]{:S(2)}) copy-start(bf16[4,2,64,512]{3,2,1,0:T(8,128)(2,1)S(1)} %pad_maximum_fusion.rest_0_) | copy-start | bytes 1572868
  20.1 10.8 %collective-permute-start.4 = (bf16[4,2,64,512]{3,2,1,0:T(8,128)(2,1)S(1)}, bf16[4,2,64,512]{3,2,1,0:T(8,128)(2,1)S(1)}, u32[]{:S(2)}, u32[]{:S(2)}) collective-permute-start(bf16[4,2,64,512]{3,2,1,0:T(8,128)(2,1)S(1)} %pad_maximum_fusion.rest_0_), channel_id=1, source_target_pairs={{0,12},{1,13},{2,14},{3,15},{4,0},{5,1},{6,2},{7,3},{8,4},{9,5},{1... | collective-permute-start | bytes 1572872 | tf_op jit(solution)/shard_map/ppermute | solution.py:26
  24.2 28.1 %copy-start.11 = (bf16[4,2,64,512]{3,2,1,0:T(8,128)(2,1)}, bf16[4,2,64,512]{3,2,1,0:T(8,128)(2,1)S(1)}, u32[]{:S(2)}) copy-start(bf16[4,2,64,512]{3,2,1,0:T(8,128)(2,1)S(1)} %pad_maximum_fusion.1.rest_0_) | copy-start | bytes 1572868
  24.2 10.5 %collective-permute-start.11 = (bf16[4,2,64,512]{3,2,1,0:T(8,128)(2,1)S(1)}, bf16[4,2,64,512]{3,2,1,0:T(8,128)(2,1)S(1)}, u32[]{:S(2)}, u32[]{:S(2)}) collective-permute-start(bf16[4,2,64,512]{3,2,1,0:T(8,128)(2,1)S(1)} %pad_maximum_fusion.1.rest_0_), channel_id=1, source_target_pairs={{0,4},{1,5},{2,6},{3,7},{4,8},{5,9},{6,10},{7,11},{8,12},{9,13},{1... | collective-permute-start | bytes 1572872 | tf_op jit(solution)/shard_map/ppermute | solution.py:26
  24.3 16.0 %collective-permute-start.6 = (bf16[4,2,64,512]{3,2,1,0:T(8,128)(2,1)S(1)}, bf16[4,2,64,512]{3,2,1,0:T(8,128)(2,1)S(1)}, u32[]{:S(2)}, u32[]{:S(2)}) collective-permute-start(bf16[4,2,64,512]{3,2,1,0:T(8,128)(2,1)S(1)} %pad_maximum_fusion.rest_0_), channel_id=1, source_target_pairs={{0,4},{1,5},{2,6},{3,7},{4,8},{5,9},{6,10},{7,11},{8,12},{9,13},{1... | collective-permute-start | bytes 1572872 | tf_op jit(solution)/shard_map/ppermute | solution.py:26
  30.9 10.4 %copy-start.14 = (bf16[4,2,64,512]{3,2,1,0:T(8,128)(2,1)}, bf16[4,2,64,512]{3,2,1,0:T(8,128)(2,1)S(1)}, u32[]{:S(2)}) copy-start(bf16[4,2,64,512]{3,2,1,0:T(8,128)(2,1)S(1)} %collective-permute-done.4.rest_1_) | copy-start | bytes 1572868
  30.9 10.4 %collective-permute-start.5 = (bf16[4,2,64,512]{3,2,1,0:T(8,128)(2,1)S(1)}, bf16[4,2,64,512]{3,2,1,0:T(8,128)(2,1)S(1)}, u32[]{:S(2)}, u32[]{:S(2)}) collective-permute-start(bf16[4,2,64,512]{3,2,1,0:T(8,128)(2,1)S(1)} %collective-permute-done.4.rest_1_), channel_id=1, source_target_pairs={{0,12},{1,13},{2,14},{3,15},{4,0},{5,1},{6,2},{7,3},{8,4},{9,5},{1... | collective-permute-start | bytes 1572872 | tf_op jit(solution)/shard_map/ppermute | solution.py:26
  34.6 18.4 %collective-permute-start.10 = (bf16[4,2,64,512]{3,2,1,0:T(8,128)(2,1)S(1)}, bf16[4,2,64,512]{3,2,1,0:T(8,128)(2,1)}, u32[]{:S(2)}, u32[]{:S(2)}) collective-permute-start(bf16[4,2,64,512]{3,2,1,0:T(8,128)(2,1)S(1)} %pad_maximum_fusion.1.rest_0_), channel_id=1, source_target_pairs={{0,12},{1,13},{2,14},{3,15},{4,0},{5,1},{6,2},{7,3},{8,4},{9,5},{1... | collective-permute-start | bytes 1572872 | tf_op jit(solution)/shard_map/ppermute | solution.py:26
  34.7 17.6 %copy-start.13 = (bf16[4,2,64,512]{3,2,1,0:T(8,128)(2,1)}, bf16[4,2,64,512]{3,2,1,0:T(8,128)(2,1)S(1)}, u32[]{:S(2)}) copy-start(bf16[4,2,64,512]{3,2,1,0:T(8,128)(2,1)S(1)} %collective-permute-done.11.rest_3_) | copy-start | bytes 1572868
  34.7 18.3 %collective-permute-start.12 = (bf16[4,2,64,512]{3,2,1,0:T(8,128)(2,1)S(1)}, bf16[4,2,64,512]{3,2,1,0:T(8,128)(2,1)}, u32[]{:S(2)}, u32[]{:S(2)}) collective-permute-start(bf16[4,2,64,512]{3,2,1,0:T(8,128)(2,1)S(1)} %collective-permute-done.11.rest_3_), channel_id=1, source_target_pairs={{0,4},{1,5},{2,6},{3,7},{4,8},{5,9},{6,10},{7,11},{8,12},{9,13},{1... | collective-permute-start | bytes 1572872 | tf_op jit(solution)/shard_map/ppermute | solution.py:26
  40.3 0.9 copy-start.15
  41.3 0.8 copy-start.16
  52.4 8.9 %copy-start.3 = (f32[128,1792]{1,0:T(8,128)S(1)}, f32[128,1792]{1,0:T(8,128)}, u32[]{:S(2)}) copy-start(f32[128,1792]{1,0:T(8,128)} %get-tuple-element.62.mine) | copy-start | bytes 2752516
  52.4 8.9 %collective-permute-start.15 = (f32[128,896]{1,0:T(8,128)}, f32[128,896]{1,0:T(8,128)S(1)}, u32[]{:S(2)}, u32[]{:S(2)}) collective-permute-start(f32[128,896]{1,0:T(8,128)} %get-tuple-element.63), channel_id=1, source_target_pairs={{0,32},{1,33},{2,34},{3,35},{4,36},{5,37},{6,38},{7,39},{8,40},{9,... | collective-permute-start | bytes 1376264 | tf_op jit(solution)/shard_map/ppermute | solution.py:26
  52.5 14.2 %copy-start.2 = (f32[128,1792]{1,0:T(8,128)S(1)}, f32[128,1792]{1,0:T(8,128)}, u32[]{:S(2)}) copy-start(f32[128,1792]{1,0:T(8,128)} %get-tuple-element.53.mine) | copy-start | bytes 2752516
  52.5 8.8 %collective-permute-start.16 = (f32[128,896]{1,0:T(8,128)}, f32[128,896]{1,0:T(8,128)S(1)}, u32[]{:S(2)}, u32[]{:S(2)}) collective-permute-start(f32[128,896]{1,0:T(8,128)} %get-tuple-element.64), channel_id=1, source_target_pairs={{0,32},{1,33},{2,34},{3,35},{4,36},{5,37},{6,38},{7,39},{8,40},{9,... | collective-permute-start | bytes 1376264 | tf_op jit(solution)/shard_map/ppermute | solution.py:26
  60.9 3.2 %collective-permute-start.18 = (f32[128,896]{1,0:T(8,128)}, f32[128,896]{1,0:T(8,128)S(1)}, u32[]{:S(2)}, u32[]{:S(2)}) collective-permute-start(f32[128,896]{1,0:T(8,128)} %get-tuple-element.68), channel_id=1, source_target_pairs={{0,32},{1,33},{2,34},{3,35},{4,36},{5,37},{6,38},{7,39},{8,40},{9,... | collective-permute-start | bytes 1376264 | tf_op jit(solution)/shard_map/ppermute | solution.py:26
  61.3 24.9 %copy-start.6 = (s32[4]{0:T(128)S(1)}, s32[4]{0:T(128)}, u32[]{:S(2)}) copy-start(s32[4]{0:T(128)} %pad_add_fusion.ids) | copy-start | bytes 52
  61.3 24.9 %copy-start = (bf16[2048,896]{1,0:T(8,128)(2,1)S(1)}, bf16[2048,896]{1,0:T(8,128)(2,1)}, u32[]{:S(2)}) copy-start(bf16[2048,896]{1,0:T(8,128)(2,1)} %wg.3) | copy-start | bytes 11010052
  61.3 24.9 %copy-start.1 = (bf16[2048,896]{1,0:T(8,128)(2,1)S(1)}, bf16[2048,896]{1,0:T(8,128)(2,1)}, u32[]{:S(2)}) copy-start(bf16[2048,896]{1,0:T(8,128)(2,1)} %wu.3) | copy-start | bytes 11010052
  62.1 19.7 %collective-permute-start.17 = (bf16[128,1920]{1,0:T(8,128)(2,1)S(1)}, bf16[128,1920]{1,0:T(8,128)(2,1)S(1)}, u32[]{:S(2)}, u32[]{:S(2)}) collective-permute-start(bf16[128,1920]{1,0:T(8,128)(2,1)S(1)} %get-tuple-element.66), channel_id=1, source_target_pairs={{0,64},{1,65},{2,66},{3,67},{4,68},{5,69},{6,70},{7,71},{8,72},{9,... | collective-permute-start | bytes 1474568 | tf_op jit(solution)/shard_map/ppermute | solution.py:26
  63.7 3.0 %collective-permute-start.7 = (f32[128,896]{1,0:T(8,128)}, f32[128,896]{1,0:T(8,128)S(1)}, u32[]{:S(2)}, u32[]{:S(2)}) collective-permute-start(f32[128,896]{1,0:T(8,128)} %get-tuple-element.54), channel_id=1, source_target_pairs={{0,32},{1,33},{2,34},{3,35},{4,36},{5,37},{6,38},{7,39},{8,40},{9,... | collective-permute-start | bytes 1376264 | tf_op jit(solution)/shard_map/ppermute | solution.py:26
  63.7 3.0 %collective-permute-start.8 = (f32[128,896]{1,0:T(8,128)}, f32[128,896]{1,0:T(8,128)S(1)}, u32[]{:S(2)}, u32[]{:S(2)}) collective-permute-start(f32[128,896]{1,0:T(8,128)} %get-tuple-element.55), channel_id=1, source_target_pairs={{0,32},{1,33},{2,34},{3,35},{4,36},{5,37},{6,38},{7,39},{8,40},{9,... | collective-permute-start | bytes 1376264 | tf_op jit(solution)/shard_map/ppermute | solution.py:26
  64.2 4.5 %collective-permute-start.13 = (f32[128,896]{1,0:T(8,128)}, f32[128,896]{1,0:T(8,128)S(1)}, u32[]{:S(2)}, u32[]{:S(2)}) collective-permute-start(f32[128,896]{1,0:T(8,128)} %get-tuple-element.59), channel_id=1, source_target_pairs={{0,32},{1,33},{2,34},{3,35},{4,36},{5,37},{6,38},{7,39},{8,40},{9,... | collective-permute-start | bytes 1376264 | tf_op jit(solution)/shard_map/ppermute | solution.py:26
  64.2 1.0 copy-start.5
  65.8 16.0 %collective-permute-start.19 = (bf16[128,1024]{1,0:T(8,128)(2,1)S(1)}, bf16[128,1024]{1,0:T(8,128)(2,1)S(1)}, u32[]{:S(2)}, u32[]{:S(2)}) collective-permute-start(bf16[128,1024]{1,0:T(8,128)(2,1)S(1)} %get-tuple-element.70), channel_id=1, source_target_pairs={{0,64},{1,65},{2,66},{3,67},{4,68},{5,69},{6,70},{7,71},{8,72},{9,... | collective-permute-start | bytes 786440 | tf_op jit(solution)/shard_map/ppermute | solution.py:26
  67.4 29.8 %collective-permute-start.9 = (bf16[128,1920]{1,0:T(8,128)(2,1)S(1)}, bf16[128,1920]{1,0:T(8,128)(2,1)S(1)}, u32[]{:S(2)}, u32[]{:S(2)}) collective-permute-start(bf16[128,1920]{1,0:T(8,128)(2,1)S(1)} %get-tuple-element.57), channel_id=1, source_target_pairs={{0,64},{1,65},{2,66},{3,67},{4,68},{5,69},{6,70},{7,71},{8,72},{9,... | collective-permute-start | bytes 1474568 | tf_op jit(solution)/shard_map/ppermute | solution.py:26
  68.6 1.0 copy-start.4
  83.0 2.3 %collective-permute-start.20 = (f32[128,896]{1,0:T(8,128)S(1)}, f32[128,896]{1,0:T(8,128)S(1)}, u32[]{:S(2)}, u32[]{:S(2)}) collective-permute-start(f32[128,896]{1,0:T(8,128)S(1)} %get-tuple-element.72.m0), channel_id=1, source_target_pairs={{0,32},{1,33},{2,34},{3,35},{4,36},{5,37},{6,38},{7,39},{8,40},{9,... | collective-permute-start | bytes 1376264 | tf_op jit(solution)/shard_map/ppermute | solution.py:26
  83.1 2.5 %collective-permute-start.21 = (f32[128,896]{1,0:T(8,128)S(1)}, f32[128,896]{1,0:T(8,128)S(1)}, u32[]{:S(2)}, u32[]{:S(2)}) collective-permute-start(f32[128,896]{1,0:T(8,128)S(1)} %get-tuple-element.73.m1), channel_id=1, source_target_pairs={{0,32},{1,33},{2,34},{3,35},{4,36},{5,37},{6,38},{7,39},{8,40},{9,... | collective-permute-start | bytes 1376264 | tf_op jit(solution)/shard_map/ppermute | solution.py:26
  83.6 2.6 %collective-permute-start.22 = (f32[128,896]{1,0:T(8,128)S(1)}, f32[128,896]{1,0:T(8,128)S(1)}, u32[]{:S(2)}, u32[]{:S(2)}) collective-permute-start(f32[128,896]{1,0:T(8,128)S(1)} %get-tuple-element.74.m2), channel_id=1, source_target_pairs={{0,32},{1,33},{2,34},{3,35},{4,36},{5,37},{6,38},{7,39},{8,40},{9,... | collective-permute-start | bytes 1376264 | tf_op jit(solution)/shard_map/ppermute | solution.py:26
  83.7 13.6 %collective-permute-start.14 = (bf16[128,1024]{1,0:T(8,128)(2,1)S(1)}, bf16[128,1024]{1,0:T(8,128)(2,1)S(1)}, u32[]{:S(2)}, u32[]{:S(2)}) collective-permute-start(bf16[128,1024]{1,0:T(8,128)(2,1)S(1)} %get-tuple-element.61), channel_id=1, source_target_pairs={{0,64},{1,65},{2,66},{3,67},{4,68},{5,69},{6,70},{7,71},{8,72},{9,... | collective-permute-start | bytes 786440 | tf_op jit(solution)/shard_map/ppermute | solution.py:26
  92.3 1.5 copy-start.9
  98.5 1.9 %collective-permute-start.23 = (f32[128,896]{1,0:T(8,128)S(1)}, f32[128,896]{1,0:T(8,128)S(1)}, u32[]{:S(2)}, u32[]{:S(2)}) collective-permute-start(f32[128,896]{1,0:T(8,128)S(1)} %get-tuple-element.76.m0), channel_id=1, source_target_pairs={{0,32},{1,33},{2,34},{3,35},{4,36},{5,37},{6,38},{7,39},{8,40},{9,... | collective-permute-start | bytes 1376264 | tf_op jit(solution)/shard_map/ppermute | solution.py:26
  98.6 2.5 %collective-permute-start.24 = (f32[128,896]{1,0:T(8,128)S(1)}, f32[128,896]{1,0:T(8,128)S(1)}, u32[]{:S(2)}, u32[]{:S(2)}) collective-permute-start(f32[128,896]{1,0:T(8,128)S(1)} %get-tuple-element.77.m1), channel_id=1, source_target_pairs={{0,32},{1,33},{2,34},{3,35},{4,36},{5,37},{6,38},{7,39},{8,40},{9,... | collective-permute-start | bytes 1376264 | tf_op jit(solution)/shard_map/ppermute | solution.py:26
  99.1 2.6 %collective-permute-start.25 = (f32[128,896]{1,0:T(8,128)S(1)}, f32[128,896]{1,0:T(8,128)S(1)}, u32[]{:S(2)}, u32[]{:S(2)}) collective-permute-start(f32[128,896]{1,0:T(8,128)S(1)} %get-tuple-element.78.m2), channel_id=1, source_target_pairs={{0,32},{1,33},{2,34},{3,35},{4,36},{5,37},{6,38},{7,39},{8,40},{9,... | collective-permute-start | bytes 1376264 | tf_op jit(solution)/shard_map/ppermute | solution.py:26
  110.2 1.6 %copy-start.10 = (bf16[512,2688]{1,0:T(8,128)(2,1)}, bf16[512,2688]{1,0:T(8,128)(2,1)S(1)}, u32[]{:S(2)}) copy-start(bf16[512,2688]{1,0:T(8,128)(2,1)S(1)} %get-tuple-element.89.d1.h1) | copy-start | bytes 8257540
  111.8 20.1 %collective-permute-start.26 = (bf16[2,528,256]{2,1,0:T(8,128)(2,1)}, bf16[2,528,256]{2,1,0:T(8,128)(2,1)S(1)}, u32[]{:S(2)}, u32[]{:S(2)}) collective-permute-start(bf16[2,528,256]{2,1,0:T(8,128)(2,1)} %get-tuple-element.84), channel_id=1, source_target_pairs={{0,1},{1,2},{2,3},{3,0},{4,5},{5,6},{6,7},{7,4},{8,9},{9,10},{10,1... | collective-permute-start | bytes 1622024 | tf_op jit(solution)/shard_map/ppermute | solution.py:26
  113.9 18.0 %collective-permute-start.27 = (bf16[2,528,256]{2,1,0:T(8,128)(2,1)S(1)}, bf16[2,528,256]{2,1,0:T(8,128)(2,1)S(1)}, u32[]{:S(2)}, u32[]{:S(2)}) collective-permute-start(bf16[2,528,256]{2,1,0:T(8,128)(2,1)S(1)} %get-tuple-element.85), channel_id=1, source_target_pairs={{0,2},{1,3},{2,0},{3,1},{4,6},{5,7},{6,4},{7,5},{8,10},{9,11},{10,... | collective-permute-start | bytes 1622024 | tf_op jit(solution)/shard_map/ppermute | solution.py:26
  115.8 16.1 %collective-permute-start.28 = (bf16[2,528,256]{2,1,0:T(8,128)(2,1)S(1)}, bf16[2,528,256]{2,1,0:T(8,128)(2,1)S(1)}, u32[]{:S(2)}, u32[]{:S(2)}) collective-permute-start(bf16[2,528,256]{2,1,0:T(8,128)(2,1)S(1)} %get-tuple-element.86), channel_id=1, source_target_pairs={{0,3},{1,0},{2,1},{3,2},{4,7},{5,4},{6,5},{7,6},{8,11},{9,8},{10,9... | collective-permute-start | bytes 1622024 | tf_op jit(solution)/shard_map/ppermute | solution.py:26
  135.1 13.2 %collective-permute-start.29 = (bf16[2,144,256]{2,1,0:T(8,128)(2,1)S(1)}, bf16[2,144,256]{2,1,0:T(8,128)(2,1)S(1)}, u32[]{:S(2)}, u32[]{:S(2)}) collective-permute-start(bf16[2,144,256]{2,1,0:T(8,128)(2,1)S(1)} %get-tuple-element.92), channel_id=1, source_target_pairs={{0,4},{1,5},{2,6},{3,7},{4,8},{5,9},{6,10},{7,11},{8,12},{9,13},{1... | collective-permute-start | bytes 442376 | tf_op jit(solution)/shard_map/ppermute | solution.py:26
  135.1 13.1 %collective-permute-start.30 = (bf16[2,144,256]{2,1,0:T(8,128)(2,1)S(1)}, bf16[2,144,256]{2,1,0:T(8,128)(2,1)S(1)}, u32[]{:S(2)}, u32[]{:S(2)}) collective-permute-start(bf16[2,144,256]{2,1,0:T(8,128)(2,1)S(1)} %get-tuple-element.93), channel_id=1, source_target_pairs={{0,8},{1,9},{2,10},{3,11},{4,12},{5,13},{6,14},{7,15},{8,0},{9,1},... | collective-permute-start | bytes 442376 | tf_op jit(solution)/shard_map/ppermute | solution.py:26
  140.3 8.0 %collective-permute-start.31 = (bf16[2,144,256]{2,1,0:T(8,128)(2,1)S(1)}, bf16[2,144,256]{2,1,0:T(8,128)(2,1)S(1)}, u32[]{:S(2)}, u32[]{:S(2)}) collective-permute-start(bf16[2,144,256]{2,1,0:T(8,128)(2,1)S(1)} %get-tuple-element.94), channel_id=1, source_target_pairs={{0,12},{1,13},{2,14},{3,15},{4,0},{5,1},{6,2},{7,3},{8,4},{9,5},{1... | collective-permute-start | bytes 442376 | tf_op jit(solution)/shard_map/ppermute | solution.py:26
  149.9 6.0 %collective-permute-start.32 = (bf16[2,80,256]{2,1,0:T(8,128)(2,1)S(1)}, bf16[2,80,256]{2,1,0:T(8,128)(2,1)S(1)}, u32[]{:S(2)}, u32[]{:S(2)}) collective-permute-start(bf16[2,80,256]{2,1,0:T(8,128)(2,1)S(1)} %get-tuple-element.98), channel_id=1, source_target_pairs={{0,16},{1,17},{2,18},{3,19},{4,20},{5,21},{6,22},{7,23},{8,24},{9,... | collective-permute-start | bytes 245768 | tf_op jit(solution)/shard_map/ppermute | solution.py:26
  (2 other events, 1.4 us)

commit v4 on v3

--- a/solution.py
+++ b/solution.py
@@ -228,7 +228,7 @@
 
 
 def _grad_in_body(width, n_before, ids, wg, wu, m0, m1, m2, o0, o1, o2, *rest):
-    before, (pair_out, own, c1, c2, c3, tick, pair, right, tops, blocks, codes, sem) = rest[:n_before], rest[n_before:]
+    before, (pair_out, own, c1, c2, c3, tick, pair, right, tops, blocks, codes, sem, moves) = rest[:n_before], rest[n_before:]
     core, s1 = ids[0], ids[2]
     half = m0.shape[0]
     tokens = 2 * half
@@ -245,8 +245,11 @@
             if i:
                 right[rows, (2 * i - 2) * width : (2 * i - 1) * width] = high
                 right[rows, (2 * i - 1) * width : 2 * i * width] = low
-    store = pltpu.make_async_copy(pair, pair_out, sem)
-    store.start()
+    store = [pltpu.make_async_copy(pair, pair_out, sem)]
+    for i, (out, earlier) in enumerate(zip((own, c1, c2, c3), before)):
+        store.append(pltpu.make_async_copy(earlier.at[0], out.at[0], moves.at[i]))
+    for copy in store:
+        copy.start()
     for part in range(4):
         some = slice(part * 512, (part + 1) * 512)
         g, u = wg[some, :], wu[some, :]
@@ -264,14 +267,13 @@
             tops[pl.ds(k, 1), pl.ds(j, 1), :] = scale[None]
             blocks[pl.ds(k, 1), rows, :] = block[None]
             codes[pl.ds(k, 1), rows, :] = code[None]
-    for out, earlier in zip((own, c1, c2, c3), before):
-        out[0] = earlier[0]
     c = own.shape[0] - 1
     own[c] = blocks[0]
     for n, out in ((1, c1), (2, c2), (3, c3)):
         out[c, 0:512, :] = codes[n]
         out[c, 512:528, :] = jnp.concatenate([tops[n], tops[n]], axis=0).astype(BF16)
-    store.wait()
+    for copy in store:
+        copy.wait()
 
 
 def grad_in(ids, wg, wu, mine, theirs, before):
@@ -292,6 +294,7 @@
             pltpu.VMEM((4, 512, tokens), F32),
             pltpu.VMEM((4, 512, tokens), BF16),
             pltpu.SemaphoreType.DMA,
+            pltpu.SemaphoreType.DMA((4,)),
         ],
         cost_estimate=_cost(
             flops=8 * tokens * 2048 * width, bytes_accessed=4 * 2048 * width + 16 * tokens * three, transcendentals=2048 * tokens
@@ -329,7 +332,7 @@
     return _call(
         functools.partial(_grad_up_body, steps),
         (out, out, TICK),
-        WHOLE,
+        DELTA,
         grid=(2 * steps,),
         in_specs=[pl.BlockSpec((512, tokens), lambda i: (lax.rem(i, steps), 0))] + [delta] * 2,
         out_specs=(
@@ -363,7 +366,7 @@
     return _call(
         _grad_down_body,
         (shape((width, depth), BF16), TICK),
-        WHOLE,
+        DELTA,
         grid=(depth // 512,),
         in_specs=[pl.BlockSpec((512, tokens), lambda i: (i, 0))] + [hidden] * 2,
         out_specs=(pl.BlockSpec((width, 512), lambda i: (0, i)), _whole(8, 128)),

time: 157 us -> 150 us (0.955)
  local copies, waits for them, and re-layouts: 7.4 us -> 2.93 us
  Pallas kernels: 64.4 us -> 61 us
    unnamed x34 -> x30, local copies, waits for them, and re-layouts: 7.34 us -> 2.88 us
    pallas_call x2, Pallas kernels: 22.5 us -> 18.9 us  [the longest x1 12.6 us: grad_weights(): _call(functools.partial(_grad_up_body, steps), (out, out, TICK), DELTA, g...]
  transfers between devices with their start and end apart: 33 -> 33, of which waited for: 15 -> 15; matrix products, arithmetic and copies ran while one was open for 1% -> 0% of each run, Pallas kernels for 32% -> 31%
where the time goes in v4:
time: 150 us
  Pallas kernels  61 us (41%)
  waiting for transfers between devices  42.6 us (28%)
  starting transfers between devices  41 us (27%)
  local copies, waits for them, and re-layouts  2.93 us (2%)
  other arithmetic  1.69 us (1%)
    ppermute x33, waiting for transfers between devices, _send(): return lax.ppermute(a, BOTH, _moves(shift))  42.6 us
    ppermute x33, starting transfers between devices, _send(): return lax.ppermute(a, BOTH, _moves(shift))  41 us
    pallas_call x2, Pallas kernels, forward(): _call(functools.partial(_forward_body, n, width), (mine,) * 2 + (other,)...  18.2 us
    pallas_call x2, Pallas kernels, grad_in(): _call(functools.partial(_grad_in_body, width, len(before)), (shape((2 * t...  14.6 us
    pallas_call x1, Pallas kernels, grad_weights(): _call(functools.partial(_grad_up_body, steps), (out, out, TICK), DELTA, g...  12.6 us
    pallas_call x1, Pallas kernels, grad_down_weight(): _call(_grad_down_body, (shape((width, depth), BF16), TICK), DELTA, grid=(...  6.25 us
  transfers between devices with their start and end apart: 33, of which 15 were waited for; matrix products, arithmetic and copies ran while one was open for 0% of the time, Pallas kernels for 31%

profile of v4, /device:TPU:0, one launch (start us, length us, event | category | flops | bytes accessed | tf_op | source)
XLA Modules:
  0.0 150.1 jit_solution(11670912345056125965)
XLA Ops:
  0.6 0.9 fusion.4
  1.5 3.4 %collective-permute-start = (bf16[2,64,512]{2,1,0:T(8,128)(2,1)S(1)}, bf16[2,64,512]{2,1,0:T(8,128)(2,1)S(1)}, u32[]{:S(2)}, u32[]{:S(2)}) collective-permute-start(bf16[2,64,512]{2,1,0:T(8,128)(2,1)S(1)} %get-tuple-element.111), channel_id=1, source_target_pairs={{0,16},{1,17},{2,18},{3,19},{4,20},{5,21},{6,22},{7,23},{8,24},{9,... | collective-permute-start | bytes 393224 | tf_op jit(solution)/shard_map/ppermute | solution.py:26
  4.9 3.5 %collective-permute-done = bf16[2,64,512]{2,1,0:T(8,128)(2,1)S(1)} collective-permute-done((bf16[2,64,512]{2,1,0:T(8,128)(2,1)S(1)}, bf16[2,64,512]{2,1,0:T(8,128)(2,1)S(1)}, u32[]{:S(2)}, u32[]{:S(2)}) %collective-permute-start) | collective-permute-done | bytes 131104 | tf_op jit(solution)/shard_map/ppermute | solution.py:26
  8.4 1.6 %collective-permute-start.3 = (bf16[2,2,64,512]{3,2,0,1:T(8,128)(2,1)S(1)}, bf16[2,2,64,512]{3,2,0,1:T(8,128)(2,1)S(1)}, u32[]{:S(2)}, u32[]{:S(2)}) collective-permute-start(bf16[2,2,64,512]{3,2,0,1:T(8,128)(2,1)S(1)} %pad_maximum_fusion.2), channel_id=1, source_target_pairs={{0,1},{1,2},{2,3},{3,0},{4,5},{5,6},{6,7},{7,4},{8,9},{9,10},{10,1... | collective-permute-start | bytes 786440 | tf_op jit(solution)/shard_map/ppermute | solution.py:26
  10.0 2.7 %collective-permute-start.2 = (bf16[2,2,64,512]{3,2,0,1:T(8,128)(2,1)S(1)}, bf16[2,2,64,512]{3,2,0,1:T(8,128)(2,1)S(1)}, u32[]{:S(2)}, u32[]{:S(2)}) collective-permute-start(bf16[2,2,64,512]{3,2,0,1:T(8,128)(2,1)S(1)} %pad_maximum_fusion.2), channel_id=1, source_target_pairs={{0,2},{1,3},{2,0},{3,1},{4,6},{5,7},{6,4},{7,5},{8,10},{9,11},{10,... | collective-permute-start | bytes 786440 | tf_op jit(solution)/shard_map/ppermute | solution.py:26
  12.7 1.4 collective-permute-start.1
  14.2 1.8 %collective-permute-done.3 = bf16[2,2,64,512]{3,2,0,1:T(8,128)(2,1)S(1)} collective-permute-done((bf16[2,2,64,512]{3,2,0,1:T(8,128)(2,1)S(1)}, bf16[2,2,64,512]{3,2,0,1:T(8,128)(2,1)S(1)}, u32[]{:S(2)}, u32[]{:S(2)}) %collective-permute-start.3) | collective-permute-done | bytes 262176 | tf_op jit(solution)/shard_map/ppermute | solution.py:26
  16.1 3.8 %collective-permute-done.2 = bf16[2,2,64,512]{3,2,0,1:T(8,128)(2,1)S(1)} collective-permute-done((bf16[2,2,64,512]{3,2,0,1:T(8,128)(2,1)S(1)}, bf16[2,2,64,512]{3,2,0,1:T(8,128)(2,1)S(1)}, u32[]{:S(2)}, u32[]{:S(2)}) %collective-permute-start.2) | collective-permute-done | bytes 262176 | tf_op jit(solution)/shard_map/ppermute | solution.py:26
  20.1 4.1 %collective-permute-start.4 = (bf16[4,2,64,512]{3,2,1,0:T(8,128)(2,1)S(1)}, bf16[4,2,64,512]{3,2,1,0:T(8,128)(2,1)S(1)}, u32[]{:S(2)}, u32[]{:S(2)}) collective-permute-start(bf16[4,2,64,512]{3,2,1,0:T(8,128)(2,1)S(1)} %pad_maximum_fusion.rest_0_), channel_id=1, source_target_pairs={{0,12},{1,13},{2,14},{3,15},{4,0},{5,1},{6,2},{7,3},{8,4},{9,5},{1... | collective-permute-start | bytes 1572872 | tf_op jit(solution)/shard_map/ppermute | solution.py:26
  24.4 6.5 %collective-permute-done.4.rest_1_ = bf16[4,2,64,512]{3,2,1,0:T(8,128)(2,1)S(1)} collective-permute-done((bf16[4,2,64,512]{3,2,1,0:T(8,128)(2,1)S(1)}, bf16[4,2,64,512]{3,2,1,0:T(8,128)(2,1)S(1)}, u32[]{:S(2)}, u32[]{:S(2)}) %collective-permute-start.4) | collective-permute-done | bytes 524320 | tf_op jit(solution)/shard_map/ppermute | solution.py:26
  30.9 3.7 %collective-permute-start.5 = (bf16[4,2,64,512]{3,2,1,0:T(8,128)(2,1)S(1)}, bf16[4,2,64,512]{3,2,1,0:T(8,128)(2,1)S(1)}, u32[]{:S(2)}, u32[]{:S(2)}) collective-permute-start(bf16[4,2,64,512]{3,2,1,0:T(8,128)(2,1)S(1)} %collective-permute-done.4.rest_1_), channel_id=1, source_target_pairs={{0,12},{1,13},{2,14},{3,15},{4,0},{5,1},{6,2},{7,3},{8,4},{9,5},{1... | collective-permute-start | bytes 1572872 | tf_op jit(solution)/shard_map/ppermute | solution.py:26
  34.7 1.9 %collective-permute-start.12 = (bf16[4,2,64,512]{3,2,1,0:T(8,128)(2,1)S(1)}, bf16[4,2,64,512]{3,2,1,0:T(8,128)(2,1)}, u32[]{:S(2)}, u32[]{:S(2)}) collective-permute-start(bf16[4,2,64,512]{3,2,1,0:T(8,128)(2,1)S(1)} %collective-permute-done.11.rest_3_), channel_id=1, source_target_pairs={{0,4},{1,5},{2,6},{3,7},{4,8},{5,9},{6,10},{7,11},{8,12},{9,13},{1... | collective-permute-start | bytes 1572872 | tf_op jit(solution)/shard_map/ppermute | solution.py:26
  36.6 0.6 pad_add_fusion.ids
  37.2 3.1 %collective-permute-done.6.rest_3_ = bf16[4,2,64,512]{3,2,1,0:T(8,128)(2,1)S(1)} collective-permute-done((bf16[4,2,64,512]{3,2,1,0:T(8,128)(2,1)S(1)}, bf16[4,2,64,512]{3,2,1,0:T(8,128)(2,1)S(1)}, u32[]{:S(2)}, u32[]{:S(2)}) %collective-permute-start.6) | collective-permute-done | bytes 524320 | tf_op jit(solution)/shard_map/ppermute | solution.py:26
  40.3 0.9 collective-permute-done.5.rest_2_
  41.3 0.8 copy-done.14
  42.0 10.3 %shard_map.84 = (f32[128,1792]{1,0:T(8,128)}, f32[128,1792]{1,0:T(8,128)}, f32[128,896]{1,0:T(8,128)}, f32[128,896]{1,0:T(8,128)}, f32[128,896]{1,0:T(8,128)}, /...) custom-call(s32[4]{0:T(128)} %pad_add_fusion.ids, bf16[4,2,64,512]{3,2,1,0:T(8,128)(2,1)} %copy-done.10, ...), custom_call_target="tpu_custom_call" | custom-call | flops 187904816 | bytes 576716 | tf_op jit(solution)/shard_map/pallas_call | solution.py:141
  53.0 7.9 %shard_map.86 = (f32[128,896]{1,0:T(8,128)}, f32[128,896]{1,0:T(8,128)}, f32[128,896]{1,0:T(8,128)}, f32[128,896]{1,0:T(8,128)}, bf16[2048,512]{1,0:T(8,128)(2,1)}) custom-call(s32[4]{0:T(128)} %pad_add_fusion.ids, bf16[4,2,64,512]{3,2,1,0:T(8,128)(2,1)} %copy-done.9, bf16[4,2,64,512]{3,2,1,0:T(8,128)(2,1)} %collective-permute-done.10.rest_1_, ...), custom_call_target="tpu_custom_call" | custom-call | flops 93952408 | bytes 393216 | tf_op jit(solution)/shard_map/pallas_call | solution.py:141
  61.3 0.8 shard_map.88
  62.1 1.6 %collective-permute-start.17 = (bf16[128,1920]{1,0:T(8,128)(2,1)S(1)}, bf16[128,1920]{1,0:T(8,128)(2,1)S(1)}, u32[]{:S(2)}, u32[]{:S(2)}) collective-permute-start(bf16[128,1920]{1,0:T(8,128)(2,1)S(1)} %get-tuple-element.66), channel_id=1, source_target_pairs={{0,64},{1,65},{2,66},{3,67},{4,68},{5,69},{6,70},{7,71},{8,72},{9,... | collective-permute-start | bytes 1474568 | tf_op jit(solution)/shard_map/ppermute | solution.py:26
  64.2 1.0 copy-done.5
  65.2 0.6 shard_map.89
  65.8 0.8 collective-permute-start.19
  66.6 0.8 shard_map.85
  67.4 1.2 collective-permute-start.9
  68.6 1.0 copy-done.4
  70.1 11.7 %collective-permute-done.19.code_h = bf16[128,1024]{1,0:T(8,128)(2,1)S(1)} collective-permute-done((bf16[128,1024]{1,0:T(8,128)(2,1)S(1)}, bf16[128,1024]{1,0:T(8,128)(2,1)S(1)}, u32[]{:S(2)}, u32[]{:S(2)}) %collective-permute-start.19) | collective-permute-done | bytes 262176 | tf_op jit(solution)/shard_map/ppermute | solution.py:26
  81.7 1.3 shard_map.90
  83.7 1.6 %collective-permute-start.14 = (bf16[128,1024]{1,0:T(8,128)(2,1)S(1)}, bf16[128,1024]{1,0:T(8,128)(2,1)S(1)}, u32[]{:S(2)}, u32[]{:S(2)}) collective-permute-start(bf16[128,1024]{1,0:T(8,128)(2,1)S(1)} %get-tuple-element.61), channel_id=1, source_target_pairs={{0,64},{1,65},{2,66},{3,67},{4,68},{5,69},{6,70},{7,71},{8,72},{9,... | collective-permute-start | bytes 786440 | tf_op jit(solution)/shard_map/ppermute | solution.py:26
  85.5 0.7 collective-permute-done.22.o2
  86.2 6.1 %shard_map.91 = (bf16[512,2688]{1,0:T(8,128)(2,1)S(1)}, f32[1,512,256]{2,1,0:T(8,128)S(1)}, bf16[1,528,256]{2,1,0:T(8,128)(2,1)S(1)}, bf16[1,528,256]{2,1,0:T(8,...) custom-call(s32[4]{0:T(128)S(1)} %copy-done.6, bf16[2048,896]{1,0:T(8,128)(2,1)S(1)} %copy-done, ...), custom_call_target="tpu_custom_call" | custom-call | flops 187904816 | bytes 917504 | tf_op jit(solution)/shard_map/pallas_call | solution.py:284
  92.3 4.9 %collective-permute-done.14.code_h = bf16[128,1024]{1,0:T(8,128)(2,1)S(1)} collective-permute-done((bf16[128,1024]{1,0:T(8,128)(2,1)S(1)}, bf16[128,1024]{1,0:T(8,128)(2,1)S(1)}, u32[]{:S(2)}, u32[]{:S(2)}) %collective-permute-start.14) | collective-permute-done | bytes 262176 | tf_op jit(solution)/shard_map/ppermute | solution.py:26
  97.2 1.3 shard_map.92
  99.2 1.2 collective-permute-done.23.o0
  100.4 0.7 collective-permute-done.24.o1
  101.1 0.7 collective-permute-done.25.o2
  101.7 8.5 %shard_map.93 = (bf16[512,2688]{1,0:T(8,128)(2,1)S(1)}, f32[2,512,256]{2,1,0:T(8,128)S(1)}, bf16[2,528,256]{2,1,0:T(8,128)(2,1)S(1)}, bf16[2,528,256]{2,1,0:T(8,...) custom-call(s32[4]{0:T(128)S(1)} %copy-done.6, bf16[2048,896]{1,0:T(8,128)(2,1)S(1)} %copy-done, ...), custom_call_target="tpu_custom_call" | custom-call | flops 187904816 | bytes 917504 | tf_op jit(solution)/shard_map/pallas_call | solution.py:284
  110.2 2.1 %collective-permute-start.26 = (bf16[2,528,256]{2,1,0:T(8,128)(2,1)S(1)}, bf16[2,528,256]{2,1,0:T(8,128)(2,1)S(1)}, u32[]{:S(2)}, u32[]{:S(2)}) collective-permute-start(bf16[2,528,256]{2,1,0:T(8,128)(2,1)S(1)} %get-tuple-element.84), channel_id=1, source_target_pairs={{0,1},{1,2},{2,3},{3,0},{4,5},{5,6},{6,7},{7,4},{8,9},{9,10},{10,1... | collective-permute-start | bytes 1622024 | tf_op jit(solution)/shard_map/ppermute | solution.py:26
  112.4 1.9 %collective-permute-start.27 = (bf16[2,528,256]{2,1,0:T(8,128)(2,1)S(1)}, bf16[2,528,256]{2,1,0:T(8,128)(2,1)S(1)}, u32[]{:S(2)}, u32[]{:S(2)}) collective-permute-start(bf16[2,528,256]{2,1,0:T(8,128)(2,1)S(1)} %get-tuple-element.85), channel_id=1, source_target_pairs={{0,2},{1,3},{2,0},{3,1},{4,6},{5,7},{6,4},{7,5},{8,10},{9,11},{10,... | collective-permute-start | bytes 1622024 | tf_op jit(solution)/shard_map/ppermute | solution.py:26
  114.3 1.6 %collective-permute-start.28 = (bf16[2,528,256]{2,1,0:T(8,128)(2,1)S(1)}, bf16[2,528,256]{2,1,0:T(8,128)(2,1)S(1)}, u32[]{:S(2)}, u32[]{:S(2)}) collective-permute-start(bf16[2,528,256]{2,1,0:T(8,128)(2,1)S(1)} %get-tuple-element.86), channel_id=1, source_target_pairs={{0,3},{1,0},{2,1},{3,2},{4,7},{5,4},{6,5},{7,6},{8,11},{9,8},{10,9... | collective-permute-start | bytes 1622024 | tf_op jit(solution)/shard_map/ppermute | solution.py:26
  115.8 12.6 %shard_map.94 = (bf16[2048,896]{1,0:T(8,128)(2,1)}, bf16[2048,896]{1,0:T(8,128)(2,1)}, f32[8,128]{1,0:T(8,128)S(1)}) custom-call(bf16[2048,512]{1,0:T(8,128)(2,1)S(1)} %copy-done.8, bf16[512,2688]{1,0:T(8,128)(2,1)S(1)} %get-tuple-element.88.d0.h0, bf16[512,2688]{1,0:T(8,128)(2,1)S(1)} %get-tuple-element.89.d1.h1), custom_call_target="tpu_custom_call" | custom-call | flops 7516192768 | bytes 14680064 | tf_op jit(solution)/shard_map/pallas_call | solution.py:332
  128.5 2.5 %shard_map.95 = (f32[2,128,256]{2,1,0:T(8,128)S(1)}, bf16[2,144,256]{2,1,0:T(8,128)(2,1)S(1)}, bf16[2,144,256]{2,1,0:T(8,128)(2,1)S(1)}, bf16[2,144,256]{2,1,0:T(8,128)(2,1)S(1)}) custom-call(s32[4]{0:T(128)S(1)} %copy-done.6, f32[2,512,256]{2,1,0:T(8,128)S(1)} %get-tuple-element.83.own, bf16[2,528,256]{2,1,0:T(8,128)(2,1)S(1)} %collective-permute-done.26.r1, ...), custom_call_target="tpu_custom_call" | custom-call | tf_op jit(solution)/shard_map/pallas_call | solution.py:412
  131.1 5.1 %collective-permute-start.30 = (bf16[2,144,256]{2,1,0:T(8,128)(2,1)S(1)}, bf16[2,144,256]{2,1,0:T(8,128)(2,1)S(1)}, u32[]{:S(2)}, u32[]{:S(2)}) collective-permute-start(bf16[2,144,256]{2,1,0:T(8,128)(2,1)S(1)} %get-tuple-element.93), channel_id=1, source_target_pairs={{0,8},{1,9},{2,10},{3,11},{4,12},{5,13},{6,14},{7,15},{8,0},{9,1},... | collective-permute-start | bytes 442376 | tf_op jit(solution)/shard_map/ppermute | solution.py:26
  136.2 6.3 %shard_map.96 = (bf16[896,2048]{1,0:T(8,128)(2,1)}, f32[8,128]{1,0:T(8,128)S(1)}) custom-call(bf16[2048,512]{1,0:T(8,128)(2,1)S(1)} %copy-done.7, bf16[512,2688]{1,0:T(8,128)(2,1)S(1)} %get-tuple-element.88.d0.h0, bf16[512,2688]{1,0:T(8,128)(2,1)S(1)} %get-tuple-element.89.d1.h1), custom_call_target="tpu_custom_call" | custom-call | flops 3758096384 | bytes 7340032 | tf_op jit(solution)/shard_map/pallas_call | solution.py:366
  142.5 0.9 shard_map.97
  143.4 3.3 %collective-permute-start.32 = (bf16[2,80,256]{2,1,0:T(8,128)(2,1)S(1)}, bf16[2,80,256]{2,1,0:T(8,128)(2,1)S(1)}, u32[]{:S(2)}, u32[]{:S(2)}) collective-permute-start(bf16[2,80,256]{2,1,0:T(8,128)(2,1)S(1)} %get-tuple-element.98), channel_id=1, source_target_pairs={{0,16},{1,17},{2,18},{3,19},{4,20},{5,21},{6,22},{7,23},{8,24},{9,... | collective-permute-start | bytes 245768 | tf_op jit(solution)/shard_map/ppermute | solution.py:26
  146.7 2.8 %collective-permute-done.32.r = bf16[2,80,256]{2,1,0:T(8,128)(2,1)S(1)} collective-permute-done((bf16[2,80,256]{2,1,0:T(8,128)(2,1)S(1)}, bf16[2,80,256]{2,1,0:T(8,128)(2,1)S(1)}, u32[]{:S(2)}, u32[]{:S(2)}) %collective-permute-start.32) | collective-permute-done | bytes 81952 | tf_op jit(solution)/shard_map/ppermute | solution.py:26
  149.4 0.7 shard_map.98
  (72 shorter events, 4.2 us)
Async XLA Ops:
  1.5 6.9 %collective-permute-start = (bf16[2,64,512]{2,1,0:T(8,128)(2,1)S(1)}, bf16[2,64,512]{2,1,0:T(8,128)(2,1)S(1)}, u32[]{:S(2)}, u32[]{:S(2)}) collective-permute-start(bf16[2,64,512]{2,1,0:T(8,128)(2,1)S(1)} %get-tuple-element.111), channel_id=1, source_target_pairs={{0,16},{1,17},{2,18},{3,19},{4,20},{5,21},{6,22},{7,23},{8,24},{9,... | collective-permute-start | bytes 393224 | tf_op jit(solution)/shard_map/ppermute | solution.py:26
  8.4 7.7 %collective-permute-start.3 = (bf16[2,2,64,512]{3,2,0,1:T(8,128)(2,1)S(1)}, bf16[2,2,64,512]{3,2,0,1:T(8,128)(2,1)S(1)}, u32[]{:S(2)}, u32[]{:S(2)}) collective-permute-start(bf16[2,2,64,512]{3,2,0,1:T(8,128)(2,1)S(1)} %pad_maximum_fusion.2), channel_id=1, source_target_pairs={{0,1},{1,2},{2,3},{3,0},{4,5},{5,6},{6,7},{7,4},{8,9},{9,10},{10,1... | collective-permute-start | bytes 786440 | tf_op jit(solution)/shard_map/ppermute | solution.py:26
  10.0 9.9 %collective-permute-start.2 = (bf16[2,2,64,512]{3,2,0,1:T(8,128)(2,1)S(1)}, bf16[2,2,64,512]{3,2,0,1:T(8,128)(2,1)S(1)}, u32[]{:S(2)}, u32[]{:S(2)}) collective-permute-start(bf16[2,2,64,512]{3,2,0,1:T(8,128)(2,1)S(1)} %pad_maximum_fusion.2), channel_id=1, source_target_pairs={{0,2},{1,3},{2,0},{3,1},{4,6},{5,7},{6,4},{7,5},{8,10},{9,11},{10,... | collective-permute-start | bytes 786440 | tf_op jit(solution)/shard_map/ppermute | solution.py:26
  12.7 7.2 %collective-permute-start.1 = (bf16[2,2,64,512]{3,2,0,1:T(8,128)(2,1)S(1)}, bf16[2,2,64,512]{3,2,0,1:T(8,128)(2,1)S(1)}, u32[]{:S(2)}, u32[]{:S(2)}) collective-permute-start(bf16[2,2,64,512]{3,2,0,1:T(8,128)(2,1)S(1)} %pad_maximum_fusion.2), channel_id=1, source_target_pairs={{0,3},{1,0},{2,1},{3,2},{4,7},{5,4},{6,5},{7,6},{8,11},{9,8},{10,9... | collective-permute-start | bytes 786440 | tf_op jit(solution)/shard_map/ppermute | solution.py:26
  20.0 21.2 %copy-start.10 = (bf16[4,2,64,512]{3,2,1,0:T(8,128)(2,1)}, bf16[4,2,64,512]{3,2,1,0:T(8,128)(2,1)S(1)}, u32[]{:S(2)}) copy-start(bf16[4,2,64,512]{3,2,1,0:T(8,128)(2,1)S(1)} %pad_maximum_fusion.rest_0_) | copy-start | bytes 1572868
  20.1 10.8 %collective-permute-start.4 = (bf16[4,2,64,512]{3,2,1,0:T(8,128)(2,1)S(1)}, bf16[4,2,64,512]{3,2,1,0:T(8,128)(2,1)S(1)}, u32[]{:S(2)}, u32[]{:S(2)}) collective-permute-start(bf16[4,2,64,512]{3,2,1,0:T(8,128)(2,1)S(1)} %pad_maximum_fusion.rest_0_), channel_id=1, source_target_pairs={{0,12},{1,13},{2,14},{3,15},{4,0},{5,1},{6,2},{7,3},{8,4},{9,5},{1... | collective-permute-start | bytes 1572872 | tf_op jit(solution)/shard_map/ppermute | solution.py:26
  24.2 28.1 %copy-start.9 = (bf16[4,2,64,512]{3,2,1,0:T(8,128)(2,1)}, bf16[4,2,64,512]{3,2,1,0:T(8,128)(2,1)S(1)}, u32[]{:S(2)}) copy-start(bf16[4,2,64,512]{3,2,1,0:T(8,128)(2,1)S(1)} %pad_maximum_fusion.1.rest_0_) | copy-start | bytes 1572868
  24.2 10.5 %collective-permute-start.11 = (bf16[4,2,64,512]{3,2,1,0:T(8,128)(2,1)S(1)}, bf16[4,2,64,512]{3,2,1,0:T(8,128)(2,1)S(1)}, u32[]{:S(2)}, u32[]{:S(2)}) collective-permute-start(bf16[4,2,64,512]{3,2,1,0:T(8,128)(2,1)S(1)} %pad_maximum_fusion.1.rest_0_), channel_id=1, source_target_pairs={{0,4},{1,5},{2,6},{3,7},{4,8},{5,9},{6,10},{7,11},{8,12},{9,13},{1... | collective-permute-start | bytes 1572872 | tf_op jit(solution)/shard_map/ppermute | solution.py:26
  24.3 16.0 %collective-permute-start.6 = (bf16[4,2,64,512]{3,2,1,0:T(8,128)(2,1)S(1)}, bf16[4,2,64,512]{3,2,1,0:T(8,128)(2,1)S(1)}, u32[]{:S(2)}, u32[]{:S(2)}) collective-permute-start(bf16[4,2,64,512]{3,2,1,0:T(8,128)(2,1)S(1)} %pad_maximum_fusion.rest_0_), channel_id=1, source_target_pairs={{0,4},{1,5},{2,6},{3,7},{4,8},{5,9},{6,10},{7,11},{8,12},{9,13},{1... | collective-permute-start | bytes 1572872 | tf_op jit(solution)/shard_map/ppermute | solution.py:26
  30.9 10.4 %copy-start.12 = (bf16[4,2,64,512]{3,2,1,0:T(8,128)(2,1)}, bf16[4,2,64,512]{3,2,1,0:T(8,128)(2,1)S(1)}, u32[]{:S(2)}) copy-start(bf16[4,2,64,512]{3,2,1,0:T(8,128)(2,1)S(1)} %collective-permute-done.4.rest_1_) | copy-start | bytes 1572868
  30.9 10.4 %collective-permute-start.5 = (bf16[4,2,64,512]{3,2,1,0:T(8,128)(2,1)S(1)}, bf16[4,2,64,512]{3,2,1,0:T(8,128)(2,1)S(1)}, u32[]{:S(2)}, u32[]{:S(2)}) collective-permute-start(bf16[4,2,64,512]{3,2,1,0:T(8,128)(2,1)S(1)} %collective-permute-done.4.rest_1_), channel_id=1, source_target_pairs={{0,12},{1,13},{2,14},{3,15},{4,0},{5,1},{6,2},{7,3},{8,4},{9,5},{1... | collective-permute-start | bytes 1572872 | tf_op jit(solution)/shard_map/ppermute | solution.py:26
  34.6 18.4 %collective-permute-start.10 = (bf16[4,2,64,512]{3,2,1,0:T(8,128)(2,1)S(1)}, bf16[4,2,64,512]{3,2,1,0:T(8,128)(2,1)}, u32[]{:S(2)}, u32[]{:S(2)}) collective-permute-start(bf16[4,2,64,512]{3,2,1,0:T(8,128)(2,1)S(1)} %pad_maximum_fusion.1.rest_0_), channel_id=1, source_target_pairs={{0,12},{1,13},{2,14},{3,15},{4,0},{5,1},{6,2},{7,3},{8,4},{9,5},{1... | collective-permute-start | bytes 1572872 | tf_op jit(solution)/shard_map/ppermute | solution.py:26
  34.7 17.6 %copy-start.11 = (bf16[4,2,64,512]{3,2,1,0:T(8,128)(2,1)}, bf16[4,2,64,512]{3,2,1,0:T(8,128)(2,1)S(1)}, u32[]{:S(2)}) copy-start(bf16[4,2,64,512]{3,2,1,0:T(8,128)(2,1)S(1)} %collective-permute-done.11.rest_3_) | copy-start | bytes 1572868
  34.7 18.2 %collective-permute-start.12 = (bf16[4,2,64,512]{3,2,1,0:T(8,128)(2,1)S(1)}, bf16[4,2,64,512]{3,2,1,0:T(8,128)(2,1)}, u32[]{:S(2)}, u32[]{:S(2)}) collective-permute-start(bf16[4,2,64,512]{3,2,1,0:T(8,128)(2,1)S(1)} %collective-permute-done.11.rest_3_), channel_id=1, source_target_pairs={{0,4},{1,5},{2,6},{3,7},{4,8},{5,9},{6,10},{7,11},{8,12},{9,13},{1... | collective-permute-start | bytes 1572872 | tf_op jit(solution)/shard_map/ppermute | solution.py:26
  40.3 0.9 copy-start.13
  41.3 0.8 copy-start.14
  52.3 8.9 %copy-start.3 = (f32[128,1792]{1,0:T(8,128)S(1)}, f32[128,1792]{1,0:T(8,128)}, u32[]{:S(2)}) copy-start(f32[128,1792]{1,0:T(8,128)} %get-tuple-element.62.mine) | copy-start | bytes 2752516
  52.4 8.9 %collective-permute-start.15 = (f32[128,896]{1,0:T(8,128)}, f32[128,896]{1,0:T(8,128)S(1)}, u32[]{:S(2)}, u32[]{:S(2)}) collective-permute-start(f32[128,896]{1,0:T(8,128)} %get-tuple-element.63), channel_id=1, source_target_pairs={{0,32},{1,33},{2,34},{3,35},{4,36},{5,37},{6,38},{7,39},{8,40},{9,... | collective-permute-start | bytes 1376264 | tf_op jit(solution)/shard_map/ppermute | solution.py:26
  52.4 14.1 %copy-start.2 = (f32[128,1792]{1,0:T(8,128)S(1)}, f32[128,1792]{1,0:T(8,128)}, u32[]{:S(2)}) copy-start(f32[128,1792]{1,0:T(8,128)} %get-tuple-element.53.mine) | copy-start | bytes 2752516
  52.5 8.8 %collective-permute-start.16 = (f32[128,896]{1,0:T(8,128)}, f32[128,896]{1,0:T(8,128)S(1)}, u32[]{:S(2)}, u32[]{:S(2)}) collective-permute-start(f32[128,896]{1,0:T(8,128)} %get-tuple-element.64), channel_id=1, source_target_pairs={{0,32},{1,33},{2,34},{3,35},{4,36},{5,37},{6,38},{7,39},{8,40},{9,... | collective-permute-start | bytes 1376264 | tf_op jit(solution)/shard_map/ppermute | solution.py:26
  60.9 3.2 %collective-permute-start.18 = (f32[128,896]{1,0:T(8,128)}, f32[128,896]{1,0:T(8,128)S(1)}, u32[]{:S(2)}, u32[]{:S(2)}) collective-permute-start(f32[128,896]{1,0:T(8,128)} %get-tuple-element.68), channel_id=1, source_target_pairs={{0,32},{1,33},{2,34},{3,35},{4,36},{5,37},{6,38},{7,39},{8,40},{9,... | collective-permute-start | bytes 1376264 | tf_op jit(solution)/shard_map/ppermute | solution.py:26
  61.2 25.0 %copy-start.6 = (s32[4]{0:T(128)S(1)}, s32[4]{0:T(128)}, u32[]{:S(2)}) copy-start(s32[4]{0:T(128)} %pad_add_fusion.ids) | copy-start | bytes 52
  61.2 25.0 %copy-start = (bf16[2048,896]{1,0:T(8,128)(2,1)S(1)}, bf16[2048,896]{1,0:T(8,128)(2,1)}, u32[]{:S(2)}) copy-start(bf16[2048,896]{1,0:T(8,128)(2,1)} %wg.3) | copy-start | bytes 11010052
  61.3 25.0 %copy-start.1 = (bf16[2048,896]{1,0:T(8,128)(2,1)S(1)}, bf16[2048,896]{1,0:T(8,128)(2,1)}, u32[]{:S(2)}) copy-start(bf16[2048,896]{1,0:T(8,128)(2,1)} %wu.3) | copy-start | bytes 11010052
  62.1 19.7 %collective-permute-start.17 = (bf16[128,1920]{1,0:T(8,128)(2,1)S(1)}, bf16[128,1920]{1,0:T(8,128)(2,1)S(1)}, u32[]{:S(2)}, u32[]{:S(2)}) collective-permute-start(bf16[128,1920]{1,0:T(8,128)(2,1)S(1)} %get-tuple-element.66), channel_id=1, source_target_pairs={{0,64},{1,65},{2,66},{3,67},{4,68},{5,69},{6,70},{7,71},{8,72},{9,... | collective-permute-start | bytes 1474568 | tf_op jit(solution)/shard_map/ppermute | solution.py:26
  63.6 3.0 %collective-permute-start.7 = (f32[128,896]{1,0:T(8,128)}, f32[128,896]{1,0:T(8,128)S(1)}, u32[]{:S(2)}, u32[]{:S(2)}) collective-permute-start(f32[128,896]{1,0:T(8,128)} %get-tuple-element.54), channel_id=1, source_target_pairs={{0,32},{1,33},{2,34},{3,35},{4,36},{5,37},{6,38},{7,39},{8,40},{9,... | collective-permute-start | bytes 1376264 | tf_op jit(solution)/shard_map/ppermute | solution.py:26
  63.6 3.0 %collective-permute-start.8 = (f32[128,896]{1,0:T(8,128)}, f32[128,896]{1,0:T(8,128)S(1)}, u32[]{:S(2)}, u32[]{:S(2)}) collective-permute-start(f32[128,896]{1,0:T(8,128)} %get-tuple-element.55), channel_id=1, source_target_pairs={{0,32},{1,33},{2,34},{3,35},{4,36},{5,37},{6,38},{7,39},{8,40},{9,... | collective-permute-start | bytes 1376264 | tf_op jit(solution)/shard_map/ppermute | solution.py:26
  64.1 4.5 %collective-permute-start.13 = (f32[128,896]{1,0:T(8,128)}, f32[128,896]{1,0:T(8,128)S(1)}, u32[]{:S(2)}, u32[]{:S(2)}) collective-permute-start(f32[128,896]{1,0:T(8,128)} %get-tuple-element.59), channel_id=1, source_target_pairs={{0,32},{1,33},{2,34},{3,35},{4,36},{5,37},{6,38},{7,39},{8,40},{9,... | collective-permute-start | bytes 1376264 | tf_op jit(solution)/shard_map/ppermute | solution.py:26
  64.1 1.0 copy-start.5
  65.8 16.0 %collective-permute-start.19 = (bf16[128,1024]{1,0:T(8,128)(2,1)S(1)}, bf16[128,1024]{1,0:T(8,128)(2,1)S(1)}, u32[]{:S(2)}, u32[]{:S(2)}) collective-permute-start(bf16[128,1024]{1,0:T(8,128)(2,1)S(1)} %get-tuple-element.70), channel_id=1, source_target_pairs={{0,64},{1,65},{2,66},{3,67},{4,68},{5,69},{6,70},{7,71},{8,72},{9,... | collective-permute-start | bytes 786440 | tf_op jit(solution)/shard_map/ppermute | solution.py:26
  67.4 29.8 %collective-permute-start.9 = (bf16[128,1920]{1,0:T(8,128)(2,1)S(1)}, bf16[128,1920]{1,0:T(8,128)(2,1)S(1)}, u32[]{:S(2)}, u32[]{:S(2)}) collective-permute-start(bf16[128,1920]{1,0:T(8,128)(2,1)S(1)} %get-tuple-element.57), channel_id=1, source_target_pairs={{0,64},{1,65},{2,66},{3,67},{4,68},{5,69},{6,70},{7,71},{8,72},{9,... | collective-permute-start | bytes 1474568 | tf_op jit(solution)/shard_map/ppermute | solution.py:26
  68.6 1.0 copy-start.4
  83.0 2.3 %collective-permute-start.20 = (f32[128,896]{1,0:T(8,128)S(1)}, f32[128,896]{1,0:T(8,128)S(1)}, u32[]{:S(2)}, u32[]{:S(2)}) collective-permute-start(f32[128,896]{1,0:T(8,128)S(1)} %get-tuple-element.72.m0), channel_id=1, source_target_pairs={{0,32},{1,33},{2,34},{3,35},{4,36},{5,37},{6,38},{7,39},{8,40},{9,... | collective-permute-start | bytes 1376264 | tf_op jit(solution)/shard_map/ppermute | solution.py:26
  83.1 2.5 %collective-permute-start.21 = (f32[128,896]{1,0:T(8,128)S(1)}, f32[128,896]{1,0:T(8,128)S(1)}, u32[]{:S(2)}, u32[]{:S(2)}) collective-permute-start(f32[128,896]{1,0:T(8,128)S(1)} %get-tuple-element.73.m1), channel_id=1, source_target_pairs={{0,32},{1,33},{2,34},{3,35},{4,36},{5,37},{6,38},{7,39},{8,40},{9,... | collective-permute-start | bytes 1376264 | tf_op jit(solution)/shard_map/ppermute | solution.py:26
  83.6 2.6 %collective-permute-start.22 = (f32[128,896]{1,0:T(8,128)S(1)}, f32[128,896]{1,0:T(8,128)S(1)}, u32[]{:S(2)}, u32[]{:S(2)}) collective-permute-start(f32[128,896]{1,0:T(8,128)S(1)} %get-tuple-element.74.m2), channel_id=1, source_target_pairs={{0,32},{1,33},{2,34},{3,35},{4,36},{5,37},{6,38},{7,39},{8,40},{9,... | collective-permute-start | bytes 1376264 | tf_op jit(solution)/shard_map/ppermute | solution.py:26
  83.7 13.5 %collective-permute-start.14 = (bf16[128,1024]{1,0:T(8,128)(2,1)S(1)}, bf16[128,1024]{1,0:T(8,128)(2,1)S(1)}, u32[]{:S(2)}, u32[]{:S(2)}) collective-permute-start(bf16[128,1024]{1,0:T(8,128)(2,1)S(1)} %get-tuple-element.61), channel_id=1, source_target_pairs={{0,64},{1,65},{2,66},{3,67},{4,68},{5,69},{6,70},{7,71},{8,72},{9,... | collective-permute-start | bytes 786440 | tf_op jit(solution)/shard_map/ppermute | solution.py:26
  98.5 1.9 %collective-permute-start.23 = (f32[128,896]{1,0:T(8,128)S(1)}, f32[128,896]{1,0:T(8,128)S(1)}, u32[]{:S(2)}, u32[]{:S(2)}) collective-permute-start(f32[128,896]{1,0:T(8,128)S(1)} %get-tuple-element.76.m0), channel_id=1, source_target_pairs={{0,32},{1,33},{2,34},{3,35},{4,36},{5,37},{6,38},{7,39},{8,40},{9,... | collective-permute-start | bytes 1376264 | tf_op jit(solution)/shard_map/ppermute | solution.py:26
  98.6 2.5 %collective-permute-start.24 = (f32[128,896]{1,0:T(8,128)S(1)}, f32[128,896]{1,0:T(8,128)S(1)}, u32[]{:S(2)}, u32[]{:S(2)}) collective-permute-start(f32[128,896]{1,0:T(8,128)S(1)} %get-tuple-element.77.m1), channel_id=1, source_target_pairs={{0,32},{1,33},{2,34},{3,35},{4,36},{5,37},{6,38},{7,39},{8,40},{9,... | collective-permute-start | bytes 1376264 | tf_op jit(solution)/shard_map/ppermute | solution.py:26
  99.1 2.6 %collective-permute-start.25 = (f32[128,896]{1,0:T(8,128)S(1)}, f32[128,896]{1,0:T(8,128)S(1)}, u32[]{:S(2)}, u32[]{:S(2)}) collective-permute-start(f32[128,896]{1,0:T(8,128)S(1)} %get-tuple-element.78.m2), channel_id=1, source_target_pairs={{0,32},{1,33},{2,34},{3,35},{4,36},{5,37},{6,38},{7,39},{8,40},{9,... | collective-permute-start | bytes 1376264 | tf_op jit(solution)/shard_map/ppermute | solution.py:26
  101.7 14.1 %copy-start.8 = (bf16[2048,512]{1,0:T(8,128)(2,1)S(1)}, bf16[2048,512]{1,0:T(8,128)(2,1)}, u32[]{:S(2)}) copy-start(bf16[2048,512]{1,0:T(8,128)(2,1)} %get-tuple-element.87.x) | copy-start | bytes 6291460
  110.2 18.3 %collective-permute-start.26 = (bf16[2,528,256]{2,1,0:T(8,128)(2,1)S(1)}, bf16[2,528,256]{2,1,0:T(8,128)(2,1)S(1)}, u32[]{:S(2)}, u32[]{:S(2)}) collective-permute-start(bf16[2,528,256]{2,1,0:T(8,128)(2,1)S(1)} %get-tuple-element.84), channel_id=1, source_target_pairs={{0,1},{1,2},{2,3},{3,0},{4,5},{5,6},{6,7},{7,4},{8,9},{9,10},{10,1... | collective-permute-start | bytes 1622024 | tf_op jit(solution)/shard_map/ppermute | solution.py:26
  112.4 16.1 %collective-permute-start.27 = (bf16[2,528,256]{2,1,0:T(8,128)(2,1)S(1)}, bf16[2,528,256]{2,1,0:T(8,128)(2,1)S(1)}, u32[]{:S(2)}, u32[]{:S(2)}) collective-permute-start(bf16[2,528,256]{2,1,0:T(8,128)(2,1)S(1)} %get-tuple-element.85), channel_id=1, source_target_pairs={{0,2},{1,3},{2,0},{3,1},{4,6},{5,7},{6,4},{7,5},{8,10},{9,11},{10,... | collective-permute-start | bytes 1622024 | tf_op jit(solution)/shard_map/ppermute | solution.py:26
  114.3 14.2 %collective-permute-start.28 = (bf16[2,528,256]{2,1,0:T(8,128)(2,1)S(1)}, bf16[2,528,256]{2,1,0:T(8,128)(2,1)S(1)}, u32[]{:S(2)}, u32[]{:S(2)}) collective-permute-start(bf16[2,528,256]{2,1,0:T(8,128)(2,1)S(1)} %get-tuple-element.86), channel_id=1, source_target_pairs={{0,3},{1,0},{2,1},{3,2},{4,7},{5,4},{6,5},{7,6},{8,11},{9,8},{10,9... | collective-permute-start | bytes 1622024 | tf_op jit(solution)/shard_map/ppermute | solution.py:26
  115.8 20.4 %copy-start.7 = (bf16[2048,512]{1,0:T(8,128)(2,1)S(1)}, bf16[2048,512]{1,0:T(8,128)(2,1)}, u32[]{:S(2)}) copy-start(bf16[2048,512]{1,0:T(8,128)(2,1)} %get-tuple-element.95.g) | copy-start | bytes 6291460
  131.0 11.5 %collective-permute-start.29 = (bf16[2,144,256]{2,1,0:T(8,128)(2,1)S(1)}, bf16[2,144,256]{2,1,0:T(8,128)(2,1)S(1)}, u32[]{:S(2)}, u32[]{:S(2)}) collective-permute-start(bf16[2,144,256]{2,1,0:T(8,128)(2,1)S(1)} %get-tuple-element.92), channel_id=1, source_target_pairs={{0,4},{1,5},{2,6},{3,7},{4,8},{5,9},{6,10},{7,11},{8,12},{9,13},{1... | collective-permute-start | bytes 442376 | tf_op jit(solution)/shard_map/ppermute | solution.py:26
  131.1 11.4 %collective-permute-start.30 = (bf16[2,144,256]{2,1,0:T(8,128)(2,1)S(1)}, bf16[2,144,256]{2,1,0:T(8,128)(2,1)S(1)}, u32[]{:S(2)}, u32[]{:S(2)}) collective-permute-start(bf16[2,144,256]{2,1,0:T(8,128)(2,1)S(1)} %get-tuple-element.93), channel_id=1, source_target_pairs={{0,8},{1,9},{2,10},{3,11},{4,12},{5,13},{6,14},{7,15},{8,0},{9,1},... | collective-permute-start | bytes 442376 | tf_op jit(solution)/shard_map/ppermute | solution.py:26
  136.2 6.3 %collective-permute-start.31 = (bf16[2,144,256]{2,1,0:T(8,128)(2,1)S(1)}, bf16[2,144,256]{2,1,0:T(8,128)(2,1)S(1)}, u32[]{:S(2)}, u32[]{:S(2)}) collective-permute-start(bf16[2,144,256]{2,1,0:T(8,128)(2,1)S(1)} %get-tuple-element.94), channel_id=1, source_target_pairs={{0,12},{1,13},{2,14},{3,15},{4,0},{5,1},{6,2},{7,3},{8,4},{9,5},{1... | collective-permute-start | bytes 442376 | tf_op jit(solution)/shard_map/ppermute | solution.py:26
  143.4 6.0 %collective-permute-start.32 = (bf16[2,80,256]{2,1,0:T(8,128)(2,1)S(1)}, bf16[2,80,256]{2,1,0:T(8,128)(2,1)S(1)}, u32[]{:S(2)}, u32[]{:S(2)}) collective-permute-start(bf16[2,80,256]{2,1,0:T(8,128)(2,1)S(1)} %get-tuple-element.98), channel_id=1, source_target_pairs={{0,16},{1,17},{2,18},{3,19},{4,20},{5,21},{6,22},{7,23},{8,24},{9,... | collective-permute-start | bytes 245768 | tf_op jit(solution)/shard_map/ppermute | solution.py:26

commit v5 on v4

--- a/solution.py
+++ b/solution.py
@@ -141,7 +141,7 @@
     *out, acts = _call(
         functools.partial(_forward_body, n, width),
         (mine,) * 2 + (other,) * (2 * n) + (shape((depth, tokens), BF16),),
-        WHOLE,
+        DELTA if n == 1 else WHOLE,
         in_specs=[SMEM] + [ANY] * (4 + n),
         out_specs=(ANY,) * (3 + 2 * n),
         scratch_shapes=[

time: 150 us -> 151 us (level)
  waiting for transfers between devices: 42.6 us -> 45.7 us
  other arithmetic: 1.69 us -> 3.34 us
    ppermute x33, waiting for transfers between devices: 42.6 us -> 45.7 us  [_send(): return lax.ppermute(a, BOTH, _moves(shift))]
    another operation x3, other arithmetic: 0.16 us -> 1.76 us  [per_device(): x, g = (jnp.stack([p[:, i] for p in near]) for i in range(2))]
  transfers between devices with their start and end apart: 33 -> 33, of which waited for: 15 -> 16; matrix products, arithmetic and copies ran while one was open for 0% -> 1% of each run, Pallas kernels for 31% -> 31%
where the time goes in v5:
time: 151 us
  Pallas kernels  59.6 us (39%)
  waiting for transfers between devices  45.7 us (30%)
  starting transfers between devices  39.6 us (26%)
  other arithmetic  3.34 us (2%)
  local copies, waits for them, and re-layouts  1.69 us (1%)
    ppermute x33, waiting for transfers between devices, _send(): return lax.ppermute(a, BOTH, _moves(shift))  45.7 us
    ppermute x33, starting transfers between devices, _send(): return lax.ppermute(a, BOTH, _moves(shift))  39.6 us
    pallas_call x2, Pallas kernels, forward(): _call(functools.partial(_forward_body, n, width), (mine,) * 2 + (other,)...  17.1 us
    pallas_call x2, Pallas kernels, grad_in(): _call(functools.partial(_grad_in_body, width, len(before)), (shape((2 * t...  14.4 us
    pallas_call x1, Pallas kernels, grad_weights(): _call(functools.partial(_grad_up_body, steps), (out, out, TICK), DELTA, g...  12.6 us
    pallas_call x1, Pallas kernels, grad_down_weight(): _call(_grad_down_body, (shape((width, depth), BF16), TICK), DELTA, grid=(...  6.25 us
  transfers between devices with their start and end apart: 33, of which 16 were waited for; matrix products, arithmetic and copies ran while one was open for 1% of the time, Pallas kernels for 31%

profile of v5, /device:TPU:0, one launch (start us, length us, event | category | flops | bytes accessed | tf_op | source)
XLA Modules:
  0.0 150.8 jit_solution(16426475043339071110)
XLA Ops:
  0.6 0.9 fusion.4
  1.5 3.4 %collective-permute-start = (bf16[2,64,512]{2,1,0:T(8,128)(2,1)S(1)}, bf16[2,64,512]{2,1,0:T(8,128)(2,1)S(1)}, u32[]{:S(2)}, u32[]{:S(2)}) collective-permute-start(bf16[2,64,512]{2,1,0:T(8,128)(2,1)S(1)} %get-tuple-element.111), channel_id=1, source_target_pairs={{0,16},{1,17},{2,18},{3,19},{4,20},{5,21},{6,22},{7,23},{8,24},{9,... | collective-permute-start | bytes 393224 | tf_op jit(solution)/shard_map/ppermute | solution.py:26
  4.9 3.5 %collective-permute-done = bf16[2,64,512]{2,1,0:T(8,128)(2,1)S(1)} collective-permute-done((bf16[2,64,512]{2,1,0:T(8,128)(2,1)S(1)}, bf16[2,64,512]{2,1,0:T(8,128)(2,1)S(1)}, u32[]{:S(2)}, u32[]{:S(2)}) %collective-permute-start) | collective-permute-done | bytes 131104 | tf_op jit(solution)/shard_map/ppermute | solution.py:26
  8.4 1.6 %collective-permute-start.3 = (bf16[2,2,64,512]{3,2,0,1:T(8,128)(2,1)S(1)}, bf16[2,2,64,512]{3,2,0,1:T(8,128)(2,1)S(1)}, u32[]{:S(2)}, u32[]{:S(2)}) collective-permute-start(bf16[2,2,64,512]{3,2,0,1:T(8,128)(2,1)S(1)} %pad_maximum_fusion.2), channel_id=1, source_target_pairs={{0,1},{1,2},{2,3},{3,0},{4,5},{5,6},{6,7},{7,4},{8,9},{9,10},{10,1... | collective-permute-start | bytes 786440 | tf_op jit(solution)/shard_map/ppermute | solution.py:26
  10.0 2.7 %collective-permute-start.2 = (bf16[2,2,64,512]{3,2,0,1:T(8,128)(2,1)S(1)}, bf16[2,2,64,512]{3,2,0,1:T(8,128)(2,1)S(1)}, u32[]{:S(2)}, u32[]{:S(2)}) collective-permute-start(bf16[2,2,64,512]{3,2,0,1:T(8,128)(2,1)S(1)} %pad_maximum_fusion.2), channel_id=1, source_target_pairs={{0,2},{1,3},{2,0},{3,1},{4,6},{5,7},{6,4},{7,5},{8,10},{9,11},{10,... | collective-permute-start | bytes 786440 | tf_op jit(solution)/shard_map/ppermute | solution.py:26
  12.7 1.4 collective-permute-start.1
  14.2 1.8 %collective-permute-done.3 = bf16[2,2,64,512]{3,2,0,1:T(8,128)(2,1)S(1)} collective-permute-done((bf16[2,2,64,512]{3,2,0,1:T(8,128)(2,1)S(1)}, bf16[2,2,64,512]{3,2,0,1:T(8,128)(2,1)S(1)}, u32[]{:S(2)}, u32[]{:S(2)}) %collective-permute-start.3) | collective-permute-done | bytes 262176 | tf_op jit(solution)/shard_map/ppermute | solution.py:26
  16.1 3.8 %collective-permute-done.2 = bf16[2,2,64,512]{3,2,0,1:T(8,128)(2,1)S(1)} collective-permute-done((bf16[2,2,64,512]{3,2,0,1:T(8,128)(2,1)S(1)}, bf16[2,2,64,512]{3,2,0,1:T(8,128)(2,1)S(1)}, u32[]{:S(2)}, u32[]{:S(2)}) %collective-permute-start.2) | collective-permute-done | bytes 262176 | tf_op jit(solution)/shard_map/ppermute | solution.py:26
  20.0 0.9 pad_maximum_fusion.rest_0_
  20.8 4.0 %collective-permute-start.4 = (bf16[4,2,64,512]{3,2,1,0:T(8,128)(2,1)}, bf16[4,2,64,512]{3,2,1,0:T(8,128)(2,1)}, u32[]{:S(2)}, u32[]{:S(2)}) collective-permute-start(bf16[4,2,64,512]{3,2,1,0:T(8,128)(2,1)} %pad_maximum_fusion.rest_0_), channel_id=1, source_target_pairs={{0,12},{1,13},{2,14},{3,15},{4,0},{5,1},{6,2},{7,3},{8,4},{9,5},{1... | collective-permute-start | bytes 1572872 | tf_op jit(solution)/shard_map/ppermute | solution.py:26
  24.9 0.9 pad_maximum_fusion.1.rest_0_
  25.7 6.1 %collective-permute-done.4.rest_1_ = bf16[4,2,64,512]{3,2,1,0:T(8,128)(2,1)} collective-permute-done((bf16[4,2,64,512]{3,2,1,0:T(8,128)(2,1)}, bf16[4,2,64,512]{3,2,1,0:T(8,128)(2,1)}, u32[]{:S(2)}, u32[]{:S(2)}) %collective-permute-start.4) | collective-permute-done | bytes 524320 | tf_op jit(solution)/shard_map/ppermute | solution.py:26
  31.9 3.7 %collective-permute-start.5 = (bf16[4,2,64,512]{3,2,1,0:T(8,128)(2,1)}, bf16[4,2,64,512]{3,2,1,0:T(8,128)(2,1)}, u32[]{:S(2)}, u32[]{:S(2)}) collective-permute-start(bf16[4,2,64,512]{3,2,1,0:T(8,128)(2,1)} %collective-permute-done.4.rest_1_), channel_id=1, source_target_pairs={{0,12},{1,13},{2,14},{3,15},{4,0},{5,1},{6,2},{7,3},{8,4},{9,5},{1... | collective-permute-start | bytes 1572872 | tf_op jit(solution)/shard_map/ppermute | solution.py:26
  35.6 0.8 collective-permute-done.11.rest_3_
  36.4 1.2 collective-permute-start.12
  37.6 0.7 pad_add_fusion.ids
  38.3 3.8 %collective-permute-done.6.rest_3_ = bf16[4,2,64,512]{3,2,1,0:T(8,128)(2,1)} collective-permute-done((bf16[4,2,64,512]{3,2,1,0:T(8,128)(2,1)}, bf16[4,2,64,512]{3,2,1,0:T(8,128)(2,1)}, u32[]{:S(2)}, u32[]{:S(2)}) %collective-permute-start.6) | collective-permute-done | bytes 524320 | tf_op jit(solution)/shard_map/ppermute | solution.py:26
  42.6 10.3 %shard_map.84 = (f32[128,1792]{1,0:T(8,128)}, f32[128,1792]{1,0:T(8,128)}, f32[128,896]{1,0:T(8,128)}, f32[128,896]{1,0:T(8,128)}, f32[128,896]{1,0:T(8,128)}, /...) custom-call(s32[4]{0:T(128)} %pad_add_fusion.ids, bf16[4,2,64,512]{3,2,1,0:T(8,128)(2,1)} %pad_maximum_fusion.rest_0_, ...), custom_call_target="tpu_custom_call" | custom-call | flops 187904816 | bytes 576716 | tf_op jit(solution)/shard_map/pallas_call | solution.py:141
  53.5 6.8 %shard_map.86 = (f32[128,896]{1,0:T(8,128)S(1)}, f32[128,896]{1,0:T(8,128)S(1)}, f32[128,896]{1,0:T(8,128)S(1)}, f32[128,896]{1,0:T(8,128)S(1)}, bf16[2048,512]{1,0:T(8,128)(2,1)S(1)}) custom-call(s32[4]{0:T(128)S(1)} %copy-done.5, bf16[4,2,64,512]{3,2,1,0:T(8,128)(2,1)} %pad_maximum_fusion.1.rest_0_, ...), custom_call_target="tpu_custom_call" | custom-call | flops 93952408 | bytes 393216 | tf_op jit(solution)/shard_map/pallas_call | solution.py:141
  60.6 0.9 shard_map.88
  61.5 1.6 %collective-permute-start.17 = (bf16[128,1920]{1,0:T(8,128)(2,1)S(1)}, bf16[128,1920]{1,0:T(8,128)(2,1)S(1)}, u32[]{:S(2)}, u32[]{:S(2)}) collective-permute-start(bf16[128,1920]{1,0:T(8,128)(2,1)S(1)} %get-tuple-element.66), channel_id=1, source_target_pairs={{0,64},{1,65},{2,66},{3,67},{4,68},{5,69},{6,70},{7,71},{8,72},{9,... | collective-permute-start | bytes 1474568 | tf_op jit(solution)/shard_map/ppermute | solution.py:26
  63.9 0.6 shard_map.89
  64.9 0.6 collective-permute-done.8.rest_1_
  65.6 0.8 shard_map.85
  66.4 0.9 collective-permute-start.9
  67.7 13.5 %collective-permute-done.19.code_h = bf16[128,1024]{1,0:T(8,128)(2,1)S(1)} collective-permute-done((bf16[128,1024]{1,0:T(8,128)(2,1)S(1)}, bf16[128,1024]{1,0:T(8,128)(2,1)S(1)}, u32[]{:S(2)}, u32[]{:S(2)}) %collective-permute-start.19) | collective-permute-done | bytes 262176 | tf_op jit(solution)/shard_map/ppermute | solution.py:26
  81.2 1.2 shard_map.90
  83.1 1.6 %collective-permute-start.14 = (bf16[128,1024]{1,0:T(8,128)(2,1)S(1)}, bf16[128,1024]{1,0:T(8,128)(2,1)S(1)}, u32[]{:S(2)}, u32[]{:S(2)}) collective-permute-start(bf16[128,1024]{1,0:T(8,128)(2,1)S(1)} %get-tuple-element.61), channel_id=1, source_target_pairs={{0,64},{1,65},{2,66},{3,67},{4,68},{5,69},{6,70},{7,71},{8,72},{9,... | collective-permute-start | bytes 786440 | tf_op jit(solution)/shard_map/ppermute | solution.py:26
  85.0 0.7 collective-permute-done.22.o2
  85.6 6.1 %shard_map.91 = (bf16[512,2688]{1,0:T(8,128)(2,1)S(1)}, f32[1,512,256]{2,1,0:T(8,128)S(1)}, bf16[1,528,256]{2,1,0:T(8,128)(2,1)S(1)}, bf16[1,528,256]{2,1,0:T(8,...) custom-call(s32[4]{0:T(128)S(1)} %copy-done.5, bf16[2048,896]{1,0:T(8,128)(2,1)S(1)} %copy-done, ...), custom_call_target="tpu_custom_call" | custom-call | flops 187904816 | bytes 917504 | tf_op jit(solution)/shard_map/pallas_call | solution.py:284
  91.7 4.9 %collective-permute-done.14.code_h = bf16[128,1024]{1,0:T(8,128)(2,1)S(1)} collective-permute-done((bf16[128,1024]{1,0:T(8,128)(2,1)S(1)}, bf16[128,1024]{1,0:T(8,128)(2,1)S(1)}, u32[]{:S(2)}, u32[]{:S(2)}) %collective-permute-start.14) | collective-permute-done | bytes 262176 | tf_op jit(solution)/shard_map/ppermute | solution.py:26
  96.6 1.2 shard_map.92
  98.5 1.2 collective-permute-done.23.o0
  99.8 0.7 collective-permute-done.24.o1
  100.4 0.7 collective-permute-done.25.o2
  101.1 8.3 %shard_map.93 = (bf16[512,2688]{1,0:T(8,128)(2,1)S(1)}, f32[2,512,256]{2,1,0:T(8,128)S(1)}, bf16[2,528,256]{2,1,0:T(8,128)(2,1)S(1)}, bf16[2,528,256]{2,1,0:T(8,...) custom-call(s32[4]{0:T(128)S(1)} %copy-done.5, bf16[2048,896]{1,0:T(8,128)(2,1)S(1)} %copy-done, ...), custom_call_target="tpu_custom_call" | custom-call | flops 187904816 | bytes 917504 | tf_op jit(solution)/shard_map/pallas_call | solution.py:284
  109.4 1.9 %collective-permute-start.26 = (bf16[2,528,256]{2,1,0:T(8,128)(2,1)S(1)}, bf16[2,528,256]{2,1,0:T(8,128)(2,1)S(1)}, u32[]{:S(2)}, u32[]{:S(2)}) collective-permute-start(bf16[2,528,256]{2,1,0:T(8,128)(2,1)S(1)} %get-tuple-element.84), channel_id=1, source_target_pairs={{0,1},{1,2},{2,3},{3,0},{4,5},{5,6},{6,7},{7,4},{8,9},{9,10},{10,1... | collective-permute-start | bytes 1622024 | tf_op jit(solution)/shard_map/ppermute | solution.py:26
  111.4 2.1 %collective-permute-start.27 = (bf16[2,528,256]{2,1,0:T(8,128)(2,1)S(1)}, bf16[2,528,256]{2,1,0:T(8,128)(2,1)S(1)}, u32[]{:S(2)}, u32[]{:S(2)}) collective-permute-start(bf16[2,528,256]{2,1,0:T(8,128)(2,1)S(1)} %get-tuple-element.85), channel_id=1, source_target_pairs={{0,2},{1,3},{2,0},{3,1},{4,6},{5,7},{6,4},{7,5},{8,10},{9,11},{10,... | collective-permute-start | bytes 1622024 | tf_op jit(solution)/shard_map/ppermute | solution.py:26
  113.5 1.6 %collective-permute-start.28 = (bf16[2,528,256]{2,1,0:T(8,128)(2,1)S(1)}, bf16[2,528,256]{2,1,0:T(8,128)(2,1)S(1)}, u32[]{:S(2)}, u32[]{:S(2)}) collective-permute-start(bf16[2,528,256]{2,1,0:T(8,128)(2,1)S(1)} %get-tuple-element.86), channel_id=1, source_target_pairs={{0,3},{1,0},{2,1},{3,2},{4,7},{5,4},{6,5},{7,6},{8,11},{9,8},{10,9... | collective-permute-start | bytes 1622024 | tf_op jit(solution)/shard_map/ppermute | solution.py:26
  115.0 1.6 %copy-done.8 = bf16[2048,512]{1,0:T(8,128)(2,1)S(1)} copy-done((bf16[2048,512]{1,0:T(8,128)(2,1)S(1)}, bf16[2048,512]{1,0:T(8,128)(2,1)}, u32[]{:S(2)}) %copy-start.8) | copy-done | bytes 2097176
  116.6 12.6 %shard_map.94 = (bf16[2048,896]{1,0:T(8,128)(2,1)}, bf16[2048,896]{1,0:T(8,128)(2,1)}, f32[8,128]{1,0:T(8,128)S(1)}) custom-call(bf16[2048,512]{1,0:T(8,128)(2,1)S(1)} %copy-done.8, bf16[512,2688]{1,0:T(8,128)(2,1)S(1)} %get-tuple-element.88.d0.h0, bf16[512,2688]{1,0:T(8,128)(2,1)S(1)} %get-tuple-element.89.d1.h1), custom_call_target="tpu_custom_call" | custom-call | flops 7516192768 | bytes 14680064 | tf_op jit(solution)/shard_map/pallas_call | solution.py:332
  129.2 2.5 %shard_map.95 = (f32[2,128,256]{2,1,0:T(8,128)S(1)}, bf16[2,144,256]{2,1,0:T(8,128)(2,1)S(1)}, bf16[2,144,256]{2,1,0:T(8,128)(2,1)S(1)}, bf16[2,144,256]{2,1,0:T(8,128)(2,1)S(1)}) custom-call(s32[4]{0:T(128)S(1)} %copy-done.5, f32[2,512,256]{2,1,0:T(8,128)S(1)} %get-tuple-element.83.own, bf16[2,528,256]{2,1,0:T(8,128)(2,1)S(1)} %collective-permute-done.26.r1, ...), custom_call_target="tpu_custom_call" | custom-call | tf_op jit(solution)/shard_map/pallas_call | solution.py:412
  131.8 5.1 %collective-permute-start.30 = (bf16[2,144,256]{2,1,0:T(8,128)(2,1)S(1)}, bf16[2,144,256]{2,1,0:T(8,128)(2,1)S(1)}, u32[]{:S(2)}, u32[]{:S(2)}) collective-permute-start(bf16[2,144,256]{2,1,0:T(8,128)(2,1)S(1)} %get-tuple-element.93), channel_id=1, source_target_pairs={{0,8},{1,9},{2,10},{3,11},{4,12},{5,13},{6,14},{7,15},{8,0},{9,1},... | collective-permute-start | bytes 442376 | tf_op jit(solution)/shard_map/ppermute | solution.py:26
  136.9 6.2 %shard_map.96 = (bf16[896,2048]{1,0:T(8,128)(2,1)}, f32[8,128]{1,0:T(8,128)S(1)}) custom-call(bf16[2048,512]{1,0:T(8,128)(2,1)S(1)} %copy-done.7, bf16[512,2688]{1,0:T(8,128)(2,1)S(1)} %get-tuple-element.88.d0.h0, bf16[512,2688]{1,0:T(8,128)(2,1)S(1)} %get-tuple-element.89.d1.h1), custom_call_target="tpu_custom_call" | custom-call | flops 3758096384 | bytes 7340032 | tf_op jit(solution)/shard_map/pallas_call | solution.py:366
  143.2 0.9 shard_map.97
  144.1 3.3 %collective-permute-start.32 = (bf16[2,80,256]{2,1,0:T(8,128)(2,1)S(1)}, bf16[2,80,256]{2,1,0:T(8,128)(2,1)S(1)}, u32[]{:S(2)}, u32[]{:S(2)}) collective-permute-start(bf16[2,80,256]{2,1,0:T(8,128)(2,1)S(1)} %get-tuple-element.98), channel_id=1, source_target_pairs={{0,16},{1,17},{2,18},{3,19},{4,20},{5,21},{6,22},{7,23},{8,24},{9,... | collective-permute-start | bytes 245768 | tf_op jit(solution)/shard_map/ppermute | solution.py:26
  147.4 2.7 %collective-permute-done.32.r = bf16[2,80,256]{2,1,0:T(8,128)(2,1)S(1)} collective-permute-done((bf16[2,80,256]{2,1,0:T(8,128)(2,1)S(1)}, bf16[2,80,256]{2,1,0:T(8,128)(2,1)S(1)}, u32[]{:S(2)}, u32[]{:S(2)}) %collective-permute-start.32) | collective-permute-done | bytes 81952 | tf_op jit(solution)/shard_map/ppermute | solution.py:26
  150.2 0.7 shard_map.98
  (64 shorter events, 4.9 us)
Async XLA Ops:
  1.5 6.9 %collective-permute-start = (bf16[2,64,512]{2,1,0:T(8,128)(2,1)S(1)}, bf16[2,64,512]{2,1,0:T(8,128)(2,1)S(1)}, u32[]{:S(2)}, u32[]{:S(2)}) collective-permute-start(bf16[2,64,512]{2,1,0:T(8,128)(2,1)S(1)} %get-tuple-element.111), channel_id=1, source_target_pairs={{0,16},{1,17},{2,18},{3,19},{4,20},{5,21},{6,22},{7,23},{8,24},{9,... | collective-permute-start | bytes 393224 | tf_op jit(solution)/shard_map/ppermute | solution.py:26
  8.4 7.7 %collective-permute-start.3 = (bf16[2,2,64,512]{3,2,0,1:T(8,128)(2,1)S(1)}, bf16[2,2,64,512]{3,2,0,1:T(8,128)(2,1)S(1)}, u32[]{:S(2)}, u32[]{:S(2)}) collective-permute-start(bf16[2,2,64,512]{3,2,0,1:T(8,128)(2,1)S(1)} %pad_maximum_fusion.2), channel_id=1, source_target_pairs={{0,1},{1,2},{2,3},{3,0},{4,5},{5,6},{6,7},{7,4},{8,9},{9,10},{10,1... | collective-permute-start | bytes 786440 | tf_op jit(solution)/shard_map/ppermute | solution.py:26
  10.0 9.9 %collective-permute-start.2 = (bf16[2,2,64,512]{3,2,0,1:T(8,128)(2,1)S(1)}, bf16[2,2,64,512]{3,2,0,1:T(8,128)(2,1)S(1)}, u32[]{:S(2)}, u32[]{:S(2)}) collective-permute-start(bf16[2,2,64,512]{3,2,0,1:T(8,128)(2,1)S(1)} %pad_maximum_fusion.2), channel_id=1, source_target_pairs={{0,2},{1,3},{2,0},{3,1},{4,6},{5,7},{6,4},{7,5},{8,10},{9,11},{10,... | collective-permute-start | bytes 786440 | tf_op jit(solution)/shard_map/ppermute | solution.py:26
  12.7 7.2 %collective-permute-start.1 = (bf16[2,2,64,512]{3,2,0,1:T(8,128)(2,1)S(1)}, bf16[2,2,64,512]{3,2,0,1:T(8,128)(2,1)S(1)}, u32[]{:S(2)}, u32[]{:S(2)}) collective-permute-start(bf16[2,2,64,512]{3,2,0,1:T(8,128)(2,1)S(1)} %pad_maximum_fusion.2), channel_id=1, source_target_pairs={{0,3},{1,0},{2,1},{3,2},{4,7},{5,4},{6,5},{7,6},{8,11},{9,8},{10,9... | collective-permute-start | bytes 786440 | tf_op jit(solution)/shard_map/ppermute | solution.py:26
  20.8 11.1 %collective-permute-start.4 = (bf16[4,2,64,512]{3,2,1,0:T(8,128)(2,1)}, bf16[4,2,64,512]{3,2,1,0:T(8,128)(2,1)}, u32[]{:S(2)}, u32[]{:S(2)}) collective-permute-start(bf16[4,2,64,512]{3,2,1,0:T(8,128)(2,1)} %pad_maximum_fusion.rest_0_), channel_id=1, source_target_pairs={{0,12},{1,13},{2,14},{3,15},{4,0},{5,1},{6,2},{7,3},{8,4},{9,5},{1... | collective-permute-start | bytes 1572872 | tf_op jit(solution)/shard_map/ppermute | solution.py:26
  25.7 10.7 %collective-permute-start.11 = (bf16[4,2,64,512]{3,2,1,0:T(8,128)(2,1)}, bf16[4,2,64,512]{3,2,1,0:T(8,128)(2,1)}, u32[]{:S(2)}, u32[]{:S(2)}) collective-permute-start(bf16[4,2,64,512]{3,2,1,0:T(8,128)(2,1)} %pad_maximum_fusion.1.rest_0_), channel_id=1, source_target_pairs={{0,4},{1,5},{2,6},{3,7},{4,8},{5,9},{6,10},{7,11},{8,12},{9,13},{1... | collective-permute-start | bytes 1572872 | tf_op jit(solution)/shard_map/ppermute | solution.py:26
  25.7 16.3 %collective-permute-start.6 = (bf16[4,2,64,512]{3,2,1,0:T(8,128)(2,1)}, bf16[4,2,64,512]{3,2,1,0:T(8,128)(2,1)}, u32[]{:S(2)}, u32[]{:S(2)}) collective-permute-start(bf16[4,2,64,512]{3,2,1,0:T(8,128)(2,1)} %pad_maximum_fusion.rest_0_), channel_id=1, source_target_pairs={{0,4},{1,5},{2,6},{3,7},{4,8},{5,9},{6,10},{7,11},{8,12},{9,13},{1... | collective-permute-start | bytes 1572872 | tf_op jit(solution)/shard_map/ppermute | solution.py:26
  31.9 10.7 %collective-permute-start.5 = (bf16[4,2,64,512]{3,2,1,0:T(8,128)(2,1)}, bf16[4,2,64,512]{3,2,1,0:T(8,128)(2,1)}, u32[]{:S(2)}, u32[]{:S(2)}) collective-permute-start(bf16[4,2,64,512]{3,2,1,0:T(8,128)(2,1)} %collective-permute-done.4.rest_1_), channel_id=1, source_target_pairs={{0,12},{1,13},{2,14},{3,15},{4,0},{5,1},{6,2},{7,3},{8,4},{9,5},{1... | collective-permute-start | bytes 1572872 | tf_op jit(solution)/shard_map/ppermute | solution.py:26
  35.6 17.9 %collective-permute-start.10 = (bf16[4,2,64,512]{3,2,1,0:T(8,128)(2,1)}, bf16[4,2,64,512]{3,2,1,0:T(8,128)(2,1)}, u32[]{:S(2)}, u32[]{:S(2)}) collective-permute-start(bf16[4,2,64,512]{3,2,1,0:T(8,128)(2,1)} %pad_maximum_fusion.1.rest_0_), channel_id=1, source_target_pairs={{0,12},{1,13},{2,14},{3,15},{4,0},{5,1},{6,2},{7,3},{8,4},{9,5},{1... | collective-permute-start | bytes 1572872 | tf_op jit(solution)/shard_map/ppermute | solution.py:26
  36.4 17.0 %collective-permute-start.12 = (bf16[4,2,64,512]{3,2,1,0:T(8,128)(2,1)}, bf16[4,2,64,512]{3,2,1,0:T(8,128)(2,1)}, u32[]{:S(2)}, u32[]{:S(2)}) collective-permute-start(bf16[4,2,64,512]{3,2,1,0:T(8,128)(2,1)} %collective-permute-done.11.rest_3_), channel_id=1, source_target_pairs={{0,4},{1,5},{2,6},{3,7},{4,8},{5,9},{6,10},{7,11},{8,12},{9,13},{1... | collective-permute-start | bytes 1572872 | tf_op jit(solution)/shard_map/ppermute | solution.py:26
  38.3 15.2 %copy-start.2 = (bf16[896,2048]{1,0:T(8,128)(2,1)S(1)}, bf16[896,2048]{1,0:T(8,128)(2,1)}, u32[]{:S(2)}) copy-start(bf16[896,2048]{1,0:T(8,128)(2,1)} %rest_4_.3) | copy-start | bytes 11010052
  38.3 15.2 %copy-start.5 = (s32[4]{0:T(128)S(1)}, s32[4]{0:T(128)}, u32[]{:S(2)}) copy-start(s32[4]{0:T(128)} %pad_add_fusion.ids) | copy-start | bytes 52
  52.8 7.7 %copy-start.4 = (f32[128,1792]{1,0:T(8,128)S(1)}, f32[128,1792]{1,0:T(8,128)}, u32[]{:S(2)}) copy-start(f32[128,1792]{1,0:T(8,128)} %get-tuple-element.62.mine) | copy-start | bytes 2752516
  52.9 7.7 %collective-permute-start.15 = (f32[128,896]{1,0:T(8,128)}, f32[128,896]{1,0:T(8,128)S(1)}, u32[]{:S(2)}, u32[]{:S(2)}) collective-permute-start(f32[128,896]{1,0:T(8,128)} %get-tuple-element.63), channel_id=1, source_target_pairs={{0,32},{1,33},{2,34},{3,35},{4,36},{5,37},{6,38},{7,39},{8,40},{9,... | collective-permute-start | bytes 1376264 | tf_op jit(solution)/shard_map/ppermute | solution.py:26
  52.9 10.1 %copy-start.10 = (f32[128,896]{1,0:T(8,128)S(1)}, f32[128,896]{1,0:T(8,128)}, u32[]{:S(2)}) copy-start(f32[128,896]{1,0:T(8,128)} %get-tuple-element.54) | copy-start | bytes 1376260
  53.0 10.1 %copy-start.9 = (f32[128,896]{1,0:T(8,128)S(1)}, f32[128,896]{1,0:T(8,128)}, u32[]{:S(2)}) copy-start(f32[128,896]{1,0:T(8,128)} %get-tuple-element.55) | copy-start | bytes 1376260
  53.0 12.6 %copy-start.3 = (f32[128,1792]{1,0:T(8,128)S(1)}, f32[128,1792]{1,0:T(8,128)}, u32[]{:S(2)}) copy-start(f32[128,1792]{1,0:T(8,128)} %get-tuple-element.53.mine) | copy-start | bytes 2752516
  53.0 7.6 %collective-permute-start.16 = (f32[128,896]{1,0:T(8,128)}, f32[128,896]{1,0:T(8,128)S(1)}, u32[]{:S(2)}, u32[]{:S(2)}) collective-permute-start(f32[128,896]{1,0:T(8,128)} %get-tuple-element.64), channel_id=1, source_target_pairs={{0,32},{1,33},{2,34},{3,35},{4,36},{5,37},{6,38},{7,39},{8,40},{9,... | collective-permute-start | bytes 1376264 | tf_op jit(solution)/shard_map/ppermute | solution.py:26
  60.3 20.9 %copy-start.6 = (bf16[2048,512]{1,0:T(8,128)(2,1)}, bf16[2048,512]{1,0:T(8,128)(2,1)S(1)}, u32[]{:S(2)}) copy-start(bf16[2048,512]{1,0:T(8,128)(2,1)S(1)} %get-tuple-element.95.g) | copy-start | bytes 6291460
  60.3 3.5 %collective-permute-start.18 = (f32[128,896]{1,0:T(8,128)S(1)}, f32[128,896]{1,0:T(8,128)S(1)}, u32[]{:S(2)}, u32[]{:S(2)}) collective-permute-start(f32[128,896]{1,0:T(8,128)S(1)} %get-tuple-element.68), channel_id=1, source_target_pairs={{0,32},{1,33},{2,34},{3,35},{4,36},{5,37},{6,38},{7,39},{8,40},{9,... | collective-permute-start | bytes 1376264 | tf_op jit(solution)/shard_map/ppermute | solution.py:26
  60.5 25.1 %copy-start = (bf16[2048,896]{1,0:T(8,128)(2,1)S(1)}, bf16[2048,896]{1,0:T(8,128)(2,1)}, u32[]{:S(2)}) copy-start(bf16[2048,896]{1,0:T(8,128)(2,1)} %wg.3) | copy-start | bytes 11010052
  60.6 25.1 %copy-start.1 = (bf16[2048,896]{1,0:T(8,128)(2,1)S(1)}, bf16[2048,896]{1,0:T(8,128)(2,1)}, u32[]{:S(2)}) copy-start(bf16[2048,896]{1,0:T(8,128)(2,1)} %wu.3) | copy-start | bytes 11010052
  61.5 19.7 %collective-permute-start.17 = (bf16[128,1920]{1,0:T(8,128)(2,1)S(1)}, bf16[128,1920]{1,0:T(8,128)(2,1)S(1)}, u32[]{:S(2)}, u32[]{:S(2)}) collective-permute-start(bf16[128,1920]{1,0:T(8,128)(2,1)S(1)} %get-tuple-element.66), channel_id=1, source_target_pairs={{0,64},{1,65},{2,66},{3,67},{4,68},{5,69},{6,70},{7,71},{8,72},{9,... | collective-permute-start | bytes 1474568 | tf_op jit(solution)/shard_map/ppermute | solution.py:26
  63.1 1.8 %collective-permute-start.7 = (f32[128,896]{1,0:T(8,128)S(1)}, f32[128,896]{1,0:T(8,128)S(1)}, u32[]{:S(2)}, u32[]{:S(2)}) collective-permute-start(f32[128,896]{1,0:T(8,128)S(1)} %copy-done.10), channel_id=1, source_target_pairs={{0,32},{1,33},{2,34},{3,35},{4,36},{5,37},{6,38},{7,39},{8,40},{9,... | collective-permute-start | bytes 1376264 | tf_op jit(solution)/shard_map/ppermute | solution.py:26
  63.1 2.5 %collective-permute-start.8 = (f32[128,896]{1,0:T(8,128)S(1)}, f32[128,896]{1,0:T(8,128)S(1)}, u32[]{:S(2)}, u32[]{:S(2)}) collective-permute-start(f32[128,896]{1,0:T(8,128)S(1)} %copy-done.9), channel_id=1, source_target_pairs={{0,32},{1,33},{2,34},{3,35},{4,36},{5,37},{6,38},{7,39},{8,40},{9,... | collective-permute-start | bytes 1376264 | tf_op jit(solution)/shard_map/ppermute | solution.py:26
  63.6 3.7 %collective-permute-start.13 = (f32[128,896]{1,0:T(8,128)S(1)}, f32[128,896]{1,0:T(8,128)S(1)}, u32[]{:S(2)}, u32[]{:S(2)}) collective-permute-start(f32[128,896]{1,0:T(8,128)S(1)} %get-tuple-element.59), channel_id=1, source_target_pairs={{0,32},{1,33},{2,34},{3,35},{4,36},{5,37},{6,38},{7,39},{8,40},{9,... | collective-permute-start | bytes 1376264 | tf_op jit(solution)/shard_map/ppermute | solution.py:26
  64.5 16.7 %collective-permute-start.19 = (bf16[128,1024]{1,0:T(8,128)(2,1)S(1)}, bf16[128,1024]{1,0:T(8,128)(2,1)S(1)}, u32[]{:S(2)}, u32[]{:S(2)}) collective-permute-start(bf16[128,1024]{1,0:T(8,128)(2,1)S(1)} %get-tuple-element.70), channel_id=1, source_target_pairs={{0,64},{1,65},{2,66},{3,67},{4,68},{5,69},{6,70},{7,71},{8,72},{9,... | collective-permute-start | bytes 786440 | tf_op jit(solution)/shard_map/ppermute | solution.py:26
  66.4 30.3 %collective-permute-start.9 = (bf16[128,1920]{1,0:T(8,128)(2,1)S(1)}, bf16[128,1920]{1,0:T(8,128)(2,1)S(1)}, u32[]{:S(2)}, u32[]{:S(2)}) collective-permute-start(bf16[128,1920]{1,0:T(8,128)(2,1)S(1)} %get-tuple-element.57), channel_id=1, source_target_pairs={{0,64},{1,65},{2,66},{3,67},{4,68},{5,69},{6,70},{7,71},{8,72},{9,... | collective-permute-start | bytes 1474568 | tf_op jit(solution)/shard_map/ppermute | solution.py:26
  82.4 2.3 %collective-permute-start.20 = (f32[128,896]{1,0:T(8,128)S(1)}, f32[128,896]{1,0:T(8,128)S(1)}, u32[]{:S(2)}, u32[]{:S(2)}) collective-permute-start(f32[128,896]{1,0:T(8,128)S(1)} %get-tuple-element.72.m0), channel_id=1, source_target_pairs={{0,32},{1,33},{2,34},{3,35},{4,36},{5,37},{6,38},{7,39},{8,40},{9,... | collective-permute-start | bytes 1376264 | tf_op jit(solution)/shard_map/ppermute | solution.py:26
  82.5 2.5 %collective-permute-start.21 = (f32[128,896]{1,0:T(8,128)S(1)}, f32[128,896]{1,0:T(8,128)S(1)}, u32[]{:S(2)}, u32[]{:S(2)}) collective-permute-start(f32[128,896]{1,0:T(8,128)S(1)} %get-tuple-element.73.m1), channel_id=1, source_target_pairs={{0,32},{1,33},{2,34},{3,35},{4,36},{5,37},{6,38},{7,39},{8,40},{9,... | collective-permute-start | bytes 1376264 | tf_op jit(solution)/shard_map/ppermute | solution.py:26
  83.0 2.6 %collective-permute-start.22 = (f32[128,896]{1,0:T(8,128)S(1)}, f32[128,896]{1,0:T(8,128)S(1)}, u32[]{:S(2)}, u32[]{:S(2)}) collective-permute-start(f32[128,896]{1,0:T(8,128)S(1)} %get-tuple-element.74.m2), channel_id=1, source_target_pairs={{0,32},{1,33},{2,34},{3,35},{4,36},{5,37},{6,38},{7,39},{8,40},{9,... | collective-permute-start | bytes 1376264 | tf_op jit(solution)/shard_map/ppermute | solution.py:26
  83.1 13.6 %collective-permute-start.14 = (bf16[128,1024]{1,0:T(8,128)(2,1)S(1)}, bf16[128,1024]{1,0:T(8,128)(2,1)S(1)}, u32[]{:S(2)}, u32[]{:S(2)}) collective-permute-start(bf16[128,1024]{1,0:T(8,128)(2,1)S(1)} %get-tuple-element.61), channel_id=1, source_target_pairs={{0,64},{1,65},{2,66},{3,67},{4,68},{5,69},{6,70},{7,71},{8,72},{9,... | collective-permute-start | bytes 786440 | tf_op jit(solution)/shard_map/ppermute | solution.py:26
  97.9 1.9 %collective-permute-start.23 = (f32[128,896]{1,0:T(8,128)S(1)}, f32[128,896]{1,0:T(8,128)S(1)}, u32[]{:S(2)}, u32[]{:S(2)}) collective-permute-start(f32[128,896]{1,0:T(8,128)S(1)} %get-tuple-element.76.m0), channel_id=1, source_target_pairs={{0,32},{1,33},{2,34},{3,35},{4,36},{5,37},{6,38},{7,39},{8,40},{9,... | collective-permute-start | bytes 1376264 | tf_op jit(solution)/shard_map/ppermute | solution.py:26
  98.0 2.5 %collective-permute-start.24 = (f32[128,896]{1,0:T(8,128)S(1)}, f32[128,896]{1,0:T(8,128)S(1)}, u32[]{:S(2)}, u32[]{:S(2)}) collective-permute-start(f32[128,896]{1,0:T(8,128)S(1)} %get-tuple-element.77.m1), channel_id=1, source_target_pairs={{0,32},{1,33},{2,34},{3,35},{4,36},{5,37},{6,38},{7,39},{8,40},{9,... | collective-permute-start | bytes 1376264 | tf_op jit(solution)/shard_map/ppermute | solution.py:26
  98.5 2.6 %collective-permute-start.25 = (f32[128,896]{1,0:T(8,128)S(1)}, f32[128,896]{1,0:T(8,128)S(1)}, u32[]{:S(2)}, u32[]{:S(2)}) collective-permute-start(f32[128,896]{1,0:T(8,128)S(1)} %get-tuple-element.78.m2), channel_id=1, source_target_pairs={{0,32},{1,33},{2,34},{3,35},{4,36},{5,37},{6,38},{7,39},{8,40},{9,... | collective-permute-start | bytes 1376264 | tf_op jit(solution)/shard_map/ppermute | solution.py:26
  109.4 19.8 %collective-permute-start.26 = (bf16[2,528,256]{2,1,0:T(8,128)(2,1)S(1)}, bf16[2,528,256]{2,1,0:T(8,128)(2,1)S(1)}, u32[]{:S(2)}, u32[]{:S(2)}) collective-permute-start(bf16[2,528,256]{2,1,0:T(8,128)(2,1)S(1)} %get-tuple-element.84), channel_id=1, source_target_pairs={{0,1},{1,2},{2,3},{3,0},{4,5},{5,6},{6,7},{7,4},{8,9},{9,10},{10,1... | collective-permute-start | bytes 1622024 | tf_op jit(solution)/shard_map/ppermute | solution.py:26
  111.4 17.9 %collective-permute-start.27 = (bf16[2,528,256]{2,1,0:T(8,128)(2,1)S(1)}, bf16[2,528,256]{2,1,0:T(8,128)(2,1)S(1)}, u32[]{:S(2)}, u32[]{:S(2)}) collective-permute-start(bf16[2,528,256]{2,1,0:T(8,128)(2,1)S(1)} %get-tuple-element.85), channel_id=1, source_target_pairs={{0,2},{1,3},{2,0},{3,1},{4,6},{5,7},{6,4},{7,5},{8,10},{9,11},{10,... | collective-permute-start | bytes 1622024 | tf_op jit(solution)/shard_map/ppermute | solution.py:26
  113.5 15.8 %collective-permute-start.28 = (bf16[2,528,256]{2,1,0:T(8,128)(2,1)S(1)}, bf16[2,528,256]{2,1,0:T(8,128)(2,1)S(1)}, u32[]{:S(2)}, u32[]{:S(2)}) collective-permute-start(bf16[2,528,256]{2,1,0:T(8,128)(2,1)S(1)} %get-tuple-element.86), channel_id=1, source_target_pairs={{0,3},{1,0},{2,1},{3,2},{4,7},{5,4},{6,5},{7,6},{8,11},{9,8},{10,9... | collective-permute-start | bytes 1622024 | tf_op jit(solution)/shard_map/ppermute | solution.py:26
  115.0 1.6 %copy-start.8 = (bf16[2048,512]{1,0:T(8,128)(2,1)S(1)}, bf16[2048,512]{1,0:T(8,128)(2,1)}, u32[]{:S(2)}) copy-start(bf16[2048,512]{1,0:T(8,128)(2,1)} %get-tuple-element.87.x) | copy-start | bytes 6291460
  116.6 20.3 %copy-start.7 = (bf16[2048,512]{1,0:T(8,128)(2,1)S(1)}, bf16[2048,512]{1,0:T(8,128)(2,1)}, u32[]{:S(2)}) copy-start(bf16[2048,512]{1,0:T(8,128)(2,1)} %copy-done.6) | copy-start | bytes 6291460
  131.7 11.5 %collective-permute-start.29 = (bf16[2,144,256]{2,1,0:T(8,128)(2,1)S(1)}, bf16[2,144,256]{2,1,0:T(8,128)(2,1)S(1)}, u32[]{:S(2)}, u32[]{:S(2)}) collective-permute-start(bf16[2,144,256]{2,1,0:T(8,128)(2,1)S(1)} %get-tuple-element.92), channel_id=1, source_target_pairs={{0,4},{1,5},{2,6},{3,7},{4,8},{5,9},{6,10},{7,11},{8,12},{9,13},{1... | collective-permute-start | bytes 442376 | tf_op jit(solution)/shard_map/ppermute | solution.py:26
  131.8 11.4 %collective-permute-start.30 = (bf16[2,144,256]{2,1,0:T(8,128)(2,1)S(1)}, bf16[2,144,256]{2,1,0:T(8,128)(2,1)S(1)}, u32[]{:S(2)}, u32[]{:S(2)}) collective-permute-start(bf16[2,144,256]{2,1,0:T(8,128)(2,1)S(1)} %get-tuple-element.93), channel_id=1, source_target_pairs={{0,8},{1,9},{2,10},{3,11},{4,12},{5,13},{6,14},{7,15},{8,0},{9,1},... | collective-permute-start | bytes 442376 | tf_op jit(solution)/shard_map/ppermute | solution.py:26
  136.9 6.3 %collective-permute-start.31 = (bf16[2,144,256]{2,1,0:T(8,128)(2,1)S(1)}, bf16[2,144,256]{2,1,0:T(8,128)(2,1)S(1)}, u32[]{:S(2)}, u32[]{:S(2)}) collective-permute-start(bf16[2,144,256]{2,1,0:T(8,128)(2,1)S(1)} %get-tuple-element.94), channel_id=1, source_target_pairs={{0,12},{1,13},{2,14},{3,15},{4,0},{5,1},{6,2},{7,3},{8,4},{9,5},{1... | collective-permute-start | bytes 442376 | tf_op jit(solution)/shard_map/ppermute | solution.py:26
  144.1 6.0 %collective-permute-start.32 = (bf16[2,80,256]{2,1,0:T(8,128)(2,1)S(1)}, bf16[2,80,256]{2,1,0:T(8,128)(2,1)S(1)}, u32[]{:S(2)}, u32[]{:S(2)}) collective-permute-start(bf16[2,80,256]{2,1,0:T(8,128)(2,1)S(1)} %get-tuple-element.98), channel_id=1, source_target_pairs={{0,16},{1,17},{2,18},{3,19},{4,20},{5,21},{6,22},{7,23},{8,24},{9,... | collective-permute-start | bytes 245768 | tf_op jit(solution)/shard_map/ppermute | solution.py:26
